TPU v7x, 32 devices: a whole 2x2x4 slice. The times are simulated.
32 devices in a mesh: ax: 16 (over z, x, core), az: 2 (over y).
Axes of the slice: x: 2, y: 2, z: 4, core: 2. Of those that a mesh axis runs over, the one named last changes fastest.
Arguments:
- initial: float32 [19, 32, 32, 256], P(None, 'ax', 'az'), as said below
- adjoint_seed: float32 [19, 32, 32, 256], P(None, 'ax', 'az'), may hold values from -6 to 6
- porosity: float32 [32, 32, 256], P('ax', 'az'), may hold values from 0.05 to 0.6
- cell_type: int32 [32, 32, 256], P('ax', 'az'), may hold values from 0 to 3
- region: int32 [32, 32, 256], P('ax', 'az'), may hold values from 0 to 8, as said below
Outputs:
- final_state: float32 [19, 32, 32, 256], P(None, 'ax', 'az')
- adjoint_state: float32 [19, 32, 32, 256], P(None, 'ax', 'az')
- sensitivity: float32 [32, 32, 256], P('ax', 'az')
- region_totals: float32 [8], replicated
Inputs may be any that keep to these rules, and one draw needn't show every extreme that they name: `cell_type`: the cells of radial index 0 and 255 are walls. All design cells of one aligned block of 2 x 16 x 256 cells share one region; each region holds four such blocks. `initial`: populations are positive.
All inputs are finite; a program needn't handle non-finite values.
Results may differ from a plain program's by a relative error of at most 0.0003.
Values sent between devices are 32-bit elements; how exact they have to be, the bound alone decides.
No kernel may reach another device: no remote copies, remote signals or barrier semaphores. Data moves between devices by JAX's collectives and lax.ppermute only.
A program may use at most 64 MiB of HBM per device.

v0:
```python
import functools

import jax
import jax.numpy as jnp
import numpy as np
from jax import lax
from jax.experimental import pallas as pl
from jax.experimental.pallas import tpu as pltpu
from jax.sharding import PartitionSpec as P

VELOCITY = [
    (0, 0, 0),
    (1, 0, 0),
    (-1, 0, 0),
    (0, 1, 0),
    (0, -1, 0),
    (0, 0, 1),
    (0, 0, -1),
    (1, 1, 0),
    (-1, -1, 0),
    (1, -1, 0),
    (-1, 1, 0),
    (1, 0, 1),
    (-1, 0, -1),
    (1, 0, -1),
    (-1, 0, 1),
    (0, 1, 1),
    (0, -1, -1),
    (0, 1, -1),
    (0, -1, 1),
]
OPPOSITE = [0, 2, 1, 4, 3, 6, 5, 8, 7, 10, 9, 12, 11, 14, 13, 16, 15, 18, 17]
INLET_SPEED = (0.05, 0.05, 0.0)
W_AXIS = 1.0 / 18.0
W_EDGE = 1.0 / 36.0


def moving(axis, sign):
    return [q for q in range(19) if VELOCITY[q][axis] == sign]


LO, HI = 0, 1
POST, ADJ, FLAG = 0, 1, 2


def face_fields(axis, side):
    sign = -1 if side == LO else 1
    fields = [(POST, q) for q in moving(axis, sign)] + [(ADJ, q) for q in moving(axis, -sign)]
    return fields + [(FLAG, 0)]


AX_SLOT = [{key: i for i, key in enumerate(face_fields(0, side))} for side in (LO, HI)]


def azimuthal_rows():
    place, corner, rest = {}, [[], []], []
    for a, sign, block in ((1, 1, 0), (0, -1, 1)):
        for side in (LO, HI):
            for kind, q in face_fields(1, side):
                leaves = VELOCITY[q][0] == (sign if kind == POST else -sign)
                if kind == FLAG or leaves:
                    corner[block].append((side, kind, q, a))
                else:
                    rest.append((side, kind, q, a))
    for block in (0, 1):
        for i, key in enumerate(corner[block]):
            place[key] = (block, i)
    for i, key in enumerate(rest):
        place[key] = (2 + i // 8, i % 8)
    return place, 2 + (len(rest) + 7) // 8


AZ_PLACE, AZ_BLOCKS = azimuthal_rows()


def pairs_of(values):
    sums = [values[q] + values[q + 1] for q in range(1, 19, 2)]
    diffs = [values[q] - values[q + 1] for q in range(1, 19, 2)]
    return sums, diffs


def projections(vec):
    va, vt, vr = vec
    return [va, vt, vr, va + vt, va - vt, va + vr, va - vr, vt + vr, vt - vr]


def linearise(pops, porous, types, regions):
    sums, diffs = pairs_of(pops)
    s0, s1, s2, s3, s4, s5, s6, s7, s8 = sums
    d0, d1, d2, d3, d4, d5, d6, d7, d8 = diffs
    at, ar, tr = s3 + s4, s5 + s6, s7 + s8
    rho = pops[0] + ((s0 + s1) + (s2 + at)) + (ar + tr)
    ma = (d0 + (d3 + d4)) + (d5 + d6)
    mt = (d1 + (d3 - d4)) + (d7 + d8)
    mr = (d2 + (d5 - d6)) + (d7 - d8)
    inv = 1.0 / rho
    ua, ut, ur = ma * inv, mt * inv, mr * inv
    third = rho * (1.0 / 3.0)
    paa = (s0 + at + ar - third) - ma * ua
    ptt = (s1 + at + tr - third) - mt * ut
    prr = (s2 + ar + tr - third) - mr * ur
    pat = (s3 - s4) - ma * ut
    par = (s5 - s6) - ma * ur
    ptr = (s7 - s8) - mt * ur
    square = (paa * paa + ptt * ptt + prr * prr) + 2.0 * (pat * pat + par * par + ptr * ptr) + 0.0001
    inv_root = lax.rsqrt(square)
    shear = 1.5 * (square * inv_root) * inv
    shifted = shear + 0.01
    viscous = 0.02 * jnp.exp((0.7 - 1.0) * jnp.log(shifted))
    omega = 1.0 / (0.5 + 3.0 * viscous)
    relaxed = (types != 2) & (types != 3)
    kappa = jnp.where(regions > 0, porous, 0.0)
    return dict(
        rho=rho,
        inv=inv,
        u=(ua, ut, ur),
        p=(paa, ptt, prr, pat, par, ptr),
        inv_root=inv_root,
        shear=shear,
        shifted=shifted,
        viscous=viscous,
        omega=omega,
        relaxed=relaxed,
        kappa=kappa,
        keep=jnp.where(relaxed, 1.0 - omega, 0.0),
        design=jnp.where(relaxed & (regions > 0), 1.0, 0.0),
        inlet=types == 2,
        outlet=types == 3,
    )


def collide(pops, lin):
    rho, relaxed, inlet = lin["rho"], lin["relaxed"], lin["inlet"]
    ua, ut, ur = (jnp.where(inlet, speed, x) for x, speed in zip(lin["u"], INLET_SPEED))
    scale = jnp.where(relaxed, (lin["omega"] - lin["kappa"]) * rho, 1.0)
    rest = jnp.where(relaxed, lin["kappa"] * rho, 0.0)
    keep = lin["keep"]
    still = 1.0 - 1.5 * (ua * ua + ut * ut + ur * ur)
    post = [keep * pops[0] + (1.0 / 3.0) * (scale * still + rest)]
    for i, cu in enumerate(projections((ua, ut, ur))):
        weight = W_AXIS if i < 3 else W_EDGE
        even = weight * (scale * (still + 4.5 * cu * cu) + rest)
        odd = (3.0 * weight) * (scale * cu)
        post.append(keep * pops[1 + 2 * i] + (even + odd))
        post.append(keep * pops[2 + 2 * i] + (even - odd))
    return post


def pull_back(back, pops, lin):
    sums, diffs = pairs_of(back)
    s0, s1, s2, s3, s4, s5, s6, s7, s8 = sums
    d0, d1, d2, d3, d4, d5, d6, d7, d8 = diffs
    at, ar, tr = s3 + s4, s5 + s6, s7 + s8
    b0 = (1.0 / 3.0) * back[0] + W_AXIS * (s0 + s1 + s2) + W_EDGE * (at + ar + tr)
    ba = W_AXIS * d0 + W_EDGE * ((d3 + d4) + (d5 + d6))
    bt = W_AXIS * d1 + W_EDGE * ((d3 - d4) + (d7 + d8))
    br = W_AXIS * d2 + W_EDGE * ((d5 - d6) + (d7 - d8))
    baa = W_AXIS * s0 + W_EDGE * (at + ar)
    btt = W_AXIS * s1 + W_EDGE * (at + tr)
    brr = W_AXIS * s2 + W_EDGE * (ar + tr)
    bat, bar, btr = W_EDGE * (s3 - s4), W_EDGE * (s5 - s6), W_EDGE * (s7 - s8)
    along = back[0] * pops[0]
    for q in range(1, 19):
        along = along + back[q] * pops[q]
    rho, inv = lin["rho"], lin["inv"]
    ua, ut, ur = lin["u"]
    qa = baa * ua + bat * ut + bar * ur
    qt = bat * ua + btt * ut + btr * ur
    qr = bar * ua + btr * ut + brr * ur
    uu = ua * ua + ut * ut + ur * ur
    slope = 3.0 * (ua * ba + ut * bt + ur * br) + 4.5 * (ua * qa + ut * qt + ur * qr) - 1.5 * (uu * b0)
    full = b0 + slope
    sens = -(lin["design"] * (rho * slope))
    relaxed, omega = lin["relaxed"], lin["omega"]
    shear_bar = (rho * full - along) * (omega * omega) * (0.9 * lin["viscous"]) / lin["shifted"]
    shear_bar = jnp.where(relaxed, shear_bar, 0.0)
    z = shear_bar * (1.5 * inv) * lin["inv_root"]
    maa, mtt, mrr, mat, mar, mtr = (z * x for x in lin["p"])
    scale = jnp.where(relaxed, omega - lin["kappa"], jnp.where(lin["outlet"], inv, 0.0))
    la = maa * ua + mat * ut + mar * ur
    lt = mat * ua + mtt * ut + mtr * ur
    lr = mar * ua + mtr * ut + mrr * ur
    va = scale * (3.0 * (ba - b0 * ua) + 9.0 * qa) - 2.0 * la
    vt = scale * (3.0 * (bt - b0 * ut) + 9.0 * qt) - 2.0 * lt
    vr = scale * (3.0 * (br - b0 * ur) + 9.0 * qr) - 2.0 * lr
    total = jnp.where(relaxed, lin["kappa"] * b0 + scale * full, 0.0)
    total = total - shear_bar * lin["shear"] * inv - (1.0 / 3.0) * (maa + mtt + mrr)
    total = total - ((la + va) * ua + (lt + vt) * ut + (lr + vr) * ur)
    keep = lin["keep"]
    taa, ttt, trr = total + maa, total + mtt, total + mrr
    sat, sar, str_ = taa + mtt, taa + mrr, ttt + mrr
    mat2, mar2, mtr2 = 2.0 * mat, 2.0 * mar, 2.0 * mtr
    evens = [taa, ttt, trr, sat + mat2, sat - mat2, sar + mar2, sar - mar2, str_ + mtr2, str_ - mtr2]
    result = [keep * back[0] + total]
    for i, odd in enumerate(projections((va, vt, vr))):
        result.append(keep * back[1 + 2 * i] + (evens[i] + odd))
        result.append(keep * back[2 + 2 * i] + (evens[i] - odd))
    return result, sens


class Fields:
    def __init__(self, own, halo):
        self.own = own
        self.halo = halo
        up_e = halo["parity"] == 0
        self.up_e = up_e

    def row(self, kind, q, a):
        rows_a = self.own[POST].shape[1]
        if 0 <= a < rows_a:
            return self.own[FLAG][a] if kind == FLAG else self.own[kind][q, a]
        e, o = self.halo["e"], self.halo["o"]
        if a < 0:
            slot = AX_SLOT[HI][(kind, q)]
            return jnp.where(self.up_e, o[slot], e[slot])
        slot = AX_SLOT[LO][(kind, q)]
        return jnp.where(self.up_e, e[slot], o[slot])

    def edge(self, side, kind, q, a):
        rows_a = self.own[POST].shape[1]
        if 0 <= a < rows_a:
            block, i = AZ_PLACE[(side, kind, q, a)]
            return self.halo["t"][block, i : i + 1, :]
        ec, oc = self.halo["ec"], self.halo["oc"]
        if a < 0:
            block, i = AZ_PLACE[(side, kind, q, 1)]
            return jnp.where(self.up_e, oc[block, i : i + 1, :], ec[block, i : i + 1, :])
        block, i = AZ_PLACE[(side, kind, q, 0)]
        return jnp.where(self.up_e, ec[block, i : i + 1, :], oc[block, i : i + 1, :])

    def moved(self, kind, q, a, shift):
        sa, st, sr = shift
        value = self.row(kind, q, a + sa)
        rows_t, rows_r = value.shape
        if st:
            value = pltpu.roll(value, (-st) % rows_t, 0)
            beyond = self.edge(LO if st > 0 else HI, kind, q, a + sa)
            at_edge = lax.broadcasted_iota(jnp.int32, value.shape, 0) == (rows_t - 1 if st > 0 else 0)
            value = jnp.where(at_edge, beyond, value)
        if sr:
            value = pltpu.roll(value, (-sr) % rows_r, 1)
        return value


def pack(own, parity, e_ref, o_ref, t_ref):
    rows_a, rows_t = own[POST].shape[1], own[POST].shape[2]
    with_flags = FLAG in own
    even = parity == 0

    def cells(kind, q, a):
        return own[FLAG][a] if kind == FLAG else own[kind][q, a]

    for slot in range(len(AX_SLOT[LO])):
        low = [key for key, i in AX_SLOT[LO].items() if i == slot][0]
        high = [key for key, i in AX_SLOT[HI].items() if i == slot][0]
        if low[0] == FLAG and not with_flags:
            continue
        low, high = cells(*low, 0), cells(*high, rows_a - 1)
        e_ref[slot] = jnp.where(even, high, low)
        o_ref[slot] = jnp.where(even, low, high)
    for (side, kind, q, a), (block, i) in AZ_PLACE.items():
        if kind == FLAG and not with_flags:
            continue
        t = 0 if side == LO else rows_t - 1
        source = own[FLAG].at[a] if kind == FLAG else own[kind].at[q, a]
        t_ref[block, i : i + 1, :] = source[t : t + 1, :]


def chunks(shape, body):
    rows_a, rows_t, rows_r = shape
    counts = (rows_a, rows_t // 8, rows_r // 128)

    def step(i, carry):
        a = i // (counts[1] * counts[2])
        t = pl.multiple_of((i // counts[2]) % counts[1] * 8, 8)
        r = pl.multiple_of(i % counts[2] * 128, 128)
        body((a, pl.ds(t, 8), pl.ds(r, 128)))
        return carry

    lax.fori_loop(0, counts[0] * counts[1] * counts[2], step, 0)


def load(ref, where):
    return [ref[(q,) + where] for q in range(19)]


def store(ref, where, values):
    for q in range(19):
        ref[(q,) + where] = values[q]


def first_kernel(parity_ref, pops, seed, porous, types, regions, post, e_out, o_out, t_out, flags):
    def body(where):
        values = load(pops, where)
        lin = linearise(values, porous[where], types[where], regions[where])
        store(post, where, collide(values, lin))

    chunks(porous.shape, body)
    flags[...] = jnp.where(types[...] != 1, 1.0, 0.0)
    pack({POST: post, ADJ: seed, FLAG: flags}, parity_ref[0], e_out, o_out, t_out)


def second_kernel(
    parity_ref, post, seed, flags, porous, types, regions, e, o, t, ec, oc,
    post_next, adj, sens, around, e_out, o_out, t_out, state, back,
):
    halo = dict(parity=parity_ref[0], e=e, o=o, t=t, ec=ec, oc=oc)
    fields = Fields({POST: post, ADJ: seed, FLAG: flags}, halo)
    rows_a = porous.shape[0]
    for a in range(rows_a):
        centre = flags[a]
        state[0, a] = post[0, a]
        back[0, a] = seed[0, a]
        for q in range(1, 19):
            direc = VELOCITY[q]
            behind = tuple(-c for c in direc)
            open_ = fields.moved(FLAG, 0, a, behind)
            around[q - 1, a] = open_
            opp = OPPOSITE[q]
            state[q, a] = jnp.where(open_ > 0, fields.moved(POST, q, a, behind), post[opp, a])
            back[opp, a] = centre * fields.moved(ADJ, opp, a, behind) + (1.0 - open_) * seed[q, a]

    def body(where):
        values = load(state, where)
        lin = linearise(values, porous[where], types[where], regions[where])
        store(post_next, where, collide(values, lin))
        result, partial_sens = pull_back(load(back, where), values, lin)
        store(adj, where, result)
        sens[where] = partial_sens

    chunks(porous.shape, body)
    pack({POST: post_next, ADJ: adj}, parity_ref[0], e_out, o_out, t_out)


def third_kernel(
    parity_ref, post, adj, flags, around, pops, porous, types, regions, sens_one, e, o, t, ec, oc,
    final, result, sens, totals, back, acc,
):
    halo = dict(parity=parity_ref[0], e=e, o=o, t=t, ec=ec, oc=oc)
    fields = Fields({POST: post, ADJ: adj, FLAG: flags}, halo)
    rows_a = porous.shape[0]
    for a in range(rows_a):
        centre = flags[a]
        final[0, a] = post[0, a]
        back[0, a] = adj[0, a]
        for q in range(1, 19):
            behind = tuple(-c for c in VELOCITY[q])
            open_ = around[q - 1, a]
            opp = OPPOSITE[q]
            final[q, a] = jnp.where(open_ > 0, fields.moved(POST, q, a, behind), post[opp, a])
            back[opp, a] = centre * fields.moved(ADJ, opp, a, behind) + (1.0 - open_) * adj[q, a]
    acc[...] = jnp.zeros_like(acc)

    def body(where):
        values = load(pops, where)
        lin = linearise(values, porous[where], types[where], regions[where])
        adjoint, partial_sens = pull_back(load(back, where), values, lin)
        store(result, where, adjoint)
        both = partial_sens + sens_one[where]
        sens[where] = both
        acc[...] += jnp.where(regions[where] > 0, both, 0.0)

    chunks(porous.shape, body)
    label = jnp.max(regions[...], axis=(0, 1, 2), keepdims=True)[0]
    total = jnp.sum(acc[...], axis=(0, 1), keepdims=True)
    lanes = lax.broadcasted_iota(jnp.int32, totals.shape, 1) + 1
    totals[...] = jnp.where(lanes == label, total, 0.0)


def call(body, out_shapes, scratch, parity, *arrays):
    return pl.pallas_call(
        body,
        out_shape=[jax.ShapeDtypeStruct(s, jnp.float32) for s in out_shapes],
        in_specs=[pl.BlockSpec(memory_space=pltpu.SMEM)]
        + [pl.BlockSpec(memory_space=pltpu.VMEM)] * len(arrays),
        out_specs=[pl.BlockSpec(memory_space=pltpu.VMEM)] * len(out_shapes),
        scratch_shapes=[pltpu.VMEM(s, jnp.float32) for s in scratch],
        compiler_params=pltpu.CompilerParams(vmem_limit_bytes=40 * 1024 * 1024),
    )(parity, *arrays)


def even_pairs(size):
    return [(i, i ^ 1) for i in range(size) if i ^ 1 < size]


def odd_pairs(size):
    return [(i, ((i + 1) ^ 1) - 1) for i in range(size) if 0 <= ((i + 1) ^ 1) - 1 < size]


def exchange(e_msg, o_msg, t_msg):
    size_a, size_t = lax.axis_size("ax"), lax.axis_size("az")
    ring = [(i, (i + 1) % size_t) for i in range(size_t)]
    t = lax.ppermute(t_msg, "az", ring)
    if size_t > 2:
        from_high = np.zeros((AZ_BLOCKS, 8, 1), bool)
        for (side, _, _, _), (block, i) in AZ_PLACE.items():
            from_high[block, i] = side == HI
        t_down = lax.ppermute(t_msg, "az", [(j, i) for i, j in ring])
        t = jnp.where(jnp.asarray(from_high), t, t_down)
    e = lax.ppermute(e_msg, "ax", even_pairs(size_a))
    o = lax.ppermute(o_msg, "ax", odd_pairs(size_a))
    corners = t[:2]
    ec = lax.ppermute(corners, "ax", even_pairs(size_a))
    oc = lax.ppermute(corners, "ax", odd_pairs(size_a))
    return e, o, t, ec, oc


def sum_all(x):
    for axis in ("az", "ax"):
        size = lax.axis_size(axis)
        if size & (size - 1):
            x = lax.psum(x, axis)
            continue
        step = 1
        while step < size:
            x = x + lax.ppermute(x, axis, [(i, i ^ step) for i in range(size)])
            step *= 2
    return x


def shards(initial, adjoint_seed, porosity, cell_type, region):
    cells = porosity.shape
    pops = (19,) + cells
    fields = len(AX_SLOT[LO])
    face, rows = cells[1:], (AZ_BLOCKS, 8, cells[2])
    parity = (lax.axis_index("ax") % 2).astype(jnp.int32).reshape(1)
    post, e, o, t, flags = call(
        first_kernel,
        [pops, (fields,) + face, (fields,) + face, rows, cells],
        [],
        parity, initial, adjoint_seed, porosity, cell_type, region,
    )
    near = exchange(e, o, t)
    post, adj, sens_one, around, e, o, t = call(
        second_kernel,
        [pops, pops, cells, (18,) + cells, (fields - 1,) + face, (fields - 1,) + face, rows],
        [pops, pops],
        parity, post, adjoint_seed, flags, porosity, cell_type, region, *near,
    )
    near = exchange(e, o, t)
    regions = lax.axis_size("ax") * lax.axis_size("az") // 4
    lanes = -(-regions // 128) * 128
    final, adjoint, sensitivity, partial = call(
        third_kernel,
        [pops, pops, cells, (1, lanes)],
        [pops, (8, 128)],
        parity, post, adj, flags, around, initial, porosity, cell_type, region, sens_one, *near,
    )
    totals = sum_all(partial)[0, :regions]
    return final, adjoint, sensitivity, totals


def solution(mesh):
    return jax.shard_map(
        shards,
        mesh=mesh,
        in_specs=(
            P(None, "ax", "az", None),
            P(None, "ax", "az", None),
            P("ax", "az", None),
            P("ax", "az", None),
            P("ax", "az", None),
        ),
        out_specs=(P(None, "ax", "az", None), P(None, "ax", "az", None), P("ax", "az", None), P()),
        check_vma=False,
    )
```

profile of v0, /device:TPU:0, one launch (start us, length us, event | category | flops | bytes accessed | tf_op | source)
XLA Modules:
  0.0 53.9 jit_solution(9160236727104208015)
XLA Ops:
  0.6 0.0 copy-start
  0.7 1.1 %copy-done = f32[19,2,16,256]{3,2,1,0:T(8,128)S(1)} copy-done((f32[19,2,16,256]{3,2,1,0:T(8,128)S(1)}, f32[19,2,16,256]{3,2,1,0:T(8,128)}, u32[]{:S(2)}) %copy-start) | copy-done | bytes 622616
  1.7 0.0 copy-start.2
  1.7 1.1 %copy-done.2 = f32[19,2,16,256]{3,2,1,0:T(8,128)S(1)} copy-done((f32[19,2,16,256]{3,2,1,0:T(8,128)S(1)}, f32[19,2,16,256]{3,2,1,0:T(8,128)}, u32[]{:S(2)}) %copy-start.2) | copy-done | bytes 622616
  2.8 0.0 copy-start.4
  2.8 0.8 %copy-done.4 = f32[2,16,256]{2,1,0:T(8,128)S(1)} copy-done((f32[2,16,256]{2,1,0:T(8,128)S(1)}, f32[2,16,256]{2,1,0:T(8,128)}, u32[]{:S(2)}) %copy-start.4) | copy-done | bytes 32792
  3.6 0.0 copy-start.6
  3.6 0.8 %copy-done.6 = s32[2,16,256]{2,1,0:T(8,128)S(1)} copy-done((s32[2,16,256]{2,1,0:T(8,128)S(1)}, s32[2,16,256]{2,1,0:T(8,128)}, u32[]{:S(2)}) %copy-start.6) | copy-done | bytes 32792
  4.3 0.0 copy-start.8
  4.3 0.8 %copy-done.8 = s32[2,16,256]{2,1,0:T(8,128)S(1)} copy-done((s32[2,16,256]{2,1,0:T(8,128)S(1)}, s32[2,16,256]{2,1,0:T(8,128)}, u32[]{:S(2)}) %copy-start.8) | copy-done | bytes 32792
  5.1 0.0 copy-start.3
  5.1 0.0 copy-start.7
  5.1 0.8 %shard_map.84 = (f32[19,2,16,256]{3,2,1,0:T(8,128)S(1)}, f32[11,16,256]{2,1,0:T(8,128)S(1)}, f32[11,16,256]{2,1,0:T(8,128)S(1)}, f32[6,8,256]{2,1,0:T(8,128)S(1)}, f32[2,16,256]{2,1,0:T(8,128)S(1)}) custom-call(s32[1]{0:T(128)} %bitcast.parity_ref, f32[19,2,16,256]{3,2,1,0:T(8,128)S(1)} %copy-done, f32[19,2,16,256]{3,2,1,0:T(8,128)S(1)} %copy-done.2, ...), custom_call_target="tpu_custom_call" | custom-call | tf_op jit(solution)/shard_map/pallas_call | solution.py:371
  5.9 0.0 copy-start.5
  5.9 0.5 collective-permute-start
  6.4 0.7 %collective-permute-start.1 = (f32[11,16,256]{2,1,0:T(8,128)S(1)}, f32[11,16,256]{2,1,0:T(8,128)S(1)}, u32[]{:S(2)}, u32[]{:S(2)}) collective-permute-start(f32[11,16,256]{2,1,0:T(8,128)S(1)} %get-tuple-element.23), channel_id=1, source_target_pairs={{2,4},{4,2},{6,8},{8,6},{10,12},{12,10},{14,16},{16,14},{18,20},{2... | collective-permute-start | bytes 540680 | tf_op jit(solution)/shard_map/ppermute | solution.py:401
  7.1 2.6 %collective-permute-start.2 = (f32[6,8,256]{2,1,0:T(8,128)S(1)}, f32[6,8,256]{2,1,0:T(8,128)S(1)}, u32[]{:S(2)}, u32[]{:S(2)}) collective-permute-start(f32[6,8,256]{2,1,0:T(8,128)S(1)} %get-tuple-element.24), channel_id=1, source_target_pairs={{0,1},{1,0},{2,3},{3,2},{4,5},{5,4},{6,7},{7,6},{8,9},{9,8},{10,11... | collective-permute-start | bytes 147464 | tf_op jit(solution)/shard_map/ppermute | solution.py:393
  9.7 2.1 %collective-permute-done.2.t = f32[6,8,256]{2,1,0:T(8,128)S(1)} collective-permute-done((f32[6,8,256]{2,1,0:T(8,128)S(1)}, f32[6,8,256]{2,1,0:T(8,128)S(1)}, u32[]{:S(2)}, u32[]{:S(2)}) %collective-permute-start.2) | collective-permute-done | bytes 49184 | tf_op jit(solution)/shard_map/ppermute | solution.py:393
  11.7 0.7 %collective-permute-start.4 = (f32[2,8,256]{2,1,0:T(8,128)S(1)}, f32[2,8,256]{2,1,0:T(8,128)S(1)}, u32[]{:S(2)}, u32[]{:S(2)}) collective-permute-start(f32[2,8,256]{2,1,0:T(8,128)S(1)} %slice.12), channel_id=1, source_target_pairs={{2,4},{4,2},{6,8},{8,6},{10,12},{12,10},{14,16},{16,14},{18,20},{2... | collective-permute-start | bytes 49160 | tf_op jit(solution)/shard_map/ppermute | solution.py:404
  12.4 4.8 %collective-permute-start.3 = (f32[2,8,256]{2,1,0:T(8,128)S(1)}, f32[2,8,256]{2,1,0:T(8,128)S(1)}, u32[]{:S(2)}, u32[]{:S(2)}) collective-permute-start(f32[2,8,256]{2,1,0:T(8,128)S(1)} %slice.12), channel_id=1, source_target_pairs={{0,2},{2,0},{4,6},{6,4},{8,10},{10,8},{12,14},{14,12},{16,18},{18,... | collective-permute-start | bytes 49160 | tf_op jit(solution)/shard_map/ppermute | solution.py:403
  17.2 0.0 collective-permute-done.4.oc
  17.2 0.8 %collective-permute-done.3.ec = f32[2,8,256]{2,1,0:T(8,128)S(1)} collective-permute-done((f32[2,8,256]{2,1,0:T(8,128)S(1)}, f32[2,8,256]{2,1,0:T(8,128)S(1)}, u32[]{:S(2)}, u32[]{:S(2)}) %collective-permute-start.3) | collective-permute-done | bytes 16416 | tf_op jit(solution)/shard_map/ppermute | solution.py:403
  18.0 0.0 collective-permute-done.e
  18.0 0.0 collective-permute-done.1.o
  18.0 0.0 copy-done.3
  18.0 0.0 copy-done.7
  18.0 0.0 copy-done.5
  18.1 0.0 copy-start.1
  18.1 1.3 %shard_map.85 = (f32[19,2,16,256]{3,2,1,0:T(8,128)S(1)}, f32[19,2,16,256]{3,2,1,0:T(8,128)S(1)}, f32[2,16,256]{2,1,0:T(8,128)S(1)}, f32[18,2,16,256]{3,2,1,0:T(8...) custom-call(s32[1]{0:T(128)} %bitcast.parity_ref, ...), custom_call_target="tpu_custom_call" | custom-call | tf_op jit(solution)/shard_map/pallas_call | solution.py:371
  19.4 1.0 %collective-permute-start.5 = (f32[10,16,256]{2,1,0:T(8,128)S(1)}, f32[10,16,256]{2,1,0:T(8,128)S(1)}, u32[]{:S(2)}, u32[]{:S(2)}) collective-permute-start(f32[10,16,256]{2,1,0:T(8,128)S(1)} %get-tuple-element.29), channel_id=1, source_target_pairs={{0,2},{2,0},{4,6},{6,4},{8,10},{10,8},{12,14},{14,12},{16,18},{18,... | collective-permute-start | bytes 491528 | tf_op jit(solution)/shard_map/ppermute | solution.py:400
  20.5 0.7 %collective-permute-start.6 = (f32[10,16,256]{2,1,0:T(8,128)S(1)}, f32[10,16,256]{2,1,0:T(8,128)S(1)}, u32[]{:S(2)}, u32[]{:S(2)}) collective-permute-start(f32[10,16,256]{2,1,0:T(8,128)S(1)} %get-tuple-element.30), channel_id=1, source_target_pairs={{2,4},{4,2},{6,8},{8,6},{10,12},{12,10},{14,16},{16,14},{18,20},{2... | collective-permute-start | bytes 491528 | tf_op jit(solution)/shard_map/ppermute | solution.py:401
  21.1 2.1 %collective-permute-start.7 = (f32[6,8,256]{2,1,0:T(8,128)S(1)}, f32[6,8,256]{2,1,0:T(8,128)S(1)}, u32[]{:S(2)}, u32[]{:S(2)}) collective-permute-start(f32[6,8,256]{2,1,0:T(8,128)S(1)} %get-tuple-element.31), channel_id=1, source_target_pairs={{0,1},{1,0},{2,3},{3,2},{4,5},{5,4},{6,7},{7,6},{8,9},{9,8},{10,11... | collective-permute-start | bytes 147464 | tf_op jit(solution)/shard_map/ppermute | solution.py:393
  23.2 2.1 %collective-permute-done.7.t = f32[6,8,256]{2,1,0:T(8,128)S(1)} collective-permute-done((f32[6,8,256]{2,1,0:T(8,128)S(1)}, f32[6,8,256]{2,1,0:T(8,128)S(1)}, u32[]{:S(2)}, u32[]{:S(2)}) %collective-permute-start.7) | collective-permute-done | bytes 49184 | tf_op jit(solution)/shard_map/ppermute | solution.py:393
  25.3 0.7 %collective-permute-start.9 = (f32[2,8,256]{2,1,0:T(8,128)S(1)}, f32[2,8,256]{2,1,0:T(8,128)S(1)}, u32[]{:S(2)}, u32[]{:S(2)}) collective-permute-start(f32[2,8,256]{2,1,0:T(8,128)S(1)} %slice.13), channel_id=1, source_target_pairs={{2,4},{4,2},{6,8},{8,6},{10,12},{12,10},{14,16},{16,14},{18,20},{2... | collective-permute-start | bytes 49160 | tf_op jit(solution)/shard_map/ppermute | solution.py:404
  25.9 5.4 %collective-permute-start.8 = (f32[2,8,256]{2,1,0:T(8,128)S(1)}, f32[2,8,256]{2,1,0:T(8,128)S(1)}, u32[]{:S(2)}, u32[]{:S(2)}) collective-permute-start(f32[2,8,256]{2,1,0:T(8,128)S(1)} %slice.13), channel_id=1, source_target_pairs={{0,2},{2,0},{4,6},{6,4},{8,10},{10,8},{12,14},{14,12},{16,18},{18,... | collective-permute-start | bytes 49160 | tf_op jit(solution)/shard_map/ppermute | solution.py:403
  31.4 0.0 collective-permute-done.9.oc
  31.4 0.8 %collective-permute-done.8.ec = f32[2,8,256]{2,1,0:T(8,128)S(1)} collective-permute-done((f32[2,8,256]{2,1,0:T(8,128)S(1)}, f32[2,8,256]{2,1,0:T(8,128)S(1)}, u32[]{:S(2)}, u32[]{:S(2)}) %collective-permute-start.8) | collective-permute-done | bytes 16416 | tf_op jit(solution)/shard_map/ppermute | solution.py:403
  32.2 0.0 collective-permute-done.5.e
  32.2 0.0 collective-permute-done.6.o
  32.2 0.0 copy-done.1
  32.2 2.1 %shard_map.86 = (f32[19,2,16,256]{3,2,1,0:T(8,128)}, f32[19,2,16,256]{3,2,1,0:T(8,128)}, f32[2,16,256]{2,1,0:T(8,128)}, f32[1,128]{1,0:T(1,128)S(1)}) custom-call(s32[1]{0:T(128)} %bitcast.parity_ref, f32[19,2,16,256]{3,2,1,0:T(8,128)S(1)} %get-tuple-element.25.post, f32[19,2,16,256]{3,2,1,0:T(8,128)S(1)} %get-tuple-element.26.adj, ...), custom_call_target="tpu_custom_call" | custom-call | tf_op jit(solution)/shard_map/pallas_call | solution.py:371
  34.3 2.0 %collective-permute-start.10 = (f32[1,128]{1,0:T(1,128)S(1)}, f32[1,128]{1,0:T(1,128)S(1)}, u32[]{:S(2)}, u32[]{:S(2)}) collective-permute-start(f32[1,128]{1,0:T(1,128)S(1)} %get-tuple-element.35), channel_id=1, source_target_pairs={{0,1},{1,0},{2,3},{3,2},{4,5},{5,4},{6,7},{7,6},{8,9},{9,8},{10,11... | collective-permute-start | bytes 1544 | tf_op jit(solution)/shard_map/ppermute | solution.py:416
  36.3 1.6 %collective-permute-done.10 = f32[1,128]{1,0:T(1,128)S(1)} collective-permute-done((f32[1,128]{1,0:T(1,128)S(1)}, f32[1,128]{1,0:T(1,128)S(1)}, u32[]{:S(2)}, u32[]{:S(2)}) %collective-permute-start.10) | collective-permute-done | bytes 544 | tf_op jit(solution)/shard_map/ppermute | solution.py:416
  37.9 0.2 collective-permute-start.11
  38.1 0.9 %collective-permute-done.11 = f32[1,128]{1,0:T(1,128)S(1)} collective-permute-done((f32[1,128]{1,0:T(1,128)S(1)}, f32[1,128]{1,0:T(1,128)S(1)}, u32[]{:S(2)}, u32[]{:S(2)}) %collective-permute-start.11) | collective-permute-done | bytes 544 | tf_op jit(solution)/shard_map/ppermute | solution.py:416
  39.0 3.1 %collective-permute-start.12 = (f32[1,128]{1,0:T(1,128)S(1)}, f32[1,128]{1,0:T(1,128)S(1)}, u32[]{:S(2)}, u32[]{:S(2)}) collective-permute-start(f32[1,128]{1,0:T(1,128)S(1)} %add.21), channel_id=1, source_target_pairs={{0,4},{2,6},{4,0},{6,2},{8,12},{10,14},{12,8},{14,10},{16,20},{18,... | collective-permute-start | bytes 1544 | tf_op jit(solution)/shard_map/ppermute | solution.py:416
  42.1 1.5 %collective-permute-done.12 = f32[1,128]{1,0:T(1,128)S(1)} collective-permute-done((f32[1,128]{1,0:T(1,128)S(1)}, f32[1,128]{1,0:T(1,128)S(1)}, u32[]{:S(2)}, u32[]{:S(2)}) %collective-permute-start.12) | collective-permute-done | bytes 544 | tf_op jit(solution)/shard_map/ppermute | solution.py:416
  43.6 3.5 %collective-permute-start.13 = (f32[1,128]{1,0:T(1,128)S(1)}, f32[1,128]{1,0:T(1,128)S(1)}, u32[]{:S(2)}, u32[]{:S(2)}) collective-permute-start(f32[1,128]{1,0:T(1,128)S(1)} %add.22), channel_id=1, source_target_pairs={{0,8},{2,10},{4,12},{6,14},{8,0},{10,2},{12,4},{14,6},{16,24},{18,... | collective-permute-start | bytes 1544 | tf_op jit(solution)/shard_map/ppermute | solution.py:416
  47.1 1.5 %collective-permute-done.13 = f32[1,128]{1,0:T(1,128)S(1)} collective-permute-done((f32[1,128]{1,0:T(1,128)S(1)}, f32[1,128]{1,0:T(1,128)S(1)}, u32[]{:S(2)}, u32[]{:S(2)}) %collective-permute-start.13) | collective-permute-done | bytes 544 | tf_op jit(solution)/shard_map/ppermute | solution.py:416
  48.6 3.2 %collective-permute-start.14 = (f32[1,128]{1,0:T(1,128)S(1)}, f32[1,128]{1,0:T(1,128)S(1)}, u32[]{:S(2)}, u32[]{:S(2)}) collective-permute-start(f32[1,128]{1,0:T(1,128)S(1)} %add.23), channel_id=1, source_target_pairs={{0,16},{2,18},{4,20},{6,22},{8,24},{10,26},{12,28},{14,30},{16,0},... | collective-permute-start | bytes 1544 | tf_op jit(solution)/shard_map/ppermute | solution.py:416
  51.8 1.5 %collective-permute-done.14 = f32[1,128]{1,0:T(1,128)S(1)} collective-permute-done((f32[1,128]{1,0:T(1,128)S(1)}, f32[1,128]{1,0:T(1,128)S(1)}, u32[]{:S(2)}, u32[]{:S(2)}) %collective-permute-start.14) | collective-permute-done | bytes 544 | tf_op jit(solution)/shard_map/ppermute | solution.py:416
  53.4 0.5 slice_bitcast_fusion
  (7 shorter events, 0.0 us)
Async XLA Ops:
  0.6 1.1 %copy-start = (f32[19,2,16,256]{3,2,1,0:T(8,128)S(1)}, f32[19,2,16,256]{3,2,1,0:T(8,128)}, u32[]{:S(2)}) copy-start(f32[19,2,16,256]{3,2,1,0:T(8,128)} %pops.3) | copy-start | bytes 1867780
  1.7 1.1 %copy-start.2 = (f32[19,2,16,256]{3,2,1,0:T(8,128)S(1)}, f32[19,2,16,256]{3,2,1,0:T(8,128)}, u32[]{:S(2)}) copy-start(f32[19,2,16,256]{3,2,1,0:T(8,128)} %seed.3) | copy-start | bytes 1867780
  2.8 0.8 %copy-start.4 = (f32[2,16,256]{2,1,0:T(8,128)S(1)}, f32[2,16,256]{2,1,0:T(8,128)}, u32[]{:S(2)}) copy-start(f32[2,16,256]{2,1,0:T(8,128)} %porous.5) | copy-start | bytes 98308
  3.6 0.8 %copy-start.6 = (s32[2,16,256]{2,1,0:T(8,128)S(1)}, s32[2,16,256]{2,1,0:T(8,128)}, u32[]{:S(2)}) copy-start(s32[2,16,256]{2,1,0:T(8,128)} %types.5) | copy-start | bytes 98308
  4.3 0.8 %copy-start.8 = (s32[2,16,256]{2,1,0:T(8,128)S(1)}, s32[2,16,256]{2,1,0:T(8,128)}, u32[]{:S(2)}) copy-start(s32[2,16,256]{2,1,0:T(8,128)} %regions.5) | copy-start | bytes 98308
  5.1 13.0 %copy-start.3 = (f32[19,2,16,256]{3,2,1,0:T(8,128)S(1)}, f32[19,2,16,256]{3,2,1,0:T(8,128)}, u32[]{:S(2)}) copy-start(f32[19,2,16,256]{3,2,1,0:T(8,128)} %seed.3) | copy-start | bytes 1867780
  5.1 13.0 %copy-start.7 = (s32[2,16,256]{2,1,0:T(8,128)S(1)}, s32[2,16,256]{2,1,0:T(8,128)}, u32[]{:S(2)}) copy-start(s32[2,16,256]{2,1,0:T(8,128)} %types.5) | copy-start | bytes 98308
  5.9 12.2 %copy-start.5 = (f32[2,16,256]{2,1,0:T(8,128)S(1)}, f32[2,16,256]{2,1,0:T(8,128)}, u32[]{:S(2)}) copy-start(f32[2,16,256]{2,1,0:T(8,128)} %porous.5) | copy-start | bytes 98308
  5.9 12.1 %collective-permute-start = (f32[11,16,256]{2,1,0:T(8,128)S(1)}, f32[11,16,256]{2,1,0:T(8,128)S(1)}, u32[]{:S(2)}, u32[]{:S(2)}) collective-permute-start(f32[11,16,256]{2,1,0:T(8,128)S(1)} %get-tuple-element.22), channel_id=1, source_target_pairs={{0,2},{2,0},{4,6},{6,4},{8,10},{10,8},{12,14},{14,12},{16,18},{18,... | collective-permute-start | bytes 540680 | tf_op jit(solution)/shard_map/ppermute | solution.py:400
  6.4 11.6 %collective-permute-start.1 = (f32[11,16,256]{2,1,0:T(8,128)S(1)}, f32[11,16,256]{2,1,0:T(8,128)S(1)}, u32[]{:S(2)}, u32[]{:S(2)}) collective-permute-start(f32[11,16,256]{2,1,0:T(8,128)S(1)} %get-tuple-element.23), channel_id=1, source_target_pairs={{2,4},{4,2},{6,8},{8,6},{10,12},{12,10},{14,16},{16,14},{18,20},{2... | collective-permute-start | bytes 540680 | tf_op jit(solution)/shard_map/ppermute | solution.py:401
  7.1 4.7 %collective-permute-start.2 = (f32[6,8,256]{2,1,0:T(8,128)S(1)}, f32[6,8,256]{2,1,0:T(8,128)S(1)}, u32[]{:S(2)}, u32[]{:S(2)}) collective-permute-start(f32[6,8,256]{2,1,0:T(8,128)S(1)} %get-tuple-element.24), channel_id=1, source_target_pairs={{0,1},{1,0},{2,3},{3,2},{4,5},{5,4},{6,7},{7,6},{8,9},{9,8},{10,11... | collective-permute-start | bytes 147464 | tf_op jit(solution)/shard_map/ppermute | solution.py:393
  11.7 5.4 %collective-permute-start.4 = (f32[2,8,256]{2,1,0:T(8,128)S(1)}, f32[2,8,256]{2,1,0:T(8,128)S(1)}, u32[]{:S(2)}, u32[]{:S(2)}) collective-permute-start(f32[2,8,256]{2,1,0:T(8,128)S(1)} %slice.12), channel_id=1, source_target_pairs={{2,4},{4,2},{6,8},{8,6},{10,12},{12,10},{14,16},{16,14},{18,20},{2... | collective-permute-start | bytes 49160 | tf_op jit(solution)/shard_map/ppermute | solution.py:404
  12.4 5.6 %collective-permute-start.3 = (f32[2,8,256]{2,1,0:T(8,128)S(1)}, f32[2,8,256]{2,1,0:T(8,128)S(1)}, u32[]{:S(2)}, u32[]{:S(2)}) collective-permute-start(f32[2,8,256]{2,1,0:T(8,128)S(1)} %slice.12), channel_id=1, source_target_pairs={{0,2},{2,0},{4,6},{6,4},{8,10},{10,8},{12,14},{14,12},{16,18},{18,... | collective-permute-start | bytes 49160 | tf_op jit(solution)/shard_map/ppermute | solution.py:403
  18.1 14.2 %copy-start.1 = (f32[19,2,16,256]{3,2,1,0:T(8,128)S(1)}, f32[19,2,16,256]{3,2,1,0:T(8,128)}, u32[]{:S(2)}) copy-start(f32[19,2,16,256]{3,2,1,0:T(8,128)} %pops.3) | copy-start | bytes 1867780
  19.4 12.8 %collective-permute-start.5 = (f32[10,16,256]{2,1,0:T(8,128)S(1)}, f32[10,16,256]{2,1,0:T(8,128)S(1)}, u32[]{:S(2)}, u32[]{:S(2)}) collective-permute-start(f32[10,16,256]{2,1,0:T(8,128)S(1)} %get-tuple-element.29), channel_id=1, source_target_pairs={{0,2},{2,0},{4,6},{6,4},{8,10},{10,8},{12,14},{14,12},{16,18},{18,... | collective-permute-start | bytes 491528 | tf_op jit(solution)/shard_map/ppermute | solution.py:400
  20.5 11.7 %collective-permute-start.6 = (f32[10,16,256]{2,1,0:T(8,128)S(1)}, f32[10,16,256]{2,1,0:T(8,128)S(1)}, u32[]{:S(2)}, u32[]{:S(2)}) collective-permute-start(f32[10,16,256]{2,1,0:T(8,128)S(1)} %get-tuple-element.30), channel_id=1, source_target_pairs={{2,4},{4,2},{6,8},{8,6},{10,12},{12,10},{14,16},{16,14},{18,20},{2... | collective-permute-start | bytes 491528 | tf_op jit(solution)/shard_map/ppermute | solution.py:401
  21.1 4.2 %collective-permute-start.7 = (f32[6,8,256]{2,1,0:T(8,128)S(1)}, f32[6,8,256]{2,1,0:T(8,128)S(1)}, u32[]{:S(2)}, u32[]{:S(2)}) collective-permute-start(f32[6,8,256]{2,1,0:T(8,128)S(1)} %get-tuple-element.31), channel_id=1, source_target_pairs={{0,1},{1,0},{2,3},{3,2},{4,5},{5,4},{6,7},{7,6},{8,9},{9,8},{10,11... | collective-permute-start | bytes 147464 | tf_op jit(solution)/shard_map/ppermute | solution.py:393
  25.3 6.1 %collective-permute-start.9 = (f32[2,8,256]{2,1,0:T(8,128)S(1)}, f32[2,8,256]{2,1,0:T(8,128)S(1)}, u32[]{:S(2)}, u32[]{:S(2)}) collective-permute-start(f32[2,8,256]{2,1,0:T(8,128)S(1)} %slice.13), channel_id=1, source_target_pairs={{2,4},{4,2},{6,8},{8,6},{10,12},{12,10},{14,16},{16,14},{18,20},{2... | collective-permute-start | bytes 49160 | tf_op jit(solution)/shard_map/ppermute | solution.py:404
  25.9 6.3 %collective-permute-start.8 = (f32[2,8,256]{2,1,0:T(8,128)S(1)}, f32[2,8,256]{2,1,0:T(8,128)S(1)}, u32[]{:S(2)}, u32[]{:S(2)}) collective-permute-start(f32[2,8,256]{2,1,0:T(8,128)S(1)} %slice.13), channel_id=1, source_target_pairs={{0,2},{2,0},{4,6},{6,4},{8,10},{10,8},{12,14},{14,12},{16,18},{18,... | collective-permute-start | bytes 49160 | tf_op jit(solution)/shard_map/ppermute | solution.py:403
  34.3 3.5 %collective-permute-start.10 = (f32[1,128]{1,0:T(1,128)S(1)}, f32[1,128]{1,0:T(1,128)S(1)}, u32[]{:S(2)}, u32[]{:S(2)}) collective-permute-start(f32[1,128]{1,0:T(1,128)S(1)} %get-tuple-element.35), channel_id=1, source_target_pairs={{0,1},{1,0},{2,3},{3,2},{4,5},{5,4},{6,7},{7,6},{8,9},{9,8},{10,11... | collective-permute-start | bytes 1544 | tf_op jit(solution)/shard_map/ppermute | solution.py:416
  37.9 1.1 %collective-permute-start.11 = (f32[1,128]{1,0:T(1,128)S(1)}, f32[1,128]{1,0:T(1,128)S(1)}, u32[]{:S(2)}, u32[]{:S(2)}) collective-permute-start(f32[1,128]{1,0:T(1,128)S(1)} %add.20), channel_id=1, source_target_pairs={{0,2},{2,0},{4,6},{6,4},{8,10},{10,8},{12,14},{14,12},{16,18},{18,... | collective-permute-start | bytes 1544 | tf_op jit(solution)/shard_map/ppermute | solution.py:416
  39.0 4.6 %collective-permute-start.12 = (f32[1,128]{1,0:T(1,128)S(1)}, f32[1,128]{1,0:T(1,128)S(1)}, u32[]{:S(2)}, u32[]{:S(2)}) collective-permute-start(f32[1,128]{1,0:T(1,128)S(1)} %add.21), channel_id=1, source_target_pairs={{0,4},{2,6},{4,0},{6,2},{8,12},{10,14},{12,8},{14,10},{16,20},{18,... | collective-permute-start | bytes 1544 | tf_op jit(solution)/shard_map/ppermute | solution.py:416
  43.6 5.0 %collective-permute-start.13 = (f32[1,128]{1,0:T(1,128)S(1)}, f32[1,128]{1,0:T(1,128)S(1)}, u32[]{:S(2)}, u32[]{:S(2)}) collective-permute-start(f32[1,128]{1,0:T(1,128)S(1)} %add.22), channel_id=1, source_target_pairs={{0,8},{2,10},{4,12},{6,14},{8,0},{10,2},{12,4},{14,6},{16,24},{18,... | collective-permute-start | bytes 1544 | tf_op jit(solution)/shard_map/ppermute | solution.py:416
  48.6 4.7 %collective-permute-start.14 = (f32[1,128]{1,0:T(1,128)S(1)}, f32[1,128]{1,0:T(1,128)S(1)}, u32[]{:S(2)}, u32[]{:S(2)}) collective-permute-start(f32[1,128]{1,0:T(1,128)S(1)} %add.23), channel_id=1, source_target_pairs={{0,16},{2,18},{4,20},{6,22},{8,24},{10,26},{12,28},{14,30},{16,0},... | collective-permute-start | bytes 1544 | tf_op jit(solution)/shard_map/ppermute | solution.py:416
where the time goes:
time: 54.4 us; the launch traced here: 53.9 us
  starting transfers between devices  31 us (57%)
  waiting for transfers between devices  12.9 us (24%)
  local copies, waits for them, and re-layouts  4.96 us (9%)
  Pallas kernels  4.25 us (8%)
  between operations  0.76 us (1%)
    ppermute x5, starting transfers between devices, sum_all(): x = x + lax.ppermute(x, axis, [(i, i ^ step) for i in range(size)])  11.9 us
    ppermute x2, starting transfers between devices, exchange(): ec = lax.ppermute(corners, 'ax', even_pairs(size_a))  10.2 us
    ppermute x5, waiting for transfers between devices, sum_all(): x = x + lax.ppermute(x, axis, [(i, i ^ step) for i in range(size)])  7.06 us
    ppermute x2, starting transfers between devices, exchange(): t = lax.ppermute(t_msg, 'az', ring)  4.68 us
    unnamed x18, local copies, waits for them, and re-layouts  4.44 us
    pallas_call x3, Pallas kernels, call(): pl.pallas_call(body, out_shape=[jax.ShapeDtypeStruct(s, jnp.float32) for...  4.25 us
    ppermute x2, waiting for transfers between devices, exchange(): t = lax.ppermute(t_msg, 'az', ring)  4.14 us
    ppermute x2, waiting for transfers between devices, exchange(): ec = lax.ppermute(corners, 'ax', even_pairs(size_a))  1.67 us
  transfers between devices with their start and end apart: 15, of which 9 were waited for; matrix products, arithmetic and copies ran while one was open for 0% of the time, Pallas kernels for 0%

commit v1 on v0

--- a/solution.py
+++ b/solution.py
@@ -40,37 +40,41 @@
 
 
 LO, HI = 0, 1
-POST, ADJ, FLAG = 0, 1, 2
-
-
-def face_fields(axis, side):
+POST, ADJ, FACTOR, FLAG = 0, 1, 2, 3
+
+
+def face_fields(kinds, axis, side):
     sign = -1 if side == LO else 1
-    fields = [(POST, q) for q in moving(axis, sign)] + [(ADJ, q) for q in moving(axis, -sign)]
-    return fields + [(FLAG, 0)]
-
-
-AX_SLOT = [{key: i for i, key in enumerate(face_fields(0, side))} for side in (LO, HI)]
-
-
-def azimuthal_rows():
-    place, corner, rest = {}, [[], []], []
-    for a, sign, block in ((1, 1, 0), (0, -1, 1)):
-        for side in (LO, HI):
-            for kind, q in face_fields(1, side):
-                leaves = VELOCITY[q][0] == (sign if kind == POST else -sign)
-                if kind == FLAG or leaves:
-                    corner[block].append((side, kind, q, a))
-                else:
-                    rest.append((side, kind, q, a))
-    for block in (0, 1):
-        for i, key in enumerate(corner[block]):
-            place[key] = (block, i)
-    for i, key in enumerate(rest):
-        place[key] = (2 + i // 8, i % 8)
-    return place, 2 + (len(rest) + 7) // 8
-
-
-AZ_PLACE, AZ_BLOCKS = azimuthal_rows()
+    fields = []
+    for kind in kinds:
+        if kind == FLAG:
+            fields.append((FLAG, 0))
+        else:
+            fields += [(kind, q) for q in moving(axis, -sign if kind == ADJ else sign)]
+    return fields
+
+
+class Layout:
+    def __init__(self, kinds, extra):
+        self.ax = [face_fields(kinds, 0, side) for side in (LO, HI)]
+        self.slot = [{key: i for i, key in enumerate(fields)} for fields in self.ax]
+        self.fields = len(self.ax[LO])
+        corner, rest = [], []
+        for a, sign in ((1, 1), (0, -1)):
+            for side in (LO, HI):
+                for kind, q in face_fields(kinds, 1, side):
+                    leaves = VELOCITY[q][0] == (-sign if kind == ADJ else sign)
+                    key = (side, kind, q, a)
+                    (corner if kind == FLAG or leaves else rest).append(key)
+        corner += extra
+        self.corner_blocks = -(-len(corner) // 8)
+        self.blocks = self.corner_blocks + -(-len(rest) // 8)
+        self.place = {key: (i // 8, i % 8) for i, key in enumerate(corner)}
+        self.place.update({key: (self.corner_blocks + i // 8, i % 8) for i, key in enumerate(rest)})
+
+
+FIRST = Layout((POST, ADJ, FACTOR, FLAG), [(LO, "label"), (HI, "label")])
+SECOND = Layout((POST, ADJ), [(LO, "sum")])
 
 
 def pairs_of(values):
@@ -199,34 +203,38 @@
 
 
 class Fields:
-    def __init__(self, own, halo):
-        self.own = own
-        self.halo = halo
-        up_e = halo["parity"] == 0
-        self.up_e = up_e
+    def __init__(self, layout, own, parity, e, o, t, ec, oc):
+        self.layout, self.own = layout, own
+        self.e, self.o, self.t, self.ec, self.oc = e, o, t, ec, oc
+        self.up_e = parity == 0
+        self.rows_a = own[POST].shape[1]
 
     def row(self, kind, q, a):
-        rows_a = self.own[POST].shape[1]
-        if 0 <= a < rows_a:
+        if 0 <= a < self.rows_a:
             return self.own[FLAG][a] if kind == FLAG else self.own[kind][q, a]
-        e, o = self.halo["e"], self.halo["o"]
         if a < 0:
-            slot = AX_SLOT[HI][(kind, q)]
-            return jnp.where(self.up_e, o[slot], e[slot])
-        slot = AX_SLOT[LO][(kind, q)]
-        return jnp.where(self.up_e, e[slot], o[slot])
+            slot = self.layout.slot[HI][(kind, q)]
+            return jnp.where(self.up_e, self.o[slot], self.e[slot])
+        slot = self.layout.slot[LO][(kind, q)]
+        return jnp.where(self.up_e, self.e[slot], self.o[slot])
+
+    def row_label(self, a):
+        slot = self.layout.fields
+        e, o = self.e[slot, 0:1, :], self.o[slot, 0:1, :]
+        return jnp.where(self.up_e, o, e) if a < 0 else jnp.where(self.up_e, e, o)
+
+    def message(self, key, a):
+        block, i = self.layout.place[key]
+        rows = (block, slice(i, i + 1))
+        if 0 <= a < self.rows_a:
+            return self.t[rows]
+        if a < 0:
+            return jnp.where(self.up_e, self.oc[rows], self.ec[rows])
+        return jnp.where(self.up_e, self.ec[rows], self.oc[rows])
 
     def edge(self, side, kind, q, a):
-        rows_a = self.own[POST].shape[1]
-        if 0 <= a < rows_a:
-            block, i = AZ_PLACE[(side, kind, q, a)]
-            return self.halo["t"][block, i : i + 1, :]
-        ec, oc = self.halo["ec"], self.halo["oc"]
-        if a < 0:
-            block, i = AZ_PLACE[(side, kind, q, 1)]
-            return jnp.where(self.up_e, oc[block, i : i + 1, :], ec[block, i : i + 1, :])
-        block, i = AZ_PLACE[(side, kind, q, 0)]
-        return jnp.where(self.up_e, ec[block, i : i + 1, :], oc[block, i : i + 1, :])
+        row = self.rows_a - 1 if a < 0 else 0 if a >= self.rows_a else a
+        return self.message((side, kind, q, row), a)
 
     def moved(self, kind, q, a, shift):
         sa, st, sr = shift
@@ -242,36 +250,30 @@
         return value
 
 
-def pack(own, parity, e_ref, o_ref, t_ref):
+def pack(layout, own, parity, e_ref, o_ref, t_ref):
     rows_a, rows_t = own[POST].shape[1], own[POST].shape[2]
-    with_flags = FLAG in own
     even = parity == 0
 
     def cells(kind, q, a):
-        return own[FLAG][a] if kind == FLAG else own[kind][q, a]
-
-    for slot in range(len(AX_SLOT[LO])):
-        low = [key for key, i in AX_SLOT[LO].items() if i == slot][0]
-        high = [key for key, i in AX_SLOT[HI].items() if i == slot][0]
-        if low[0] == FLAG and not with_flags:
-            continue
-        low, high = cells(*low, 0), cells(*high, rows_a - 1)
+        return own[FLAG].at[a] if kind == FLAG else own[kind].at[q, a]
+
+    for key, (block, i) in layout.place.items():
+        if len(key) == 4:
+            side, kind, q, a = key
+            t = 0 if side == LO else rows_t - 1
+            t_ref[block, i : i + 1, :] = cells(kind, q, a)[t : t + 1, :]
+    for slot in range(layout.fields):
+        low = cells(*layout.ax[LO][slot], 0)[...]
+        high = cells(*layout.ax[HI][slot], rows_a - 1)[...]
         e_ref[slot] = jnp.where(even, high, low)
         o_ref[slot] = jnp.where(even, low, high)
-    for (side, kind, q, a), (block, i) in AZ_PLACE.items():
-        if kind == FLAG and not with_flags:
-            continue
-        t = 0 if side == LO else rows_t - 1
-        source = own[FLAG].at[a] if kind == FLAG else own[kind].at[q, a]
-        t_ref[block, i : i + 1, :] = source[t : t + 1, :]
-
-
-def chunks(shape, body):
-    rows_a, rows_t, rows_r = shape
-    counts = (rows_a, rows_t // 8, rows_r // 128)
+
+
+def chunks(rows_a, shape, body):
+    counts = (len(rows_a), shape[1] // 8, shape[2] // 128)
 
     def step(i, carry):
-        a = i // (counts[1] * counts[2])
+        a = rows_a[0] + i // (counts[1] * counts[2])
         t = pl.multiple_of((i // counts[2]) % counts[1] * 8, 8)
         r = pl.multiple_of(i % counts[2] * 128, 128)
         body((a, pl.ds(t, 8), pl.ds(r, 128)))
@@ -289,31 +291,75 @@
         ref[(q,) + where] = values[q]
 
 
-def first_kernel(parity_ref, pops, seed, porous, types, regions, post, e_out, o_out, t_out, flags):
+def label_of(regions, wide):
+    label = jnp.max(jnp.max(regions[...], axis=0), axis=(0, 1), keepdims=True)
+    return jnp.broadcast_to(label.astype(jnp.float32), (1, wide))
+
+
+def porosity_factors(lin):
+    ua, ut, ur = lin["u"]
+    weight = -(lin["design"] * lin["rho"])
+    still = -1.5 * (ua * ua + ut * ut + ur * ur)
+    result = [(1.0 / 3.0) * weight * still]
+    for i, cu in enumerate(projections((ua, ut, ur))):
+        scaled = (W_AXIS if i < 3 else W_EDGE) * weight
+        even, odd = scaled * (still + 4.5 * cu * cu), 3.0 * scaled * cu
+        result += [even + odd, even - odd]
+    return result
+
+
+def first_kernel(
+    parity_ref, pops_hbm, seed_hbm, porous_hbm, types_hbm, regions_hbm,
+    post, factors, e_out, o_out, t_out, flags, pops, seed, porous, types, regions, sems,
+):
+    rows_a = porous.shape[0]
+    loads = [
+        pltpu.make_async_copy(source, target, sems.at[i])
+        for i, (source, target) in enumerate(
+            [(types_hbm, types), (regions_hbm, regions), (porous_hbm, porous)]
+            + [(pops_hbm.at[:, a], pops.at[:, a]) for a in range(rows_a)]
+            + [(seed_hbm, seed)]
+        )
+    ]
+    for copy in loads:
+        copy.start()
+    for copy in loads[:3]:
+        copy.wait()
+    flags[...] = jnp.where(types[...] != 1, 1.0, 0.0)
+    label = label_of(regions, porous.shape[2])
+    for side in (LO, HI):
+        block, i = FIRST.place[(side, "label")]
+        t_out[block, i : i + 1, :] = label
+    for out in (e_out, o_out):
+        out[FIRST.fields] = jnp.broadcast_to(label, out.shape[1:])
+
     def body(where):
         values = load(pops, where)
         lin = linearise(values, porous[where], types[where], regions[where])
         store(post, where, collide(values, lin))
-
-    chunks(porous.shape, body)
-    flags[...] = jnp.where(types[...] != 1, 1.0, 0.0)
-    pack({POST: post, ADJ: seed, FLAG: flags}, parity_ref[0], e_out, o_out, t_out)
+        store(factors, where, porosity_factors(lin))
+
+    for a in range(rows_a):
+        loads[3 + a].wait()
+        chunks([a], porous.shape, body)
+    loads[-1].wait()
+    own = {POST: post, ADJ: seed, FACTOR: factors, FLAG: flags}
+    pack(FIRST, own, parity_ref[0], e_out, o_out, t_out)
 
 
 def second_kernel(
-    parity_ref, post, seed, flags, porous, types, regions, e, o, t, ec, oc,
-    post_next, adj, sens, around, e_out, o_out, t_out, state, back,
+    parity_ref, post, seed, factors, flags, porous, types, regions, e, o, t, ec, oc,
+    post_next, adj, sens, around, e_out, o_out, t_out, state, back, parts,
 ):
-    halo = dict(parity=parity_ref[0], e=e, o=o, t=t, ec=ec, oc=oc)
-    fields = Fields({POST: post, ADJ: seed, FLAG: flags}, halo)
-    rows_a = porous.shape[0]
+    own = {POST: post, ADJ: seed, FACTOR: factors, FLAG: flags}
+    fields = Fields(FIRST, own, parity_ref[0], e, o, t, ec, oc)
+    rows_a, rows_t, rows_r = porous.shape
     for a in range(rows_a):
         centre = flags[a]
         state[0, a] = post[0, a]
         back[0, a] = seed[0, a]
         for q in range(1, 19):
-            direc = VELOCITY[q]
-            behind = tuple(-c for c in direc)
+            behind = tuple(-c for c in VELOCITY[q])
             open_ = fields.moved(FLAG, 0, a, behind)
             around[q - 1, a] = open_
             opp = OPPOSITE[q]
@@ -328,53 +374,90 @@
         store(adj, where, result)
         sens[where] = partial_sens
 
-    chunks(porous.shape, body)
-    pack({POST: post_next, ADJ: adj}, parity_ref[0], e_out, o_out, t_out)
+    chunks(range(rows_a), porous.shape, body)
+    pack(SECOND, {POST: post_next, ADJ: adj}, parity_ref[0], e_out, o_out, t_out)
+    sums = {(i, st): [] for i in (-1, 0, 1) for st in (-1, 0, 1)}
+    for a in range(rows_a):
+        sums[(0, 0)] += [sens[a], factors[0, a] * adj[0, a]]
+        for q in range(1, 19):
+            behind = tuple(-c for c in VELOCITY[q])
+            open_, value = around[q - 1, a], adj[q, a]
+            sums[(0, 0)].append(jnp.where(open_ > 0, 0.0, factors[OPPOSITE[q], a]) * value)
+            term = jnp.where(open_ > 0, fields.moved(FACTOR, q, a, behind), 0.0) * value
+            from_a = a + behind[0]
+            beyond = -1 if from_a < 0 else 1 if from_a >= rows_a else 0
+            sums[(beyond, behind[1])].append(term)
+    at_t = lax.broadcasted_iota(jnp.int32, (rows_t, rows_r), 0)
+    rows = []
+    for beyond in (-1, 0, 1):
+        low, centre, high = (functools.reduce(jnp.add, sums[(beyond, st)]) for st in (-1, 0, 1))
+        inner = centre + jnp.where(at_t == 0, 0.0, low) + jnp.where(at_t == rows_t - 1, 0.0, high)
+        label = label_of(regions, rows_r) if beyond == 0 else fields.row_label(beyond)
+        a = {-1: -1, 0: 0, 1: rows_a}[beyond]
+        rows.append((jnp.sum(inner, axis=0, keepdims=True), label))
+        rows.append((high[rows_t - 1 : rows_t], fields.message((LO, "label"), a)))
+        rows.append((low[0:1], fields.message((HI, "label"), a)))
+    parts[...] = jnp.zeros_like(parts)
+    for i, (value, label) in enumerate(rows):
+        parts[0, i : i + 1, :] = value
+        parts[1, i : i + 1, :] = label
+    lanes = lax.broadcasted_iota(jnp.int32, parts.shape[1:], 1) + 1
+    total = jnp.sum(parts[0], axis=1, keepdims=True)
+    chosen = jnp.where(lanes == parts[1].astype(jnp.int32), total, 0.0)
+    block, i = SECOND.place[(LO, "sum")]
+    t_out[block, i : i + 1, :] = jnp.sum(chosen, axis=0, keepdims=True)
 
 
 def third_kernel(
     parity_ref, post, adj, flags, around, pops, porous, types, regions, sens_one, e, o, t, ec, oc,
-    final, result, sens, totals, back, acc,
+    final_hbm, result_hbm, sens, final, result, back, sems,
 ):
-    halo = dict(parity=parity_ref[0], e=e, o=o, t=t, ec=ec, oc=oc)
-    fields = Fields({POST: post, ADJ: adj, FLAG: flags}, halo)
+    fields = Fields(SECOND, {POST: post, ADJ: adj}, parity_ref[0], e, o, t, ec, oc)
     rows_a = porous.shape[0]
+    stores = []
     for a in range(rows_a):
-        centre = flags[a]
         final[0, a] = post[0, a]
-        back[0, a] = adj[0, a]
         for q in range(1, 19):
             behind = tuple(-c for c in VELOCITY[q])
-            open_ = around[q - 1, a]
-            opp = OPPOSITE[q]
-            final[q, a] = jnp.where(open_ > 0, fields.moved(POST, q, a, behind), post[opp, a])
-            back[opp, a] = centre * fields.moved(ADJ, opp, a, behind) + (1.0 - open_) * adj[q, a]
-    acc[...] = jnp.zeros_like(acc)
+            moved = fields.moved(POST, q, a, behind)
+            final[q, a] = jnp.where(around[q - 1, a] > 0, moved, post[OPPOSITE[q], a])
+        stores.append(pltpu.make_async_copy(final.at[:, a], final_hbm.at[:, a], sems.at[a]))
+        stores[-1].start()
 
     def body(where):
         values = load(pops, where)
         lin = linearise(values, porous[where], types[where], regions[where])
         adjoint, partial_sens = pull_back(load(back, where), values, lin)
         store(result, where, adjoint)
-        both = partial_sens + sens_one[where]
-        sens[where] = both
-        acc[...] += jnp.where(regions[where] > 0, both, 0.0)
-
-    chunks(porous.shape, body)
-    label = jnp.max(regions[...], axis=(0, 1, 2), keepdims=True)[0]
-    total = jnp.sum(acc[...], axis=(0, 1), keepdims=True)
-    lanes = lax.broadcasted_iota(jnp.int32, totals.shape, 1) + 1
-    totals[...] = jnp.where(lanes == label, total, 0.0)
-
-
-def call(body, out_shapes, scratch, parity, *arrays):
+        sens[where] = partial_sens + sens_one[where]
+
+    for a in range(rows_a):
+        centre = flags[a]
+        back[0, a] = adj[0, a]
+        for q in range(1, 19):
+            behind = tuple(-c for c in VELOCITY[q])
+            opp = OPPOSITE[q]
+            ahead = centre * fields.moved(ADJ, opp, a, behind)
+            back[opp, a] = ahead + (1.0 - around[q - 1, a]) * adj[q, a]
+        chunks([a], porous.shape, body)
+        stores.append(pltpu.make_async_copy(result.at[:, a], result_hbm.at[:, a], sems.at[rows_a + a]))
+        stores[-1].start()
+    for copy in stores:
+        copy.wait()
+
+
+VMEM, HBM = pltpu.VMEM, pltpu.HBM
+
+
+def call(body, in_spaces, outs, scratch, parity, *arrays):
+    spaces = in_spaces + [VMEM] * (len(arrays) - len(in_spaces))
     return pl.pallas_call(
         body,
-        out_shape=[jax.ShapeDtypeStruct(s, jnp.float32) for s in out_shapes],
+        out_shape=[jax.ShapeDtypeStruct(shape, jnp.float32) for shape, _ in outs],
         in_specs=[pl.BlockSpec(memory_space=pltpu.SMEM)]
-        + [pl.BlockSpec(memory_space=pltpu.VMEM)] * len(arrays),
-        out_specs=[pl.BlockSpec(memory_space=pltpu.VMEM)] * len(out_shapes),
-        scratch_shapes=[pltpu.VMEM(s, jnp.float32) for s in scratch],
+        + [pl.BlockSpec(memory_space=space) for space in spaces],
+        out_specs=[pl.BlockSpec(memory_space=space) for _, space in outs],
+        scratch_shapes=scratch,
         compiler_params=pltpu.CompilerParams(vmem_limit_bytes=40 * 1024 * 1024),
     )(parity, *arrays)
 
@@ -387,67 +470,83 @@
     return [(i, ((i + 1) ^ 1) - 1) for i in range(size) if 0 <= ((i + 1) ^ 1) - 1 < size]
 
 
-def exchange(e_msg, o_msg, t_msg):
+def exchange(layout, e_msg, o_msg, t_msg, totals_row=None):
     size_a, size_t = lax.axis_size("ax"), lax.axis_size("az")
     ring = [(i, (i + 1) % size_t) for i in range(size_t)]
     t = lax.ppermute(t_msg, "az", ring)
     if size_t > 2:
-        from_high = np.zeros((AZ_BLOCKS, 8, 1), bool)
-        for (side, _, _, _), (block, i) in AZ_PLACE.items():
-            from_high[block, i] = side == HI
+        from_high = np.zeros((layout.blocks, 8, 1), bool)
+        for key, (block, i) in layout.place.items():
+            from_high[block, i] = key[0] == HI
         t_down = lax.ppermute(t_msg, "az", [(j, i) for i, j in ring])
         t = jnp.where(jnp.asarray(from_high), t, t_down)
     e = lax.ppermute(e_msg, "ax", even_pairs(size_a))
     o = lax.ppermute(o_msg, "ax", odd_pairs(size_a))
-    corners = t[:2]
+    corners = t[: layout.corner_blocks]
+    total = None
+    if totals_row is not None:
+        block, i = totals_row
+        total = t_msg[block, i : i + 1]
+        total = total + t[block, i : i + 1] if size_t == 2 else sum_over(total, "az", 1)
+        corners = lax.dynamic_update_slice(corners, total[None], (block, i, 0))
     ec = lax.ppermute(corners, "ax", even_pairs(size_a))
     oc = lax.ppermute(corners, "ax", odd_pairs(size_a))
-    return e, o, t, ec, oc
-
-
-def sum_all(x):
-    for axis in ("az", "ax"):
-        size = lax.axis_size(axis)
-        if size & (size - 1):
-            x = lax.psum(x, axis)
-            continue
-        step = 1
-        while step < size:
-            x = x + lax.ppermute(x, axis, [(i, i ^ step) for i in range(size)])
-            step *= 2
+    if totals_row is not None:
+        if size_a & (size_a - 1):
+            total = lax.psum(total, "ax")
+        elif size_a > 1:
+            total = sum_over(total + ec[block, i : i + 1], "ax", 2)
+    return (e, o, t, ec, oc), total
+
+
+def sum_over(x, axis, step):
+    size = lax.axis_size(axis)
+    if size & (size - 1):
+        return lax.psum(x, axis)
+    while step < size:
+        x = x + lax.ppermute(x, axis, [(i, i ^ step) for i in range(size)])
+        step *= 2
     return x
 
 
 def shards(initial, adjoint_seed, porosity, cell_type, region):
     cells = porosity.shape
     pops = (19,) + cells
-    fields = len(AX_SLOT[LO])
-    face, rows = cells[1:], (AZ_BLOCKS, 8, cells[2])
+    face, wide = cells[1:], cells[2]
     parity = (lax.axis_index("ax") % 2).astype(jnp.int32).reshape(1)
-    post, e, o, t, flags = call(
+    scratch = functools.partial(pltpu.VMEM, dtype=jnp.float32)
+    ints = functools.partial(pltpu.VMEM, dtype=jnp.int32)
+
+    def messages(layout, more):
+        axial = (layout.fields + more,) + face
+        return [(axial, VMEM), (axial, VMEM), ((layout.blocks, 8, wide), VMEM)]
+
+    post, factors, e, o, t, flags = call(
         first_kernel,
-        [pops, (fields,) + face, (fields,) + face, rows, cells],
-        [],
+        [HBM] * 5,
+        [(pops, VMEM), (pops, VMEM)] + messages(FIRST, 1) + [(cells, VMEM)],
+        [scratch(pops), scratch(pops), scratch(cells), ints(cells), ints(cells)]
+        + [pltpu.SemaphoreType.DMA((4 + cells[0],))],
         parity, initial, adjoint_seed, porosity, cell_type, region,
     )
-    near = exchange(e, o, t)
+    near, _ = exchange(FIRST, e, o, t)
     post, adj, sens_one, around, e, o, t = call(
         second_kernel,
-        [pops, pops, cells, (18,) + cells, (fields - 1,) + face, (fields - 1,) + face, rows],
-        [pops, pops],
-        parity, post, adjoint_seed, flags, porosity, cell_type, region, *near,
+        [],
+        [(pops, VMEM), (pops, VMEM), (cells, VMEM), ((18,) + cells, VMEM)] + messages(SECOND, 0),
+        [scratch(pops), scratch(pops), scratch((2, 16, wide))],
+        parity, post, adjoint_seed, factors, flags, porosity, cell_type, region, *near,
     )
-    near = exchange(e, o, t)
-    regions = lax.axis_size("ax") * lax.axis_size("az") // 4
-    lanes = -(-regions // 128) * 128
-    final, adjoint, sensitivity, partial = call(
+    near, totals = exchange(SECOND, e, o, t, SECOND.place[(LO, "sum")])
+    final, adjoint, sensitivity = call(
         third_kernel,
-        [pops, pops, cells, (1, lanes)],
-        [pops, (8, 128)],
+        [],
+        [(pops, HBM), (pops, HBM), (cells, VMEM)],
+        [scratch(pops), scratch(pops), scratch(pops), pltpu.SemaphoreType.DMA((2 * cells[0],))],
         parity, post, adj, flags, around, initial, porosity, cell_type, region, sens_one, *near,
     )
-    totals = sum_all(partial)[0, :regions]
-    return final, adjoint, sensitivity, totals
+    regions = lax.axis_size("ax") * lax.axis_size("az") // 4
+    return final, adjoint, sensitivity, totals[0, :regions]
 
 
 def solution(mesh):

time: 54.4 us -> 50.2 us (0.923)
  the two profiles are of different devices: /device:TPU:0 before, /device:TPU:3 now
where the time goes in v1:
time: 50.2 us; the launch traced here: 49.8 us
  starting transfers between devices  25.3 us (50%)
  waiting for transfers between devices  12.9 us (26%)
  Pallas kernels  5.78 us (12%)
  local copies, waits for them, and re-layouts  4.48 us (9%)
  between operations  0.79 us (2%)
  other arithmetic  0.53 us (1%)
    ppermute x2, starting transfers between devices, exchange(): oc = lax.ppermute(corners, 'ax', odd_pairs(size_a))  6.78 us
    ppermute x2, starting transfers between devices, exchange(): o = lax.ppermute(o_msg, 'ax', odd_pairs(size_a))  6.74 us
    pallas_call x3, Pallas kernels, call(): pl.pallas_call(body, out_shape=[jax.ShapeDtypeStruct(shape, jnp.float32)...  5.78 us
    ppermute x2, waiting for transfers between devices, exchange(): oc = lax.ppermute(corners, 'ax', odd_pairs(size_a))  4.59 us
    ppermute x3, starting transfers between devices, sum_over(): x = x + lax.ppermute(x, axis, [(i, i ^ step) for i in range(size)])  4.47 us
    unnamed x20, local copies, waits for them, and re-layouts  4.44 us
    ppermute x2, waiting for transfers between devices, exchange(): t = lax.ppermute(t_msg, 'az', ring)  4.09 us
    ppermute x2, starting transfers between devices, exchange(): e = lax.ppermute(e_msg, 'ax', even_pairs(size_a))  3.66 us
  transfers between devices with their start and end apart: 13, of which 7 were waited for; matrix products, arithmetic and copies ran while one was open for 1% of the time, Pallas kernels for 0%

profile of v1, /device:TPU:3, one launch (start us, length us, event | category | flops | bytes accessed | tf_op | source)
XLA Modules:
  0.0 49.8 jit_solution(3111808450409755472)
XLA Ops:
  0.6 0.0 copy-start
  0.7 1.1 %copy-done = f32[19,2,16,256]{3,2,1,0:T(8,128)S(1)} copy-done((f32[19,2,16,256]{3,2,1,0:T(8,128)S(1)}, f32[19,2,16,256]{3,2,1,0:T(8,128)}, u32[]{:S(2)}) %copy-start) | copy-done | bytes 622616
  1.7 0.0 copy-start.2
  1.7 1.1 %copy-done.2 = f32[19,2,16,256]{3,2,1,0:T(8,128)S(1)} copy-done((f32[19,2,16,256]{3,2,1,0:T(8,128)S(1)}, f32[19,2,16,256]{3,2,1,0:T(8,128)}, u32[]{:S(2)}) %copy-start.2) | copy-done | bytes 622616
  2.8 0.0 copy-start.4
  2.8 0.8 %copy-done.4 = f32[2,16,256]{2,1,0:T(8,128)S(1)} copy-done((f32[2,16,256]{2,1,0:T(8,128)S(1)}, f32[2,16,256]{2,1,0:T(8,128)}, u32[]{:S(2)}) %copy-start.4) | copy-done | bytes 32792
  3.6 0.0 copy-start.6
  3.6 0.8 %copy-done.6 = s32[2,16,256]{2,1,0:T(8,128)S(1)} copy-done((s32[2,16,256]{2,1,0:T(8,128)S(1)}, s32[2,16,256]{2,1,0:T(8,128)}, u32[]{:S(2)}) %copy-start.6) | copy-done | bytes 32792
  4.3 0.0 copy-start.8
  4.3 0.8 %copy-done.8 = s32[2,16,256]{2,1,0:T(8,128)S(1)} copy-done((s32[2,16,256]{2,1,0:T(8,128)S(1)}, s32[2,16,256]{2,1,0:T(8,128)}, u32[]{:S(2)}) %copy-start.8) | copy-done | bytes 32792
  5.1 0.0 copy-start.3
  5.1 1.4 %shard_map.84 = (f32[19,2,16,256]{3,2,1,0:T(8,128)S(1)}, f32[19,2,16,256]{3,2,1,0:T(8,128)S(1)}, f32[17,16,256]{2,1,0:T(8,128)S(1)}, f32[17,16,256]{2,1,0:T(8,12...) custom-call(s32[1]{0:T(128)} %bitcast.parity_ref, f32[19,2,16,256]{3,2,1,0:T(8,128)S(1)} %copy-done, ...), custom_call_target="tpu_custom_call" | custom-call | tf_op jit(solution)/shard_map/pallas_call | solution.py:454
  6.5 0.7 %collective-permute-start = (f32[17,16,256]{2,1,0:T(8,128)S(1)}, f32[17,16,256]{2,1,0:T(8,128)S(1)}, u32[]{:S(2)}, u32[]{:S(2)}) collective-permute-start(f32[17,16,256]{2,1,0:T(8,128)S(1)} %get-tuple-element.23), channel_id=1, source_target_pairs={{0,2},{2,0},{4,6},{6,4},{8,10},{10,8},{12,14},{14,12},{16,18},{18,... | collective-permute-start | bytes 835592 | tf_op jit(solution)/shard_map/ppermute | solution.py:483
  7.2 3.1 %collective-permute-start.1 = (f32[17,16,256]{2,1,0:T(8,128)S(1)}, f32[17,16,256]{2,1,0:T(8,128)S(1)}, u32[]{:S(2)}, u32[]{:S(2)}) collective-permute-start(f32[17,16,256]{2,1,0:T(8,128)S(1)} %get-tuple-element.24), channel_id=1, source_target_pairs={{2,4},{4,2},{6,8},{8,6},{10,12},{12,10},{14,16},{16,14},{18,20},{2... | collective-permute-start | bytes 835592 | tf_op jit(solution)/shard_map/ppermute | solution.py:484
  10.3 1.3 %collective-permute-start.2 = (f32[9,8,256]{2,1,0:T(8,128)S(1)}, f32[9,8,256]{2,1,0:T(8,128)S(1)}, u32[]{:S(2)}, u32[]{:S(2)}) collective-permute-start(f32[9,8,256]{2,1,0:T(8,128)S(1)} %get-tuple-element.25), channel_id=1, source_target_pairs={{0,1},{1,0},{2,3},{3,2},{4,5},{5,4},{6,7},{7,6},{8,9},{9,8},{10,11... | collective-permute-start | bytes 221192 | tf_op jit(solution)/shard_map/ppermute | solution.py:476
  11.6 2.5 %collective-permute-done.2.t = f32[9,8,256]{2,1,0:T(8,128)S(1)} collective-permute-done((f32[9,8,256]{2,1,0:T(8,128)S(1)}, f32[9,8,256]{2,1,0:T(8,128)S(1)}, u32[]{:S(2)}, u32[]{:S(2)}) %collective-permute-start.2) | collective-permute-done | bytes 73760 | tf_op jit(solution)/shard_map/ppermute | solution.py:476
  14.1 4.0 %collective-permute-start.4 = (f32[3,8,256]{2,1,0:T(8,128)S(1)}, f32[3,8,256]{2,1,0:T(8,128)S(1)}, u32[]{:S(2)}, u32[]{:S(2)}) collective-permute-start(f32[3,8,256]{2,1,0:T(8,128)S(1)} %slice.24), channel_id=1, source_target_pairs={{2,4},{4,2},{6,8},{8,6},{10,12},{12,10},{14,16},{16,14},{18,20},{2... | collective-permute-start | bytes 73736 | tf_op jit(solution)/shard_map/ppermute | solution.py:493
  18.1 0.1 collective-permute-start.3
  18.2 1.9 %collective-permute-done.4.oc = f32[3,8,256]{2,1,0:T(8,128)S(1)} collective-permute-done((f32[3,8,256]{2,1,0:T(8,128)S(1)}, f32[3,8,256]{2,1,0:T(8,128)S(1)}, u32[]{:S(2)}, u32[]{:S(2)}) %collective-permute-start.4) | collective-permute-done | bytes 24608 | tf_op jit(solution)/shard_map/ppermute | solution.py:493
  20.1 0.0 collective-permute-done.3.ec
  20.1 0.0 collective-permute-done.e
  20.1 0.0 collective-permute-done.1.o
  20.1 0.0 copy-done.3
  20.2 0.0 copy-start.1
  20.2 0.0 copy-start.7
  20.2 0.0 copy-start.9
  20.2 1.8 %shard_map.85 = (f32[19,2,16,256]{3,2,1,0:T(8,128)S(1)}, f32[19,2,16,256]{3,2,1,0:T(8,128)S(1)}, f32[2,16,256]{2,1,0:T(8,128)S(1)}, f32[18,2,16,256]{3,2,1,0:T(8...) custom-call(s32[1]{0:T(128)} %bitcast.parity_ref, ...), custom_call_target="tpu_custom_call" | custom-call | tf_op jit(solution)/shard_map/pallas_call | solution.py:454
  22.0 0.0 copy-start.5
  22.0 1.8 %collective-permute-start.7 = (f32[6,8,256]{2,1,0:T(8,128)S(1)}, f32[6,8,256]{2,1,0:T(8,128)S(1)}, u32[]{:S(2)}, u32[]{:S(2)}) collective-permute-start(f32[6,8,256]{2,1,0:T(8,128)S(1)} %get-tuple-element.32), channel_id=1, source_target_pairs={{0,1},{1,0},{2,3},{3,2},{4,5},{5,4},{6,7},{7,6},{8,9},{9,8},{10,11... | collective-permute-start | bytes 147464 | tf_op jit(solution)/shard_map/ppermute | solution.py:476
  23.8 1.6 %collective-permute-done.7.t = f32[6,8,256]{2,1,0:T(8,128)S(1)} collective-permute-done((f32[6,8,256]{2,1,0:T(8,128)S(1)}, f32[6,8,256]{2,1,0:T(8,128)S(1)}, u32[]{:S(2)}, u32[]{:S(2)}) %collective-permute-start.7) | collective-permute-done | bytes 49184 | tf_op jit(solution)/shard_map/ppermute | solution.py:476
  25.4 0.4 collective-permute-start.8
  25.9 0.8 %collective-permute-done.8.ec = f32[2,8,256]{2,1,0:T(8,128)S(1)} collective-permute-done((f32[2,8,256]{2,1,0:T(8,128)S(1)}, f32[2,8,256]{2,1,0:T(8,128)S(1)}, u32[]{:S(2)}, u32[]{:S(2)}) %collective-permute-start.8) | collective-permute-done | bytes 16416 | tf_op jit(solution)/shard_map/ppermute | solution.py:492
  26.7 0.0 collective-permute-start.10
  26.7 2.4 %collective-permute-done.10 = f32[1,256]{1,0:T(1,128)S(1)} collective-permute-done((f32[1,256]{1,0:T(1,128)S(1)}, f32[1,256]{1,0:T(1,128)S(1)}, u32[]{:S(2)}, u32[]{:S(2)}) %collective-permute-start.10) | collective-permute-done | bytes 1056 | tf_op jit(solution)/shard_map/ppermute | solution.py:507
  29.1 2.0 %collective-permute-start.11 = (f32[1,256]{1,0:T(1,128)S(1)}, f32[1,256]{1,0:T(1,128)S(1)}, u32[]{:S(2)}, u32[]{:S(2)}) collective-permute-start(f32[1,256]{1,0:T(1,128)S(1)} %add.45), channel_id=1, source_target_pairs={{0,8},{2,10},{4,12},{6,14},{8,0},{10,2},{12,4},{14,6},{16,24},{18,... | collective-permute-start | bytes 3080 | tf_op jit(solution)/shard_map/ppermute | solution.py:507
  31.1 1.0 %collective-permute-done.11 = f32[1,256]{1,0:T(1,128)S(1)} collective-permute-done((f32[1,256]{1,0:T(1,128)S(1)}, f32[1,256]{1,0:T(1,128)S(1)}, u32[]{:S(2)}, u32[]{:S(2)}) %collective-permute-start.11) | collective-permute-done | bytes 1056 | tf_op jit(solution)/shard_map/ppermute | solution.py:507
  32.1 2.5 %collective-permute-start.12 = (f32[1,256]{1,0:T(1,128)S(1)}, f32[1,256]{1,0:T(1,128)S(1)}, u32[]{:S(2)}, u32[]{:S(2)}) collective-permute-start(f32[1,256]{1,0:T(1,128)S(1)} %add.46), channel_id=1, source_target_pairs={{0,16},{2,18},{4,20},{6,22},{8,24},{10,26},{12,28},{14,30},{16,0},... | collective-permute-start | bytes 3080 | tf_op jit(solution)/shard_map/ppermute | solution.py:507
  34.6 2.9 %collective-permute-start.5 = (f32[10,16,256]{2,1,0:T(8,128)S(1)}, f32[10,16,256]{2,1,0:T(8,128)S(1)}, u32[]{:S(2)}, u32[]{:S(2)}) collective-permute-start(f32[10,16,256]{2,1,0:T(8,128)S(1)} %get-tuple-element.30), channel_id=1, source_target_pairs={{0,2},{2,0},{4,6},{6,4},{8,10},{10,8},{12,14},{14,12},{16,18},{18,... | collective-permute-start | bytes 491528 | tf_op jit(solution)/shard_map/ppermute | solution.py:483
  37.5 3.7 %collective-permute-start.6 = (f32[10,16,256]{2,1,0:T(8,128)S(1)}, f32[10,16,256]{2,1,0:T(8,128)S(1)}, u32[]{:S(2)}, u32[]{:S(2)}) collective-permute-start(f32[10,16,256]{2,1,0:T(8,128)S(1)} %get-tuple-element.31), channel_id=1, source_target_pairs={{2,4},{4,2},{6,8},{8,6},{10,12},{12,10},{14,16},{16,14},{18,20},{2... | collective-permute-start | bytes 491528 | tf_op jit(solution)/shard_map/ppermute | solution.py:484
  41.2 2.8 %collective-permute-start.9 = (f32[2,8,256]{2,1,0:T(8,128)S(1)}, f32[2,8,256]{2,1,0:T(8,128)S(1)}, u32[]{:S(2)}, u32[]{:S(2)}) collective-permute-start(f32[2,8,256]{2,1,0:T(8,128)S(1)} %dynamic_update_slice.3), channel_id=1, source_target_pairs={{2,4},{4,2},{6,8},{8,6},{10,12},{12,10},{14,16},{16,14},{18,20},{2... | collective-permute-start | bytes 49160 | tf_op jit(solution)/shard_map/ppermute | solution.py:493
  43.9 0.0 collective-permute-done.12
  44.0 0.5 %fusion.1 = f32[8]{0:T(128)} fusion(f32[1,256]{1,0:T(1,128)S(1)} %collective-permute-done.12, f32[1,256]{1,0:T(1,128)S(1)} %add.46), kind=kLoop, calls=%fused_computation.4 | loop fusion | flops 8 | bytes 96 | tf_op jit(solution)/shard_map/squeeze | solution.py:549
  44.5 2.6 %collective-permute-done.9.oc = f32[2,8,256]{2,1,0:T(8,128)S(1)} collective-permute-done((f32[2,8,256]{2,1,0:T(8,128)S(1)}, f32[2,8,256]{2,1,0:T(8,128)S(1)}, u32[]{:S(2)}, u32[]{:S(2)}) %collective-permute-start.9) | collective-permute-done | bytes 16416 | tf_op jit(solution)/shard_map/ppermute | solution.py:493
  47.1 0.0 collective-permute-done.5.e
  47.1 0.0 collective-permute-done.6.o
  47.1 0.0 copy-done.1
  47.1 0.0 copy-done.7
  47.1 0.0 copy-done.9
  47.1 0.0 copy-done.5
  47.2 2.6 %shard_map.86 = (f32[19,2,16,256]{3,2,1,0:T(8,128)}, f32[19,2,16,256]{3,2,1,0:T(8,128)}, f32[2,16,256]{2,1,0:T(8,128)}) custom-call(s32[1]{0:T(128)} %bitcast.parity_ref, f32[19,2,16,256]{3,2,1,0:T(8,128)S(1)} %get-tuple-element.26.post, f32[19,2,16,256]{3,2,1,0:T(8,128)S(1)} %get-tuple-element.27.adj, f32[2,16,256]{2,1,0:T(8,128)S(1)} %get-tuple-element.22.flags, ...), custom_call_target="tpu_custom_call" | custom-call | tf_op jit(solution)/shard_map/pallas_call | solution.py:454
  (7 shorter events, 0.0 us)
Async XLA Ops:
  0.6 1.1 %copy-start = (f32[19,2,16,256]{3,2,1,0:T(8,128)S(1)}, f32[19,2,16,256]{3,2,1,0:T(8,128)}, u32[]{:S(2)}) copy-start(f32[19,2,16,256]{3,2,1,0:T(8,128)} %pops.1) | copy-start | bytes 1867780
  1.7 1.1 %copy-start.2 = (f32[19,2,16,256]{3,2,1,0:T(8,128)S(1)}, f32[19,2,16,256]{3,2,1,0:T(8,128)}, u32[]{:S(2)}) copy-start(f32[19,2,16,256]{3,2,1,0:T(8,128)} %seed.1) | copy-start | bytes 1867780
  2.8 0.8 %copy-start.4 = (f32[2,16,256]{2,1,0:T(8,128)S(1)}, f32[2,16,256]{2,1,0:T(8,128)}, u32[]{:S(2)}) copy-start(f32[2,16,256]{2,1,0:T(8,128)} %porous.3) | copy-start | bytes 98308
  3.6 0.8 %copy-start.6 = (s32[2,16,256]{2,1,0:T(8,128)S(1)}, s32[2,16,256]{2,1,0:T(8,128)}, u32[]{:S(2)}) copy-start(s32[2,16,256]{2,1,0:T(8,128)} %types.3) | copy-start | bytes 98308
  4.3 0.8 %copy-start.8 = (s32[2,16,256]{2,1,0:T(8,128)S(1)}, s32[2,16,256]{2,1,0:T(8,128)}, u32[]{:S(2)}) copy-start(s32[2,16,256]{2,1,0:T(8,128)} %regions.3) | copy-start | bytes 98308
  5.1 15.1 %copy-start.3 = (f32[19,2,16,256]{3,2,1,0:T(8,128)S(1)}, f32[19,2,16,256]{3,2,1,0:T(8,128)}, u32[]{:S(2)}) copy-start(f32[19,2,16,256]{3,2,1,0:T(8,128)} %seed.1) | copy-start | bytes 1867780
  6.5 13.7 %collective-permute-start = (f32[17,16,256]{2,1,0:T(8,128)S(1)}, f32[17,16,256]{2,1,0:T(8,128)S(1)}, u32[]{:S(2)}, u32[]{:S(2)}) collective-permute-start(f32[17,16,256]{2,1,0:T(8,128)S(1)} %get-tuple-element.23), channel_id=1, source_target_pairs={{0,2},{2,0},{4,6},{6,4},{8,10},{10,8},{12,14},{14,12},{16,18},{18,... | collective-permute-start | bytes 835592 | tf_op jit(solution)/shard_map/ppermute | solution.py:483
  7.2 12.9 %collective-permute-start.1 = (f32[17,16,256]{2,1,0:T(8,128)S(1)}, f32[17,16,256]{2,1,0:T(8,128)S(1)}, u32[]{:S(2)}, u32[]{:S(2)}) collective-permute-start(f32[17,16,256]{2,1,0:T(8,128)S(1)} %get-tuple-element.24), channel_id=1, source_target_pairs={{2,4},{4,2},{6,8},{8,6},{10,12},{12,10},{14,16},{16,14},{18,20},{2... | collective-permute-start | bytes 835592 | tf_op jit(solution)/shard_map/ppermute | solution.py:484
  10.3 3.8 %collective-permute-start.2 = (f32[9,8,256]{2,1,0:T(8,128)S(1)}, f32[9,8,256]{2,1,0:T(8,128)S(1)}, u32[]{:S(2)}, u32[]{:S(2)}) collective-permute-start(f32[9,8,256]{2,1,0:T(8,128)S(1)} %get-tuple-element.25), channel_id=1, source_target_pairs={{0,1},{1,0},{2,3},{3,2},{4,5},{5,4},{6,7},{7,6},{8,9},{9,8},{10,11... | collective-permute-start | bytes 221192 | tf_op jit(solution)/shard_map/ppermute | solution.py:476
  14.1 6.0 %collective-permute-start.4 = (f32[3,8,256]{2,1,0:T(8,128)S(1)}, f32[3,8,256]{2,1,0:T(8,128)S(1)}, u32[]{:S(2)}, u32[]{:S(2)}) collective-permute-start(f32[3,8,256]{2,1,0:T(8,128)S(1)} %slice.24), channel_id=1, source_target_pairs={{2,4},{4,2},{6,8},{8,6},{10,12},{12,10},{14,16},{16,14},{18,20},{2... | collective-permute-start | bytes 73736 | tf_op jit(solution)/shard_map/ppermute | solution.py:493
  18.1 2.0 %collective-permute-start.3 = (f32[3,8,256]{2,1,0:T(8,128)S(1)}, f32[3,8,256]{2,1,0:T(8,128)S(1)}, u32[]{:S(2)}, u32[]{:S(2)}) collective-permute-start(f32[3,8,256]{2,1,0:T(8,128)S(1)} %slice.24), channel_id=1, source_target_pairs={{0,2},{2,0},{4,6},{6,4},{8,10},{10,8},{12,14},{14,12},{16,18},{18,... | collective-permute-start | bytes 73736 | tf_op jit(solution)/shard_map/ppermute | solution.py:492
  20.2 27.0 %copy-start.1 = (f32[19,2,16,256]{3,2,1,0:T(8,128)S(1)}, f32[19,2,16,256]{3,2,1,0:T(8,128)}, u32[]{:S(2)}) copy-start(f32[19,2,16,256]{3,2,1,0:T(8,128)} %pops.1) | copy-start | bytes 1867780
  20.2 27.0 %copy-start.7 = (s32[2,16,256]{2,1,0:T(8,128)S(1)}, s32[2,16,256]{2,1,0:T(8,128)}, u32[]{:S(2)}) copy-start(s32[2,16,256]{2,1,0:T(8,128)} %types.3) | copy-start | bytes 98308
  20.2 26.9 %copy-start.9 = (s32[2,16,256]{2,1,0:T(8,128)S(1)}, s32[2,16,256]{2,1,0:T(8,128)}, u32[]{:S(2)}) copy-start(s32[2,16,256]{2,1,0:T(8,128)} %regions.3) | copy-start | bytes 98308
  22.0 25.2 %copy-start.5 = (f32[2,16,256]{2,1,0:T(8,128)S(1)}, f32[2,16,256]{2,1,0:T(8,128)}, u32[]{:S(2)}) copy-start(f32[2,16,256]{2,1,0:T(8,128)} %porous.3) | copy-start | bytes 98308
  22.0 3.4 %collective-permute-start.7 = (f32[6,8,256]{2,1,0:T(8,128)S(1)}, f32[6,8,256]{2,1,0:T(8,128)S(1)}, u32[]{:S(2)}, u32[]{:S(2)}) collective-permute-start(f32[6,8,256]{2,1,0:T(8,128)S(1)} %get-tuple-element.32), channel_id=1, source_target_pairs={{0,1},{1,0},{2,3},{3,2},{4,5},{5,4},{6,7},{7,6},{8,9},{9,8},{10,11... | collective-permute-start | bytes 147464 | tf_op jit(solution)/shard_map/ppermute | solution.py:476
  25.4 1.3 %collective-permute-start.8 = (f32[2,8,256]{2,1,0:T(8,128)S(1)}, f32[2,8,256]{2,1,0:T(8,128)S(1)}, u32[]{:S(2)}, u32[]{:S(2)}) collective-permute-start(f32[2,8,256]{2,1,0:T(8,128)S(1)} %dynamic_update_slice.3), channel_id=1, source_target_pairs={{0,2},{2,0},{4,6},{6,4},{8,10},{10,8},{12,14},{14,12},{16,18},{18,... | collective-permute-start | bytes 49160 | tf_op jit(solution)/shard_map/ppermute | solution.py:492
  26.7 2.4 %collective-permute-start.10 = (f32[1,256]{1,0:T(1,128)S(1)}, f32[1,256]{1,0:T(1,128)S(1)}, u32[]{:S(2)}, u32[]{:S(2)}) collective-permute-start(f32[1,256]{1,0:T(1,128)S(1)} %fusion), channel_id=1, source_target_pairs={{0,4},{2,6},{4,0},{6,2},{8,12},{10,14},{12,8},{14,10},{16,20},{18,... | collective-permute-start | bytes 3080 | tf_op jit(solution)/shard_map/ppermute | solution.py:507
  29.1 2.9 %collective-permute-start.11 = (f32[1,256]{1,0:T(1,128)S(1)}, f32[1,256]{1,0:T(1,128)S(1)}, u32[]{:S(2)}, u32[]{:S(2)}) collective-permute-start(f32[1,256]{1,0:T(1,128)S(1)} %add.45), channel_id=1, source_target_pairs={{0,8},{2,10},{4,12},{6,14},{8,0},{10,2},{12,4},{14,6},{16,24},{18,... | collective-permute-start | bytes 3080 | tf_op jit(solution)/shard_map/ppermute | solution.py:507
  32.1 11.9 %collective-permute-start.12 = (f32[1,256]{1,0:T(1,128)S(1)}, f32[1,256]{1,0:T(1,128)S(1)}, u32[]{:S(2)}, u32[]{:S(2)}) collective-permute-start(f32[1,256]{1,0:T(1,128)S(1)} %add.46), channel_id=1, source_target_pairs={{0,16},{2,18},{4,20},{6,22},{8,24},{10,26},{12,28},{14,30},{16,0},... | collective-permute-start | bytes 3080 | tf_op jit(solution)/shard_map/ppermute | solution.py:507
  34.6 12.6 %collective-permute-start.5 = (f32[10,16,256]{2,1,0:T(8,128)S(1)}, f32[10,16,256]{2,1,0:T(8,128)S(1)}, u32[]{:S(2)}, u32[]{:S(2)}) collective-permute-start(f32[10,16,256]{2,1,0:T(8,128)S(1)} %get-tuple-element.30), channel_id=1, source_target_pairs={{0,2},{2,0},{4,6},{6,4},{8,10},{10,8},{12,14},{14,12},{16,18},{18,... | collective-permute-start | bytes 491528 | tf_op jit(solution)/shard_map/ppermute | solution.py:483
  37.5 9.6 %collective-permute-start.6 = (f32[10,16,256]{2,1,0:T(8,128)S(1)}, f32[10,16,256]{2,1,0:T(8,128)S(1)}, u32[]{:S(2)}, u32[]{:S(2)}) collective-permute-start(f32[10,16,256]{2,1,0:T(8,128)S(1)} %get-tuple-element.31), channel_id=1, source_target_pairs={{2,4},{4,2},{6,8},{8,6},{10,12},{12,10},{14,16},{16,14},{18,20},{2... | collective-permute-start | bytes 491528 | tf_op jit(solution)/shard_map/ppermute | solution.py:484
  41.2 6.0 %collective-permute-start.9 = (f32[2,8,256]{2,1,0:T(8,128)S(1)}, f32[2,8,256]{2,1,0:T(8,128)S(1)}, u32[]{:S(2)}, u32[]{:S(2)}) collective-permute-start(f32[2,8,256]{2,1,0:T(8,128)S(1)} %dynamic_update_slice.3), channel_id=1, source_target_pairs={{2,4},{4,2},{6,8},{8,6},{10,12},{12,10},{14,16},{16,14},{18,20},{2... | collective-permute-start | bytes 49160 | tf_op jit(solution)/shard_map/ppermute | solution.py:493

commit v2 on v1

--- a/solution.py
+++ b/solution.py
@@ -73,7 +73,7 @@
         self.place.update({key: (self.corner_blocks + i // 8, i % 8) for i, key in enumerate(rest)})
 
 
-FIRST = Layout((POST, ADJ, FACTOR, FLAG), [(LO, "label"), (HI, "label")])
+FIRST = Layout((POST, ADJ, FACTOR, FLAG), [(LO, "label"), (HI, "label"), (LO, "own")])
 SECOND = Layout((POST, ADJ), [(LO, "sum")])
 
 
@@ -203,7 +203,7 @@
 
 
 class Fields:
-    def __init__(self, layout, own, parity, e, o, t, ec, oc):
+    def __init__(self, layout, own, parity, e, o, t, ec=None, oc=None):
         self.layout, self.own = layout, own
         self.e, self.o, self.t, self.ec, self.oc = e, o, t, ec, oc
         self.up_e = parity == 0
@@ -218,19 +218,17 @@
         slot = self.layout.slot[LO][(kind, q)]
         return jnp.where(self.up_e, self.e[slot], self.o[slot])
 
-    def row_label(self, a):
-        slot = self.layout.fields
-        e, o = self.e[slot, 0:1, :], self.o[slot, 0:1, :]
-        return jnp.where(self.up_e, o, e) if a < 0 else jnp.where(self.up_e, e, o)
-
     def message(self, key, a):
         block, i = self.layout.place[key]
         rows = (block, slice(i, i + 1))
         if 0 <= a < self.rows_a:
             return self.t[rows]
-        if a < 0:
-            return jnp.where(self.up_e, self.oc[rows], self.ec[rows])
-        return jnp.where(self.up_e, self.ec[rows], self.oc[rows])
+        if self.ec is None:
+            rows = (self.layout.fields, slice(8 * block + i, 8 * block + i + 1))
+            e, o = self.e[rows], self.o[rows]
+        else:
+            e, o = self.ec[rows], self.oc[rows]
+        return jnp.where(self.up_e, o, e) if a < 0 else jnp.where(self.up_e, e, o)
 
     def edge(self, side, kind, q, a):
         row = self.rows_a - 1 if a < 0 else 0 if a >= self.rows_a else a
@@ -250,21 +248,25 @@
         return value
 
 
-def pack(layout, own, parity, e_ref, o_ref, t_ref):
-    rows_a, rows_t = own[POST].shape[1], own[POST].shape[2]
-    even = parity == 0
-
-    def cells(kind, q, a):
-        return own[FLAG].at[a] if kind == FLAG else own[kind].at[q, a]
-
+def cells(own, kind, q, a):
+    return own[FLAG].at[a] if kind == FLAG else own[kind].at[q, a]
+
+
+def pack_azimuthal(layout, own, t_ref):
+    rows_t = own[POST].shape[2]
     for key, (block, i) in layout.place.items():
         if len(key) == 4:
             side, kind, q, a = key
             t = 0 if side == LO else rows_t - 1
-            t_ref[block, i : i + 1, :] = cells(kind, q, a)[t : t + 1, :]
+            t_ref[block, i : i + 1, :] = cells(own, kind, q, a)[t : t + 1, :]
+
+
+def pack_axial(layout, own, parity, e_ref, o_ref):
+    rows_a = own[POST].shape[1]
+    even = parity == 0
     for slot in range(layout.fields):
-        low = cells(*layout.ax[LO][slot], 0)[...]
-        high = cells(*layout.ax[HI][slot], rows_a - 1)[...]
+        low = cells(own, *layout.ax[LO][slot], 0)[...]
+        high = cells(own, *layout.ax[HI][slot], rows_a - 1)[...]
         e_ref[slot] = jnp.where(even, high, low)
         o_ref[slot] = jnp.where(even, low, high)
 
@@ -308,48 +310,84 @@
     return result
 
 
-def first_kernel(
-    parity_ref, pops_hbm, seed_hbm, porous_hbm, types_hbm, regions_hbm,
-    post, factors, e_out, o_out, t_out, flags, pops, seed, porous, types, regions, sems,
+def edge_kernel(
+    pops_hbm, seed_hbm, porous_hbm, types_hbm, regions_hbm,
+    pops, seed, porous, types, regions, t_out, edge, edge_post, edge_factors, sems,
 ):
-    rows_a = porous.shape[0]
-    loads = [
-        pltpu.make_async_copy(source, target, sems.at[i])
-        for i, (source, target) in enumerate(
-            [(types_hbm, types), (regions_hbm, regions), (porous_hbm, porous)]
-            + [(pops_hbm.at[:, a], pops.at[:, a]) for a in range(rows_a)]
-            + [(seed_hbm, seed)]
-        )
-    ]
+    rows_a, rows_t, rows_r = porous.shape
+    pairs = [(types_hbm, types), (regions_hbm, regions), (porous_hbm, porous)]
+    pairs += [(pops_hbm, pops), (seed_hbm, seed)]
+    loads = [pltpu.make_async_copy(*pair, sems.at[i]) for i, pair in enumerate(pairs)]
     for copy in loads:
         copy.start()
     for copy in loads[:3]:
         copy.wait()
-    flags[...] = jnp.where(types[...] != 1, 1.0, 0.0)
-    label = label_of(regions, porous.shape[2])
-    for side in (LO, HI):
-        block, i = FIRST.place[(side, "label")]
+    label = label_of(regions, rows_r)
+    for key in ((LO, "label"), (HI, "label"), (LO, "own")):
+        block, i = FIRST.place[key]
         t_out[block, i : i + 1, :] = label
-    for out in (e_out, o_out):
-        out[FIRST.fields] = jnp.broadcast_to(label, out.shape[1:])
-
+    columns = [(a, t) for a in range(rows_a) for t in (0, rows_t - 1)]
+
+    def gather(source, target):
+        for i, (a, t) in enumerate(columns):
+            target[i : i + 1, :] = source[a, t : t + 1, :]
+
+    gather(porous, edge.at[19])
+    gather_types = jnp.concatenate([types[a, t : t + 1, :] for a, t in columns] * 2)
+    gather_regions = jnp.concatenate([regions[a, t : t + 1, :] for a, t in columns] * 2)
+    for i in range(len(columns), edge.shape[1]):
+        edge[:, i, :] = jnp.ones((edge.shape[0], rows_r), jnp.float32)
+    loads[3].wait()
+    for q in range(19):
+        gather(pops.at[q], edge.at[q])
+    values = [edge[q] for q in range(19)]
+    lin = linearise(values, edge[19], gather_types, gather_regions)
+    post = collide(values, lin)
+    factors = porosity_factors(lin)
+    for q in range(19):
+        edge_post[q] = post[q]
+        edge_factors[q] = factors[q]
+    edge[0] = jnp.where(gather_types != 1, 1.0, 0.0)
+    loads[4].wait()
+    for key, (block, i) in FIRST.place.items():
+        if len(key) == 4:
+            side, kind, q, a = key
+            t = 0 if side == LO else rows_t - 1
+            k = columns.index((a, t))
+            if kind == ADJ:
+                row = seed[q, a, t : t + 1, :]
+            elif kind == FLAG:
+                row = edge[0, k : k + 1, :]
+            else:
+                row = (edge_post if kind == POST else edge_factors)[q, k : k + 1, :]
+            t_out[block, i : i + 1, :] = row
+
+
+def first_kernel(
+    parity_ref, pops, seed, porous, types, regions, post, factors, e_out, o_out, flags
+):
     def body(where):
         values = load(pops, where)
         lin = linearise(values, porous[where], types[where], regions[where])
         store(post, where, collide(values, lin))
         store(factors, where, porosity_factors(lin))
 
-    for a in range(rows_a):
-        loads[3 + a].wait()
-        chunks([a], porous.shape, body)
-    loads[-1].wait()
+    chunks(range(porous.shape[0]), porous.shape, body)
+    flags[...] = jnp.where(types[...] != 1, 1.0, 0.0)
     own = {POST: post, ADJ: seed, FACTOR: factors, FLAG: flags}
-    pack(FIRST, own, parity_ref[0], e_out, o_out, t_out)
+    pack_axial(FIRST, own, parity_ref[0], e_out, o_out)
+
+
+def forward_kernel(t_near, t, corners):
+    for block in range(FIRST.corner_blocks):
+        corners[block] = t_near[block]
+    block, i = FIRST.place[(LO, "own")]
+    corners[block, i : i + 1, :] = t[block, i : i + 1, :]
 
 
 def second_kernel(
     parity_ref, post, seed, factors, flags, porous, types, regions, e, o, t, ec, oc,
-    post_next, adj, sens, around, e_out, o_out, t_out, state, back, parts,
+    post_next, adj, sens, around, e_out, o_out, t_out, partial, state, back, parts,
 ):
     own = {POST: post, ADJ: seed, FACTOR: factors, FLAG: flags}
     fields = Fields(FIRST, own, parity_ref[0], e, o, t, ec, oc)
@@ -375,7 +413,8 @@
         sens[where] = partial_sens
 
     chunks(range(rows_a), porous.shape, body)
-    pack(SECOND, {POST: post_next, ADJ: adj}, parity_ref[0], e_out, o_out, t_out)
+    pack_axial(SECOND, {POST: post_next, ADJ: adj}, parity_ref[0], e_out, o_out)
+    pack_azimuthal(SECOND, {POST: post_next, ADJ: adj}, t_out)
     sums = {(i, st): [] for i in (-1, 0, 1) for st in (-1, 0, 1)}
     for a in range(rows_a):
         sums[(0, 0)] += [sens[a], factors[0, a] * adj[0, a]]
@@ -392,8 +431,8 @@
     for beyond in (-1, 0, 1):
         low, centre, high = (functools.reduce(jnp.add, sums[(beyond, st)]) for st in (-1, 0, 1))
         inner = centre + jnp.where(at_t == 0, 0.0, low) + jnp.where(at_t == rows_t - 1, 0.0, high)
-        label = label_of(regions, rows_r) if beyond == 0 else fields.row_label(beyond)
         a = {-1: -1, 0: 0, 1: rows_a}[beyond]
+        label = fields.message((LO, "own"), a) if beyond else label_of(regions, rows_r)
         rows.append((jnp.sum(inner, axis=0, keepdims=True), label))
         rows.append((high[rows_t - 1 : rows_t], fields.message((LO, "label"), a)))
         rows.append((low[0:1], fields.message((HI, "label"), a)))
@@ -404,15 +443,22 @@
     lanes = lax.broadcasted_iota(jnp.int32, parts.shape[1:], 1) + 1
     total = jnp.sum(parts[0], axis=1, keepdims=True)
     chosen = jnp.where(lanes == parts[1].astype(jnp.int32), total, 0.0)
-    block, i = SECOND.place[(LO, "sum")]
-    t_out[block, i : i + 1, :] = jnp.sum(chosen, axis=0, keepdims=True)
+    partial[...] = jnp.sum(chosen, axis=0, keepdims=True)
+
+
+def corner_kernel(e, o, t, total, e_out, o_out):
+    slot, (row, i) = SECOND.fields, SECOND.place[(LO, "sum")]
+    for out in (e_out, o_out):
+        for block in range(SECOND.corner_blocks):
+            out[slot, 8 * block : 8 * block + 8, :] = t[block]
+        out[slot, 8 * row + i : 8 * row + i + 1, :] = total[...]
 
 
 def third_kernel(
-    parity_ref, post, adj, flags, around, pops, porous, types, regions, sens_one, e, o, t, ec, oc,
+    parity_ref, post, adj, flags, around, pops, porous, types, regions, sens_one, e, o, t,
     final_hbm, result_hbm, sens, final, result, back, sems,
 ):
-    fields = Fields(SECOND, {POST: post, ADJ: adj}, parity_ref[0], e, o, t, ec, oc)
+    fields = Fields(SECOND, {POST: post, ADJ: adj}, parity_ref[0], e, o, t)
     rows_a = porous.shape[0]
     stores = []
     for a in range(rows_a):
@@ -449,17 +495,17 @@
 VMEM, HBM = pltpu.VMEM, pltpu.HBM
 
 
-def call(body, in_spaces, outs, scratch, parity, *arrays):
-    spaces = in_spaces + [VMEM] * (len(arrays) - len(in_spaces))
+def call(body, in_spaces, outs, scratch, *arrays, aliases=None, cost=None):
     return pl.pallas_call(
         body,
-        out_shape=[jax.ShapeDtypeStruct(shape, jnp.float32) for shape, _ in outs],
-        in_specs=[pl.BlockSpec(memory_space=pltpu.SMEM)]
-        + [pl.BlockSpec(memory_space=space) for space in spaces],
-        out_specs=[pl.BlockSpec(memory_space=space) for _, space in outs],
+        out_shape=[jax.ShapeDtypeStruct(shape, dtype) for shape, dtype, _ in outs],
+        in_specs=[pl.BlockSpec(memory_space=space) for space in in_spaces],
+        out_specs=[pl.BlockSpec(memory_space=space) for _, _, space in outs],
         scratch_shapes=scratch,
-        compiler_params=pltpu.CompilerParams(vmem_limit_bytes=40 * 1024 * 1024),
-    )(parity, *arrays)
+        input_output_aliases=aliases or {},
+        cost_estimate=cost,
+        compiler_params=pltpu.CompilerParams(vmem_limit_bytes=16 * 1024 * 1024),
+    )(*arrays)
 
 
 def even_pairs(size):
@@ -470,83 +516,113 @@
     return [(i, ((i + 1) ^ 1) - 1) for i in range(size) if 0 <= ((i + 1) ^ 1) - 1 < size]
 
 
-def exchange(layout, e_msg, o_msg, t_msg, totals_row=None):
-    size_a, size_t = lax.axis_size("ax"), lax.axis_size("az")
-    ring = [(i, (i + 1) % size_t) for i in range(size_t)]
-    t = lax.ppermute(t_msg, "az", ring)
-    if size_t > 2:
+def send_azimuthal(layout, message):
+    size = lax.axis_size("az")
+    ring = [(i, (i + 1) % size) for i in range(size)]
+    t = lax.ppermute(message, "az", ring)
+    if size > 2:
         from_high = np.zeros((layout.blocks, 8, 1), bool)
         for key, (block, i) in layout.place.items():
             from_high[block, i] = key[0] == HI
-        t_down = lax.ppermute(t_msg, "az", [(j, i) for i, j in ring])
+        t_down = lax.ppermute(message, "az", [(j, i) for i, j in ring])
         t = jnp.where(jnp.asarray(from_high), t, t_down)
-    e = lax.ppermute(e_msg, "ax", even_pairs(size_a))
-    o = lax.ppermute(o_msg, "ax", odd_pairs(size_a))
-    corners = t[: layout.corner_blocks]
-    total = None
-    if totals_row is not None:
-        block, i = totals_row
-        total = t_msg[block, i : i + 1]
-        total = total + t[block, i : i + 1] if size_t == 2 else sum_over(total, "az", 1)
-        corners = lax.dynamic_update_slice(corners, total[None], (block, i, 0))
-    ec = lax.ppermute(corners, "ax", even_pairs(size_a))
-    oc = lax.ppermute(corners, "ax", odd_pairs(size_a))
-    if totals_row is not None:
-        if size_a & (size_a - 1):
-            total = lax.psum(total, "ax")
-        elif size_a > 1:
-            total = sum_over(total + ec[block, i : i + 1], "ax", 2)
-    return (e, o, t, ec, oc), total
-
-
-def sum_over(x, axis, step):
+    return t
+
+
+def send_axial(e_message, o_message):
+    size = lax.axis_size("ax")
+    e = lax.ppermute(e_message, "ax", even_pairs(size))
+    return e, lax.ppermute(o_message, "ax", odd_pairs(size))
+
+
+def sum_over(x, axis, step, last_after=None):
     size = lax.axis_size(axis)
     if size & (size - 1):
         return lax.psum(x, axis)
     while step < size:
+        if last_after is not None and 2 * step == size:
+            x, _ = lax.optimization_barrier((x, last_after))
         x = x + lax.ppermute(x, axis, [(i, i ^ step) for i in range(size)])
         step *= 2
     return x
 
 
 def shards(initial, adjoint_seed, porosity, cell_type, region):
-    cells = porosity.shape
-    pops = (19,) + cells
-    face, wide = cells[1:], cells[2]
-    parity = (lax.axis_index("ax") % 2).astype(jnp.int32).reshape(1)
-    scratch = functools.partial(pltpu.VMEM, dtype=jnp.float32)
-    ints = functools.partial(pltpu.VMEM, dtype=jnp.int32)
-
-    def messages(layout, more):
-        axial = (layout.fields + more,) + face
-        return [(axial, VMEM), (axial, VMEM), ((layout.blocks, 8, wide), VMEM)]
-
-    post, factors, e, o, t, flags = call(
+    cells_ = porosity.shape
+    pops = (19,) + cells_
+    wide = cells_[2]
+    f32, i32 = jnp.float32, jnp.int32
+    size_a, size_t = lax.axis_size("ax"), lax.axis_size("az")
+    parity = (lax.axis_index("ax") % 2).astype(i32).reshape(1)
+
+    def axial(fields):
+        return [((fields,) + cells_[1:], f32, VMEM)] * 2
+
+    inputs = (initial, adjoint_seed, porosity, cell_type, region)
+    *near_inputs, t = call(
+        edge_kernel,
+        [HBM] * 5,
+        [(x.shape, x.dtype, VMEM) for x in inputs] + [((FIRST.blocks, 8, wide), f32, VMEM)],
+        [VMEM((20, 8, wide), f32), VMEM((19, 8, wide), f32), VMEM((19, 8, wide), f32)]
+        + [pltpu.SemaphoreType.DMA((5,))],
+        *(pltpu.with_memory_space_constraint(x, HBM) for x in inputs),
+    )
+    post, factors, e, o, flags = call(
         first_kernel,
-        [HBM] * 5,
-        [(pops, VMEM), (pops, VMEM)] + messages(FIRST, 1) + [(cells, VMEM)],
-        [scratch(pops), scratch(pops), scratch(cells), ints(cells), ints(cells)]
-        + [pltpu.SemaphoreType.DMA((4 + cells[0],))],
-        parity, initial, adjoint_seed, porosity, cell_type, region,
+        [pltpu.SMEM] + [VMEM] * 5,
+        [(pops, f32, VMEM), (pops, f32, VMEM)] + axial(FIRST.fields) + [(cells_, f32, VMEM)],
+        [],
+        parity, *near_inputs,
     )
-    near, _ = exchange(FIRST, e, o, t)
-    post, adj, sens_one, around, e, o, t = call(
+    t_near = send_azimuthal(FIRST, t)
+    e, o = send_axial(e, o)
+    corners = call(
+        forward_kernel,
+        [VMEM] * 2,
+        [((FIRST.corner_blocks, 8, wide), f32, VMEM)],
+        [],
+        t_near, t,
+        cost=pl.CostEstimate(flops=1 << 30, bytes_accessed=40 << 20, transcendentals=0),
+    )[0]
+    ec, oc = send_axial(corners, corners)
+    post, adj, sens_one, around, e, o, t, total = call(
         second_kernel,
+        [pltpu.SMEM] + [VMEM] * 12,
+        [(pops, f32, VMEM), (pops, f32, VMEM), (cells_, f32, VMEM), ((18,) + cells_, f32, VMEM)]
+        + axial(SECOND.fields + 1)
+        + [((SECOND.blocks, 8, wide), f32, VMEM), ((1, wide), f32, VMEM)],
+        [VMEM(pops, f32), VMEM(pops, f32), VMEM((2, 16, wide), f32)],
+        parity, post, adjoint_seed, factors, flags, porosity, cell_type, region, e, o, t_near, ec, oc,
+    )
+    t_near = send_azimuthal(SECOND, t)
+    halving = size_a % 4 == 0 and size_a & (size_a - 1) == 0
+    if halving:
+        total = total + lax.ppermute(total, "ax", [(i, i ^ 2) for i in range(size_a)])
+    e, o = call(
+        corner_kernel,
+        [VMEM] * 4,
+        axial(SECOND.fields + 1),
         [],
-        [(pops, VMEM), (pops, VMEM), (cells, VMEM), ((18,) + cells, VMEM)] + messages(SECOND, 0),
-        [scratch(pops), scratch(pops), scratch((2, 16, wide))],
-        parity, post, adjoint_seed, factors, flags, porosity, cell_type, region, *near,
+        e, o, t_near, total,
+        aliases={0: 0, 1: 1},
     )
-    near, totals = exchange(SECOND, e, o, t, SECOND.place[(LO, "sum")])
+    e, o = send_axial(e, o)
+    if halving:
+        block, i = SECOND.place[(LO, "sum")]
+        total = total + e[SECOND.fields, 8 * block + i : 8 * block + i + 1]
+        total = sum_over(total, "az", 1)
+        totals = sum_over(total, "ax", 4, o)
+    else:
+        totals = lax.psum(total, ("ax", "az"))
     final, adjoint, sensitivity = call(
         third_kernel,
-        [],
-        [(pops, HBM), (pops, HBM), (cells, VMEM)],
-        [scratch(pops), scratch(pops), scratch(pops), pltpu.SemaphoreType.DMA((2 * cells[0],))],
-        parity, post, adj, flags, around, initial, porosity, cell_type, region, sens_one, *near,
+        [pltpu.SMEM] + [VMEM] * 12,
+        [(pops, f32, HBM), (pops, f32, HBM), (cells_, f32, VMEM)],
+        [VMEM(pops, f32), VMEM(pops, f32), VMEM(pops, f32)]
+        + [pltpu.SemaphoreType.DMA((2 * cells_[0],))],
+        parity, post, adj, flags, around, initial, porosity, cell_type, region, sens_one, e, o, t_near,
     )
-    regions = lax.axis_size("ax") * lax.axis_size("az") // 4
-    return final, adjoint, sensitivity, totals[0, :regions]
+    return final, adjoint, sensitivity, totals[0, : size_a * size_t // 4]
 
 
 def solution(mesh):

time: 50.2 us -> 40.8 us (0.81)
  the two profiles are of different devices: /device:TPU:3 before, /device:TPU:0 now
where the time goes in v2:
time: 40.8 us; the launch traced here: 40.6 us
  starting transfers between devices  22.7 us (56%)
  waiting for transfers between devices  10.1 us (25%)
  Pallas kernels  6.57 us (16%)
  between operations  0.78 us (2%)
  other arithmetic  0.53 us (1%)
    ppermute x3, starting transfers between devices, sum_over(): x = x + lax.ppermute(x, axis, [(i, i ^ step) for i in range(size)])  7.61 us
    pallas_call x6, Pallas kernels, call(): pl.pallas_call(body, out_shape=[jax.ShapeDtypeStruct(shape, dtype) for sh...  6.57 us
    ppermute x3, starting transfers between devices, send_axial(): e = lax.ppermute(e_message, 'ax', even_pairs(size))  5.75 us
    ppermute x2, starting transfers between devices, send_azimuthal(): t = lax.ppermute(message, 'az', ring)  5.1 us
    ppermute x3, waiting for transfers between devices, sum_over(): x = x + lax.ppermute(x, axis, [(i, i ^ step) for i in range(size)])  4.71 us
    ppermute x2, waiting for transfers between devices, send_azimuthal(): t = lax.ppermute(message, 'az', ring)  2.34 us
    ppermute x1, starting transfers between devices, shards(): lax.ppermute(total, 'ax', [(i, i ^ 2) for i in range(size_a)])  2.21 us
    ppermute x3, starting transfers between devices, send_axial(): return (e, lax.ppermute(o_message, 'ax', odd_pairs(size)))  1.98 us
  transfers between devices with their start and end apart: 12, of which 6 were waited for; matrix products, arithmetic and copies ran while one was open for 0% of the time, Pallas kernels for 6%

profile of v2, /device:TPU:0, one launch (start us, length us, event | category | flops | bytes accessed | tf_op | source)
XLA Modules:
  0.0 40.6 jit_solution(7065600203608640821)
XLA Ops:
  0.6 1.4 %shard_map.84 = (f32[19,2,16,256]{3,2,1,0:T(8,128)S(1)}, f32[19,2,16,256]{3,2,1,0:T(8,128)S(1)}, f32[2,16,256]{2,1,0:T(8,128)S(1)}, s32[2,16,256]{2,1,0:T(8,128)...) custom-call(f32[19,2,16,256]{3,2,1,0:T(8,128)} %pops.1, f32[19,2,16,256]{3,2,1,0:T(8,128)} %seed.1, ...), custom_call_target="tpu_custom_call" | custom-call | tf_op jit(solution)/shard_map/pallas_call | solution.py:499
  2.1 0.8 %shard_map.85 = (f32[19,2,16,256]{3,2,1,0:T(8,128)S(1)}, f32[19,2,16,256]{3,2,1,0:T(8,128)S(1)}, f32[16,16,256]{2,1,0:T(8,128)S(1)}, f32[16,16,256]{2,1,0:T(8,128)S(1)}, f32[2,16,256]{2,1,0:T(8,128)S(1)}) custom-call(s32[1]{0:T(128)} %bitcast.parity_ref, f32[19,2,16,256]{3,2,1,0:T(8,128)S(1)} %get-tuple-element.29.pops, ...), custom_call_target="tpu_custom_call" | custom-call | tf_op jit(solution)/shard_map/pallas_call | solution.py:499
  2.9 0.5 %collective-permute-start = (f32[16,16,256]{2,1,0:T(8,128)S(1)}, f32[16,16,256]{2,1,0:T(8,128)S(1)}, u32[]{:S(2)}, u32[]{:S(2)}) collective-permute-start(f32[16,16,256]{2,1,0:T(8,128)S(1)} %get-tuple-element.37), channel_id=1, source_target_pairs={{0,2},{2,0},{4,6},{6,4},{8,10},{10,8},{12,14},{14,12},{16,18},{18,... | collective-permute-start | bytes 786440 | tf_op jit(solution)/shard_map/ppermute | solution.py:534
  3.4 0.7 %collective-permute-start.1 = (f32[16,16,256]{2,1,0:T(8,128)S(1)}, f32[16,16,256]{2,1,0:T(8,128)S(1)}, u32[]{:S(2)}, u32[]{:S(2)}) collective-permute-start(f32[16,16,256]{2,1,0:T(8,128)S(1)} %get-tuple-element.38), channel_id=1, source_target_pairs={{2,4},{4,2},{6,8},{8,6},{10,12},{12,10},{14,16},{16,14},{18,20},{2... | collective-permute-start | bytes 786440 | tf_op jit(solution)/shard_map/ppermute | solution.py:535
  4.1 0.0 copy-start.1
  4.1 0.0 copy-start.2
  4.1 0.0 copy-start.3
  4.1 0.0 copy-start.4
  4.1 2.6 %collective-permute-start.2 = (f32[9,8,256]{2,1,0:T(8,128)S(1)}, f32[9,8,256]{2,1,0:T(8,128)S(1)}, u32[]{:S(2)}, u32[]{:S(2)}) collective-permute-start(f32[9,8,256]{2,1,0:T(8,128)S(1)} %get-tuple-element.39.t), channel_id=1, source_target_pairs={{0,1},{1,0},{2,3},{3,2},{4,5},{5,4},{6,7},{7,6},{8,9},{9,8},{10,11... | collective-permute-start | bytes 221192 | tf_op jit(solution)/shard_map/ppermute | solution.py:522
  6.7 2.3 %collective-permute-done.2.t_near.t = f32[9,8,256]{2,1,0:T(8,128)S(1)} collective-permute-done((f32[9,8,256]{2,1,0:T(8,128)S(1)}, f32[9,8,256]{2,1,0:T(8,128)S(1)}, u32[]{:S(2)}, u32[]{:S(2)}) %collective-permute-start.2) | collective-permute-done | bytes 73760 | tf_op jit(solution)/shard_map/ppermute | solution.py:522
  9.1 0.7 %collective-permute-start.4 = (f32[3,8,256]{2,1,0:T(8,128)S(1)}, f32[3,8,256]{2,1,0:T(8,128)S(1)}, u32[]{:S(2)}, u32[]{:S(2)}) collective-permute-start(f32[3,8,256]{2,1,0:T(8,128)S(1)} %shard_map.86), channel_id=1, source_target_pairs={{2,4},{4,2},{6,8},{8,6},{10,12},{12,10},{14,16},{16,14},{18,20},{2... | collective-permute-start | bytes 73736 | tf_op jit(solution)/shard_map/ppermute | solution.py:535
  9.7 5.1 %collective-permute-start.3 = (f32[3,8,256]{2,1,0:T(8,128)S(1)}, f32[3,8,256]{2,1,0:T(8,128)S(1)}, u32[]{:S(2)}, u32[]{:S(2)}) collective-permute-start(f32[3,8,256]{2,1,0:T(8,128)S(1)} %shard_map.86), channel_id=1, source_target_pairs={{0,2},{2,0},{4,6},{6,4},{8,10},{10,8},{12,14},{14,12},{16,18},{18,... | collective-permute-start | bytes 73736 | tf_op jit(solution)/shard_map/ppermute | solution.py:534
  14.8 0.0 collective-permute-done.4.oc
  14.8 0.8 %collective-permute-done.3.ec = f32[3,8,256]{2,1,0:T(8,128)S(1)} collective-permute-done((f32[3,8,256]{2,1,0:T(8,128)S(1)}, f32[3,8,256]{2,1,0:T(8,128)S(1)}, u32[]{:S(2)}, u32[]{:S(2)}) %collective-permute-start.3) | collective-permute-done | bytes 24608 | tf_op jit(solution)/shard_map/ppermute | solution.py:534
  15.6 0.0 collective-permute-done.e
  15.6 0.0 collective-permute-done.1.o
  15.6 0.0 copy-done.1
  15.6 0.0 copy-done.2
  15.6 0.0 copy-done.3
  15.7 0.0 copy-done.4
  15.7 0.0 copy-start
  15.7 1.7 %shard_map.87 = (f32[19,2,16,256]{3,2,1,0:T(8,128)S(1)}, f32[19,2,16,256]{3,2,1,0:T(8,128)S(1)}, f32[2,16,256]{2,1,0:T(8,128)S(1)}, f32[18,2,16,256]{3,2,1,0:T(8...) custom-call(s32[1]{0:T(128)} %bitcast.parity_ref, ...), custom_call_target="tpu_custom_call" | custom-call | tf_op jit(solution)/shard_map/pallas_call | solution.py:499
  17.4 2.5 %collective-permute-start.5 = (f32[6,8,256]{2,1,0:T(8,128)S(1)}, f32[6,8,256]{2,1,0:T(8,128)S(1)}, u32[]{:S(2)}, u32[]{:S(2)}) collective-permute-start(f32[6,8,256]{2,1,0:T(8,128)S(1)} %get-tuple-element.46), channel_id=1, source_target_pairs={{0,1},{1,0},{2,3},{3,2},{4,5},{5,4},{6,7},{7,6},{8,9},{9,8},{10,11... | collective-permute-start | bytes 147464 | tf_op jit(solution)/shard_map/ppermute | solution.py:522
  19.9 2.2 %collective-permute-start.6 = (f32[1,256]{1,0:T(1,128)S(1)}, f32[1,256]{1,0:T(1,128)S(1)}, u32[]{:S(2)}, u32[]{:S(2)}) collective-permute-start(f32[1,256]{1,0:T(1,128)S(1)} %get-tuple-element.47), channel_id=1, source_target_pairs={{0,4},{2,6},{4,0},{6,2},{8,12},{10,14},{12,8},{14,10},{16,20},{18,... | collective-permute-start | bytes 3080 | tf_op jit(solution)/shard_map/ppermute | solution.py:600
  22.1 1.5 %collective-permute-done.6 = f32[1,256]{1,0:T(1,128)S(1)} collective-permute-done((f32[1,256]{1,0:T(1,128)S(1)}, f32[1,256]{1,0:T(1,128)S(1)}, u32[]{:S(2)}, u32[]{:S(2)}) %collective-permute-start.6) | collective-permute-done | bytes 1056 | tf_op jit(solution)/shard_map/ppermute | solution.py:600
  23.7 0.0 collective-permute-done.5.t
  23.7 0.2 collective-permute-start.7
  23.9 0.7 %collective-permute-start.8 = (f32[11,16,256]{2,1,0:T(8,128)S(1)}, f32[11,16,256]{2,1,0:T(8,128)S(1)}, u32[]{:S(2)}, u32[]{:S(2)}) collective-permute-start(f32[11,16,256]{2,1,0:T(8,128)S(1)} %get-tuple-element.49), channel_id=1, source_target_pairs={{2,4},{4,2},{6,8},{8,6},{10,12},{12,10},{14,16},{16,14},{18,20},{2... | collective-permute-start | bytes 540680 | tf_op jit(solution)/shard_map/ppermute | solution.py:535
  24.5 0.6 %collective-permute-done.7.e = f32[11,16,256]{2,1,0:T(8,128)S(1)} collective-permute-done((f32[11,16,256]{2,1,0:T(8,128)S(1)}, f32[11,16,256]{2,1,0:T(8,128)S(1)}, u32[]{:S(2)}, u32[]{:S(2)}) %collective-permute-start.7) | collective-permute-done | bytes 180256 | tf_op jit(solution)/shard_map/ppermute | solution.py:534
  25.2 0.4 %collective-permute-start.9 = (f32[1,256]{1,0:T(1,128)S(1)}, f32[1,256]{1,0:T(1,128)S(1)}, u32[]{:S(2)}, u32[]{:S(2)}) collective-permute-start(f32[1,256]{1,0:T(1,128)S(1)} %fusion), channel_id=1, source_target_pairs={{0,1},{1,0},{2,3},{3,2},{4,5},{5,4},{6,7},{7,6},{8,9},{9,8},{10,11... | collective-permute-start | bytes 3080 | tf_op jit(solution)/shard_map/ppermute | solution.py:545
  25.6 3.2 %collective-permute-done.9 = f32[1,256]{1,0:T(1,128)S(1)} collective-permute-done((f32[1,256]{1,0:T(1,128)S(1)}, f32[1,256]{1,0:T(1,128)S(1)}, u32[]{:S(2)}, u32[]{:S(2)}) %collective-permute-start.9) | collective-permute-done | bytes 1056 | tf_op jit(solution)/shard_map/ppermute | solution.py:545
  28.7 4.2 %collective-permute-start.10 = (f32[1,256]{1,0:T(1,128)S(1)}, f32[1,256]{1,0:T(1,128)S(1)}, u32[]{:S(2)}, u32[]{:S(2)}) collective-permute-start(f32[1,256]{1,0:T(1,128)S(1)} %add.22), channel_id=1, source_target_pairs={{0,8},{2,10},{4,12},{6,14},{8,0},{10,2},{12,4},{14,6},{16,24},{18,... | collective-permute-start | bytes 3080 | tf_op jit(solution)/shard_map/ppermute | solution.py:545
  32.9 1.5 %collective-permute-done.10 = f32[1,256]{1,0:T(1,128)S(1)} collective-permute-done((f32[1,256]{1,0:T(1,128)S(1)}, f32[1,256]{1,0:T(1,128)S(1)}, u32[]{:S(2)}, u32[]{:S(2)}) %collective-permute-start.10) | collective-permute-done | bytes 1056 | tf_op jit(solution)/shard_map/ppermute | solution.py:545
  34.5 0.0 collective-permute-done.8.o
  34.5 3.0 %collective-permute-start.11 = (f32[1,256]{1,0:T(1,128)S(1)}, f32[1,256]{1,0:T(1,128)S(1)}, u32[]{:S(2)}, u32[]{:S(2)}) collective-permute-start(f32[1,256]{1,0:T(1,128)S(1)} %add.23), channel_id=1, source_target_pairs={{0,16},{2,18},{4,20},{6,22},{8,24},{10,26},{12,28},{14,30},{16,0},... | collective-permute-start | bytes 3080 | tf_op jit(solution)/shard_map/ppermute | solution.py:545
  37.5 0.0 copy-done
  37.5 2.6 %shard_map.89 = (f32[19,2,16,256]{3,2,1,0:T(8,128)}, f32[19,2,16,256]{3,2,1,0:T(8,128)}, f32[2,16,256]{2,1,0:T(8,128)}) custom-call(s32[1]{0:T(128)} %bitcast.parity_ref, f32[19,2,16,256]{3,2,1,0:T(8,128)S(1)} %get-tuple-element.40.post, f32[19,2,16,256]{3,2,1,0:T(8,128)S(1)} %get-tuple-element.41.adj, f32[2,16,256]{2,1,0:T(8,128)S(1)} %get-tuple-element.36.flags, ...), custom_call_target="tpu_custom_call" | custom-call | tf_op jit(solution)/shard_map/pallas_call | solution.py:499
  40.1 0.0 collective-permute-done.11
  40.1 0.5 %fusion.1 = f32[8]{0:T(128)} fusion(f32[1,256]{1,0:T(1,128)S(1)} %collective-permute-done.11, f32[1,256]{1,0:T(1,128)S(1)} %add.23), kind=kLoop, calls=%fused_computation.3 | loop fusion | flops 8 | bytes 96 | tf_op jit(solution)/shard_map/squeeze | solution.py:625
  (6 shorter events, 0.0 us)
Async XLA Ops:
  2.9 12.7 %collective-permute-start = (f32[16,16,256]{2,1,0:T(8,128)S(1)}, f32[16,16,256]{2,1,0:T(8,128)S(1)}, u32[]{:S(2)}, u32[]{:S(2)}) collective-permute-start(f32[16,16,256]{2,1,0:T(8,128)S(1)} %get-tuple-element.37), channel_id=1, source_target_pairs={{0,2},{2,0},{4,6},{6,4},{8,10},{10,8},{12,14},{14,12},{16,18},{18,... | collective-permute-start | bytes 786440 | tf_op jit(solution)/shard_map/ppermute | solution.py:534
  3.4 12.2 %collective-permute-start.1 = (f32[16,16,256]{2,1,0:T(8,128)S(1)}, f32[16,16,256]{2,1,0:T(8,128)S(1)}, u32[]{:S(2)}, u32[]{:S(2)}) collective-permute-start(f32[16,16,256]{2,1,0:T(8,128)S(1)} %get-tuple-element.38), channel_id=1, source_target_pairs={{2,4},{4,2},{6,8},{8,6},{10,12},{12,10},{14,16},{16,14},{18,20},{2... | collective-permute-start | bytes 786440 | tf_op jit(solution)/shard_map/ppermute | solution.py:535
  4.1 11.6 %copy-start.1 = (f32[19,2,16,256]{3,2,1,0:T(8,128)S(1)}, f32[19,2,16,256]{3,2,1,0:T(8,128)}, u32[]{:S(2)}) copy-start(f32[19,2,16,256]{3,2,1,0:T(8,128)} %seed.1) | copy-start | bytes 1867780
  4.1 11.6 %copy-start.2 = (f32[2,16,256]{2,1,0:T(8,128)S(1)}, f32[2,16,256]{2,1,0:T(8,128)}, u32[]{:S(2)}) copy-start(f32[2,16,256]{2,1,0:T(8,128)} %porous.3) | copy-start | bytes 98308
  4.1 11.6 %copy-start.3 = (s32[2,16,256]{2,1,0:T(8,128)S(1)}, s32[2,16,256]{2,1,0:T(8,128)}, u32[]{:S(2)}) copy-start(s32[2,16,256]{2,1,0:T(8,128)} %types.3) | copy-start | bytes 98308
  4.1 11.6 %copy-start.4 = (s32[2,16,256]{2,1,0:T(8,128)S(1)}, s32[2,16,256]{2,1,0:T(8,128)}, u32[]{:S(2)}) copy-start(s32[2,16,256]{2,1,0:T(8,128)} %regions.3) | copy-start | bytes 98308
  4.1 4.9 %collective-permute-start.2 = (f32[9,8,256]{2,1,0:T(8,128)S(1)}, f32[9,8,256]{2,1,0:T(8,128)S(1)}, u32[]{:S(2)}, u32[]{:S(2)}) collective-permute-start(f32[9,8,256]{2,1,0:T(8,128)S(1)} %get-tuple-element.39.t), channel_id=1, source_target_pairs={{0,1},{1,0},{2,3},{3,2},{4,5},{5,4},{6,7},{7,6},{8,9},{9,8},{10,11... | collective-permute-start | bytes 221192 | tf_op jit(solution)/shard_map/ppermute | solution.py:522
  9.1 5.7 %collective-permute-start.4 = (f32[3,8,256]{2,1,0:T(8,128)S(1)}, f32[3,8,256]{2,1,0:T(8,128)S(1)}, u32[]{:S(2)}, u32[]{:S(2)}) collective-permute-start(f32[3,8,256]{2,1,0:T(8,128)S(1)} %shard_map.86), channel_id=1, source_target_pairs={{2,4},{4,2},{6,8},{8,6},{10,12},{12,10},{14,16},{16,14},{18,20},{2... | collective-permute-start | bytes 73736 | tf_op jit(solution)/shard_map/ppermute | solution.py:535
  9.7 5.9 %collective-permute-start.3 = (f32[3,8,256]{2,1,0:T(8,128)S(1)}, f32[3,8,256]{2,1,0:T(8,128)S(1)}, u32[]{:S(2)}, u32[]{:S(2)}) collective-permute-start(f32[3,8,256]{2,1,0:T(8,128)S(1)} %shard_map.86), channel_id=1, source_target_pairs={{0,2},{2,0},{4,6},{6,4},{8,10},{10,8},{12,14},{14,12},{16,18},{18,... | collective-permute-start | bytes 73736 | tf_op jit(solution)/shard_map/ppermute | solution.py:534
  15.7 21.9 %copy-start = (f32[19,2,16,256]{3,2,1,0:T(8,128)S(1)}, f32[19,2,16,256]{3,2,1,0:T(8,128)}, u32[]{:S(2)}) copy-start(f32[19,2,16,256]{3,2,1,0:T(8,128)} %pops.1) | copy-start | bytes 1867780
  17.4 6.3 %collective-permute-start.5 = (f32[6,8,256]{2,1,0:T(8,128)S(1)}, f32[6,8,256]{2,1,0:T(8,128)S(1)}, u32[]{:S(2)}, u32[]{:S(2)}) collective-permute-start(f32[6,8,256]{2,1,0:T(8,128)S(1)} %get-tuple-element.46), channel_id=1, source_target_pairs={{0,1},{1,0},{2,3},{3,2},{4,5},{5,4},{6,7},{7,6},{8,9},{9,8},{10,11... | collective-permute-start | bytes 147464 | tf_op jit(solution)/shard_map/ppermute | solution.py:522
  19.9 3.8 %collective-permute-start.6 = (f32[1,256]{1,0:T(1,128)S(1)}, f32[1,256]{1,0:T(1,128)S(1)}, u32[]{:S(2)}, u32[]{:S(2)}) collective-permute-start(f32[1,256]{1,0:T(1,128)S(1)} %get-tuple-element.47), channel_id=1, source_target_pairs={{0,4},{2,6},{4,0},{6,2},{8,12},{10,14},{12,8},{14,10},{16,20},{18,... | collective-permute-start | bytes 3080 | tf_op jit(solution)/shard_map/ppermute | solution.py:600
  23.7 1.5 %collective-permute-start.7 = (f32[11,16,256]{2,1,0:T(8,128)S(1)}, f32[11,16,256]{2,1,0:T(8,128)S(1)}, u32[]{:S(2)}, u32[]{:S(2)}) collective-permute-start(f32[11,16,256]{2,1,0:T(8,128)S(1)} %get-tuple-element.48), channel_id=1, source_target_pairs={{0,2},{2,0},{4,6},{6,4},{8,10},{10,8},{12,14},{14,12},{16,18},{18,... | collective-permute-start | bytes 540680 | tf_op jit(solution)/shard_map/ppermute | solution.py:534
  23.9 10.6 %collective-permute-start.8 = (f32[11,16,256]{2,1,0:T(8,128)S(1)}, f32[11,16,256]{2,1,0:T(8,128)S(1)}, u32[]{:S(2)}, u32[]{:S(2)}) collective-permute-start(f32[11,16,256]{2,1,0:T(8,128)S(1)} %get-tuple-element.49), channel_id=1, source_target_pairs={{2,4},{4,2},{6,8},{8,6},{10,12},{12,10},{14,16},{16,14},{18,20},{2... | collective-permute-start | bytes 540680 | tf_op jit(solution)/shard_map/ppermute | solution.py:535
  25.2 3.6 %collective-permute-start.9 = (f32[1,256]{1,0:T(1,128)S(1)}, f32[1,256]{1,0:T(1,128)S(1)}, u32[]{:S(2)}, u32[]{:S(2)}) collective-permute-start(f32[1,256]{1,0:T(1,128)S(1)} %fusion), channel_id=1, source_target_pairs={{0,1},{1,0},{2,3},{3,2},{4,5},{5,4},{6,7},{7,6},{8,9},{9,8},{10,11... | collective-permute-start | bytes 3080 | tf_op jit(solution)/shard_map/ppermute | solution.py:545
  28.7 5.7 %collective-permute-start.10 = (f32[1,256]{1,0:T(1,128)S(1)}, f32[1,256]{1,0:T(1,128)S(1)}, u32[]{:S(2)}, u32[]{:S(2)}) collective-permute-start(f32[1,256]{1,0:T(1,128)S(1)} %add.22), channel_id=1, source_target_pairs={{0,8},{2,10},{4,12},{6,14},{8,0},{10,2},{12,4},{14,6},{16,24},{18,... | collective-permute-start | bytes 3080 | tf_op jit(solution)/shard_map/ppermute | solution.py:545
  34.5 5.6 %collective-permute-start.11 = (f32[1,256]{1,0:T(1,128)S(1)}, f32[1,256]{1,0:T(1,128)S(1)}, u32[]{:S(2)}, u32[]{:S(2)}) collective-permute-start(f32[1,256]{1,0:T(1,128)S(1)} %add.23), channel_id=1, source_target_pairs={{0,16},{2,18},{4,20},{6,22},{8,24},{10,26},{12,28},{14,30},{16,0},... | collective-permute-start | bytes 3080 | tf_op jit(solution)/shard_map/ppermute | solution.py:545

commit v3 on v2

--- a/solution.py
+++ b/solution.py
@@ -40,7 +40,7 @@
 
 
 LO, HI = 0, 1
-POST, ADJ, FACTOR, FLAG = 0, 1, 2, 3
+POST, ADJ, FACTOR, FLAG, MOTION = 0, 1, 2, 3, 4
 
 
 def face_fields(kinds, axis, side):
@@ -49,13 +49,15 @@
     for kind in kinds:
         if kind == FLAG:
             fields.append((FLAG, 0))
+        elif kind == FACTOR and axis == 0:
+            fields += [(MOTION, k) for k in range(4)]
         else:
             fields += [(kind, q) for q in moving(axis, -sign if kind == ADJ else sign)]
     return fields
 
 
 class Layout:
-    def __init__(self, kinds, extra):
+    def __init__(self, kinds, extra, least_blocks=0):
         self.ax = [face_fields(kinds, 0, side) for side in (LO, HI)]
         self.slot = [{key: i for i, key in enumerate(fields)} for fields in self.ax]
         self.fields = len(self.ax[LO])
@@ -68,12 +70,12 @@
                     (corner if kind == FLAG or leaves else rest).append(key)
         corner += extra
         self.corner_blocks = -(-len(corner) // 8)
-        self.blocks = self.corner_blocks + -(-len(rest) // 8)
+        self.blocks = max(self.corner_blocks + -(-len(rest) // 8), least_blocks)
         self.place = {key: (i // 8, i % 8) for i, key in enumerate(corner)}
         self.place.update({key: (self.corner_blocks + i // 8, i % 8) for i, key in enumerate(rest)})
 
 
-FIRST = Layout((POST, ADJ, FACTOR, FLAG), [(LO, "label"), (HI, "label"), (LO, "own")])
+FIRST = Layout((POST, ADJ, FACTOR, FLAG), [(LO, "label"), (HI, "label"), (LO, "own")], 18)
 SECOND = Layout((POST, ADJ), [(LO, "sum")])
 
 
@@ -203,20 +205,26 @@
 
 
 class Fields:
-    def __init__(self, layout, own, parity, e, o, t, ec=None, oc=None):
+    def __init__(self, layout, own, parity, real, e, o, t, ec=None, oc=None):
         self.layout, self.own = layout, own
         self.e, self.o, self.t, self.ec, self.oc = e, o, t, ec, oc
         self.up_e = parity == 0
+        self.o_real = real == 1
         self.rows_a = own[POST].shape[1]
 
     def row(self, kind, q, a):
         if 0 <= a < self.rows_a:
             return self.own[FLAG][a] if kind == FLAG else self.own[kind][q, a]
-        if a < 0:
-            slot = self.layout.slot[HI][(kind, q)]
-            return jnp.where(self.up_e, self.o[slot], self.e[slot])
-        slot = self.layout.slot[LO][(kind, q)]
-        return jnp.where(self.up_e, self.e[slot], self.o[slot])
+        if kind == FACTOR:
+            weight, *velocity = (self.row(MOTION, k, a) for k in range(4))
+            return porosity_factor(q, weight, velocity)
+        slot = self.layout.slot[HI if a < 0 else LO][(kind, q)]
+        return self.beyond(kind, a, self.e[slot], self.o[slot])
+
+    def beyond(self, kind, a, e, o):
+        if kind in (ADJ, FLAG):
+            o = jnp.where(self.o_real, o, 0.0)
+        return jnp.where(self.up_e, o, e) if a < 0 else jnp.where(self.up_e, e, o)
 
     def message(self, key, a):
         block, i = self.layout.place[key]
@@ -228,7 +236,7 @@
             e, o = self.e[rows], self.o[rows]
         else:
             e, o = self.ec[rows], self.oc[rows]
-        return jnp.where(self.up_e, o, e) if a < 0 else jnp.where(self.up_e, e, o)
+        return self.beyond(key[1], a, e, o)
 
     def edge(self, side, kind, q, a):
         row = self.rows_a - 1 if a < 0 else 0 if a >= self.rows_a else a
@@ -298,9 +306,22 @@
     return jnp.broadcast_to(label.astype(jnp.float32), (1, wide))
 
 
+def porosity_factor(q, weight, velocity):
+    ua, ut, ur = velocity
+    pair = (q - 1) // 2
+    cu = projections(velocity)[pair]
+    scaled = (W_AXIS if pair < 3 else W_EDGE) * weight
+    still = -1.5 * (ua * ua + ut * ut + ur * ur)
+    return scaled * (still + 4.5 * cu * cu + (3.0 * cu if q % 2 else -3.0 * cu))
+
+
+def factor_weight(lin):
+    return -(lin["design"] * lin["rho"])
+
+
 def porosity_factors(lin):
     ua, ut, ur = lin["u"]
-    weight = -(lin["design"] * lin["rho"])
+    weight = factor_weight(lin)
     still = -1.5 * (ua * ua + ut * ut + ur * ur)
     result = [(1.0 / 3.0) * weight * still]
     for i, cu in enumerate(projections((ua, ut, ur))):
@@ -364,17 +385,19 @@
 
 
 def first_kernel(
-    parity_ref, pops, seed, porous, types, regions, post, factors, e_out, o_out, flags
+    parity_ref, real_ref, pops, seed, porous, types, regions, post, factors, e_out, o_out, flags, motion
 ):
     def body(where):
         values = load(pops, where)
         lin = linearise(values, porous[where], types[where], regions[where])
         store(post, where, collide(values, lin))
         store(factors, where, porosity_factors(lin))
+        for k, value in enumerate([factor_weight(lin), *lin["u"]]):
+            motion[(k,) + where] = value
 
     chunks(range(porous.shape[0]), porous.shape, body)
     flags[...] = jnp.where(types[...] != 1, 1.0, 0.0)
-    own = {POST: post, ADJ: seed, FACTOR: factors, FLAG: flags}
+    own = {POST: post, ADJ: seed, MOTION: motion, FLAG: flags}
     pack_axial(FIRST, own, parity_ref[0], e_out, o_out)
 
 
@@ -386,11 +409,11 @@
 
 
 def second_kernel(
-    parity_ref, post, seed, factors, flags, porous, types, regions, e, o, t, ec, oc,
+    parity_ref, real_ref, post, seed, factors, flags, porous, types, regions, e, o, t, ec, oc,
     post_next, adj, sens, around, e_out, o_out, t_out, partial, state, back, parts,
 ):
     own = {POST: post, ADJ: seed, FACTOR: factors, FLAG: flags}
-    fields = Fields(FIRST, own, parity_ref[0], e, o, t, ec, oc)
+    fields = Fields(FIRST, own, parity_ref[0], real_ref[0], e, o, t, ec, oc)
     rows_a, rows_t, rows_r = porous.shape
     for a in range(rows_a):
         centre = flags[a]
@@ -455,10 +478,10 @@
 
 
 def third_kernel(
-    parity_ref, post, adj, flags, around, pops, porous, types, regions, sens_one, e, o, t,
+    parity_ref, real_ref, post, adj, flags, around, pops, porous, types, regions, sens_one, e, o, t,
     final_hbm, result_hbm, sens, final, result, back, sems,
 ):
-    fields = Fields(SECOND, {POST: post, ADJ: adj}, parity_ref[0], e, o, t)
+    fields = Fields(SECOND, {POST: post, ADJ: adj}, parity_ref[0], real_ref[0], e, o, t)
     rows_a = porous.shape[0]
     stores = []
     for a in range(rows_a):
@@ -508,12 +531,17 @@
     )(*arrays)
 
 
-def even_pairs(size):
-    return [(i, i ^ 1) for i in range(size) if i ^ 1 < size]
-
-
-def odd_pairs(size):
-    return [(i, ((i + 1) ^ 1) - 1) for i in range(size) if 0 <= ((i + 1) ^ 1) - 1 < size]
+def axial_pairs(flip):
+    size_a, size_t = lax.axis_size("ax"), lax.axis_size("az")
+    pairs = []
+    for a in range(size_a):
+        partner = ((a + flip) ^ 1) - flip
+        for t in range(size_t):
+            if 0 <= partner < size_a:
+                pairs.append((a * size_t + t, partner * size_t + t))
+            elif size_t % 2 == 0:
+                pairs.append((a * size_t + t, a * size_t + (t ^ 1)))
+    return pairs
 
 
 def send_azimuthal(layout, message):
@@ -530,21 +558,18 @@
 
 
 def send_axial(e_message, o_message):
-    size = lax.axis_size("ax")
-    e = lax.ppermute(e_message, "ax", even_pairs(size))
-    return e, lax.ppermute(o_message, "ax", odd_pairs(size))
-
-
-def sum_over(x, axis, step, last_after=None):
-    size = lax.axis_size(axis)
-    if size & (size - 1):
-        return lax.psum(x, axis)
-    while step < size:
-        if last_after is not None and 2 * step == size:
-            x, _ = lax.optimization_barrier((x, last_after))
-        x = x + lax.ppermute(x, axis, [(i, i ^ step) for i in range(size)])
-        step *= 2
-    return x
+    e = lax.ppermute(e_message, ("ax", "az"), axial_pairs(0))
+    return e, lax.ppermute(o_message, ("ax", "az"), axial_pairs(1))
+
+
+def add_partner(x, flip_a, flip_t=0):
+    size_a, size_t = lax.axis_size("ax"), lax.axis_size("az")
+    pairs = [
+        (a * size_t + t, (a ^ flip_a) * size_t + (t ^ flip_t))
+        for a in range(size_a)
+        for t in range(size_t)
+    ]
+    return x + lax.ppermute(x, ("ax", "az"), pairs)
 
 
 def shards(initial, adjoint_seed, porosity, cell_type, region):
@@ -553,7 +578,9 @@
     wide = cells_[2]
     f32, i32 = jnp.float32, jnp.int32
     size_a, size_t = lax.axis_size("ax"), lax.axis_size("az")
-    parity = (lax.axis_index("ax") % 2).astype(i32).reshape(1)
+    index = lax.axis_index("ax")
+    real = (index != 0) & (index != size_a - 1)
+    place = ((index % 2).astype(i32).reshape(1), real.astype(i32).reshape(1))
 
     def axial(fields):
         return [((fields,) + cells_[1:], f32, VMEM)] * 2
@@ -569,10 +596,10 @@
     )
     post, factors, e, o, flags = call(
         first_kernel,
-        [pltpu.SMEM] + [VMEM] * 5,
+        [pltpu.SMEM] * 2 + [VMEM] * 5,
         [(pops, f32, VMEM), (pops, f32, VMEM)] + axial(FIRST.fields) + [(cells_, f32, VMEM)],
-        [],
-        parity, *near_inputs,
+        [VMEM((4,) + cells_, f32)],
+        *place, *near_inputs,
     )
     t_near = send_azimuthal(FIRST, t)
     e, o = send_axial(e, o)
@@ -587,17 +614,17 @@
     ec, oc = send_axial(corners, corners)
     post, adj, sens_one, around, e, o, t, total = call(
         second_kernel,
-        [pltpu.SMEM] + [VMEM] * 12,
+        [pltpu.SMEM] * 2 + [VMEM] * 12,
         [(pops, f32, VMEM), (pops, f32, VMEM), (cells_, f32, VMEM), ((18,) + cells_, f32, VMEM)]
         + axial(SECOND.fields + 1)
         + [((SECOND.blocks, 8, wide), f32, VMEM), ((1, wide), f32, VMEM)],
         [VMEM(pops, f32), VMEM(pops, f32), VMEM((2, 16, wide), f32)],
-        parity, post, adjoint_seed, factors, flags, porosity, cell_type, region, e, o, t_near, ec, oc,
+        *place, post, adjoint_seed, factors, flags, porosity, cell_type, region, e, o, t_near, ec, oc,
     )
     t_near = send_azimuthal(SECOND, t)
-    halving = size_a % 4 == 0 and size_a & (size_a - 1) == 0
+    halving = size_a >= 4 and not (size_a & (size_a - 1) or size_t & (size_t - 1))
     if halving:
-        total = total + lax.ppermute(total, "ax", [(i, i ^ 2) for i in range(size_a)])
+        total = add_partner(total, 3)
     e, o = call(
         corner_kernel,
         [VMEM] * 4,
@@ -609,18 +636,22 @@
     e, o = send_axial(e, o)
     if halving:
         block, i = SECOND.place[(LO, "sum")]
-        total = total + e[SECOND.fields, 8 * block + i : 8 * block + i + 1]
-        total = sum_over(total, "az", 1)
-        totals = sum_over(total, "ax", 4, o)
+        totals = total + e[SECOND.fields, 8 * block + i : 8 * block + i + 1]
+        flips = [(1, 1 << k) for k in range(size_t.bit_length() - 1)]
+        flips += [((1 << k) | 1, 0) for k in range(2, size_a.bit_length() - 1)]
+        for flip in flips:
+            if flip == flips[-1]:
+                totals, _ = lax.optimization_barrier((totals, o))
+            totals = add_partner(totals, *flip)
     else:
         totals = lax.psum(total, ("ax", "az"))
     final, adjoint, sensitivity = call(
         third_kernel,
-        [pltpu.SMEM] + [VMEM] * 12,
+        [pltpu.SMEM] * 2 + [VMEM] * 12,
         [(pops, f32, HBM), (pops, f32, HBM), (cells_, f32, VMEM)],
         [VMEM(pops, f32), VMEM(pops, f32), VMEM(pops, f32)]
         + [pltpu.SemaphoreType.DMA((2 * cells_[0],))],
-        parity, post, adj, flags, around, initial, porosity, cell_type, region, sens_one, e, o, t_near,
+        *place, post, adj, flags, around, initial, porosity, cell_type, region, sens_one, e, o, t_near,
     )
     return final, adjoint, sensitivity, totals[0, : size_a * size_t // 4]
 

time: 40.8 us -> 34.3 us (0.84)
  starting transfers between devices: 22.7 us -> 15.7 us
    ppermute x10, starting transfers between devices: 17.6 us -> 10.9 us  [the longest x4 6.61 us: add_partner(): return x + lax.ppermute(x, ('ax', 'az'), pairs)]
    ppermute x2, waiting for transfers between devices: 2.34 us -> 2.81 us  [send_azimuthal(): t = lax.ppermute(message, 'az', ring)]
  transfers between devices with their start and end apart: 12 -> 12, of which waited for: 6 -> 5; matrix products, arithmetic and copies ran while one was open for 0% -> 0% of each run, Pallas kernels for 6% -> 10%
where the time goes in v3:
time: 34.3 us; the launch traced here: 34.1 us
  starting transfers between devices  15.7 us (46%)
  waiting for transfers between devices  10.5 us (31%)
  Pallas kernels  6.58 us (19%)
  between operations  0.76 us (2%)
  other arithmetic  0.53 us (2%)
    ppermute x4, starting transfers between devices, add_partner(): return x + lax.ppermute(x, ('ax', 'az'), pairs)  6.61 us
    pallas_call x6, Pallas kernels, call(): pl.pallas_call(body, out_shape=[jax.ShapeDtypeStruct(shape, dtype) for sh...  6.58 us
    ppermute x4, waiting for transfers between devices, add_partner(): return x + lax.ppermute(x, ('ax', 'az'), pairs)  5.67 us
    ppermute x2, starting transfers between devices, send_azimuthal(): t = lax.ppermute(message, 'az', ring)  4.81 us
    ppermute x3, starting transfers between devices, send_axial(): return (e, lax.ppermute(o_message, ('ax', 'az'), axial_pairs(1)))  3.38 us
    ppermute x2, waiting for transfers between devices, send_azimuthal(): t = lax.ppermute(message, 'az', ring)  2.81 us
    ppermute x3, waiting for transfers between devices, send_axial(): return (e, lax.ppermute(o_message, ('ax', 'az'), axial_pairs(1)))  2 us
    ppermute x3, starting transfers between devices, send_axial(): e = lax.ppermute(e_message, ('ax', 'az'), axial_pairs(0))  0.95 us
  transfers between devices with their start and end apart: 12, of which 5 were waited for; matrix products, arithmetic and copies ran while one was open for 0% of the time, Pallas kernels for 10%

profile of v3, /device:TPU:0, one launch (start us, length us, event | category | flops | bytes accessed | tf_op | source)
XLA Modules:
  0.0 34.1 jit_solution(16575376764832918228)
XLA Ops:
  0.6 1.4 %shard_map.84 = (f32[19,2,16,256]{3,2,1,0:T(8,128)S(1)}, f32[19,2,16,256]{3,2,1,0:T(8,128)S(1)}, f32[2,16,256]{2,1,0:T(8,128)S(1)}, s32[2,16,256]{2,1,0:T(8,128)...) custom-call(f32[19,2,16,256]{3,2,1,0:T(8,128)} %pops.1, f32[19,2,16,256]{3,2,1,0:T(8,128)} %seed.1, ...), custom_call_target="tpu_custom_call" | custom-call | tf_op jit(solution)/shard_map/pallas_call | solution.py:522
  2.0 3.0 %collective-permute-start.2 = (f32[18,8,256]{2,1,0:T(8,128)S(1)}, f32[18,8,256]{2,1,0:T(8,128)S(1)}, u32[]{:S(2)}, u32[]{:S(2)}) collective-permute-start(f32[18,8,256]{2,1,0:T(8,128)S(1)} %get-tuple-element.39.t), channel_id=1, source_target_pairs={{0,1},{1,0},{2,3},{3,2},{4,5},{5,4},{6,7},{7,6},{8,9},{9,8},{10,11... | collective-permute-start | bytes 442376 | tf_op jit(solution)/shard_map/ppermute | solution.py:550
  5.1 0.8 %shard_map.85 = (f32[19,2,16,256]{3,2,1,0:T(8,128)S(1)}, f32[19,2,16,256]{3,2,1,0:T(8,128)S(1)}, f32[15,16,256]{2,1,0:T(8,128)S(1)}, f32[15,16,256]{2,1,0:T(8,128)S(1)}, f32[2,16,256]{2,1,0:T(8,128)S(1)}) custom-call(s32[1]{0:T(128)} %bitcast.parity_ref, s32[1]{0:T(128)} %bitcast.1.real_ref, f32[19,2,16,256]{3,2,1,0:T(8,128)S(1)} %get-tuple-element.29.pops, ...), custom_call_target="tpu_custom_call" | custom-call | tf_op jit(solution)/shard_map/pallas_call | solution.py:522
  5.9 0.1 collective-permute-start
  5.9 0.0 copy-start
  6.0 0.0 copy-start.2
  6.0 0.0 copy-start.3
  6.0 0.0 copy-start.4
  6.0 0.1 collective-permute-start.1
  6.1 2.8 %collective-permute-done.2.t_near.t = f32[18,8,256]{2,1,0:T(8,128)S(1)} collective-permute-done((f32[18,8,256]{2,1,0:T(8,128)S(1)}, f32[18,8,256]{2,1,0:T(8,128)S(1)}, u32[]{:S(2)}, u32[]{:S(2)}) %collective-permute-start.2) | collective-permute-done | bytes 147488 | tf_op jit(solution)/shard_map/ppermute | solution.py:550
  8.9 1.7 %collective-permute-start.4 = (f32[3,8,256]{2,1,0:T(8,128)S(1)}, f32[3,8,256]{2,1,0:T(8,128)S(1)}, u32[]{:S(2)}, u32[]{:S(2)}) collective-permute-start(f32[3,8,256]{2,1,0:T(8,128)S(1)} %shard_map.86), channel_id=1, source_target_pairs={{0,1},{1,0},{2,4},{3,5},{4,2},{5,3},{6,8},{7,9},{8,6},{9,7},{10,12... | collective-permute-start | bytes 73736 | tf_op jit(solution)/shard_map/ppermute | solution.py:562
  10.7 0.1 collective-permute-start.3
  10.8 2.0 %collective-permute-done.4.oc = f32[3,8,256]{2,1,0:T(8,128)S(1)} collective-permute-done((f32[3,8,256]{2,1,0:T(8,128)S(1)}, f32[3,8,256]{2,1,0:T(8,128)S(1)}, u32[]{:S(2)}, u32[]{:S(2)}) %collective-permute-start.4) | collective-permute-done | bytes 24608 | tf_op jit(solution)/shard_map/ppermute | solution.py:562
  12.8 0.0 collective-permute-done.3.ec
  12.8 0.0 collective-permute-done.e
  12.8 0.0 collective-permute-done.1.o
  12.8 0.0 copy-done
  12.8 0.0 copy-done.2
  12.8 0.0 copy-done.3
  12.8 0.0 copy-done.4
  12.8 0.0 copy-start.1
  12.8 1.8 %shard_map.87 = (f32[19,2,16,256]{3,2,1,0:T(8,128)S(1)}, f32[19,2,16,256]{3,2,1,0:T(8,128)S(1)}, f32[2,16,256]{2,1,0:T(8,128)S(1)}, f32[18,2,16,256]{3,2,1,0:T(8...) custom-call(s32[1]{0:T(128)} %bitcast.parity_ref, ...), custom_call_target="tpu_custom_call" | custom-call | tf_op jit(solution)/shard_map/pallas_call | solution.py:522
  14.6 1.8 %collective-permute-start.5 = (f32[6,8,256]{2,1,0:T(8,128)S(1)}, f32[6,8,256]{2,1,0:T(8,128)S(1)}, u32[]{:S(2)}, u32[]{:S(2)}) collective-permute-start(f32[6,8,256]{2,1,0:T(8,128)S(1)} %get-tuple-element.46), channel_id=1, source_target_pairs={{0,1},{1,0},{2,3},{3,2},{4,5},{5,4},{6,7},{7,6},{8,9},{9,8},{10,11... | collective-permute-start | bytes 147464 | tf_op jit(solution)/shard_map/ppermute | solution.py:550
  16.4 0.2 collective-permute-start.6
  16.6 2.7 %collective-permute-done.6 = f32[1,256]{1,0:T(1,128)S(1)} collective-permute-done((f32[1,256]{1,0:T(1,128)S(1)}, f32[1,256]{1,0:T(1,128)S(1)}, u32[]{:S(2)}, u32[]{:S(2)}) %collective-permute-start.6) | collective-permute-done | bytes 1056 | tf_op jit(solution)/shard_map/ppermute | solution.py:572
  19.4 0.0 collective-permute-done.5.t
  19.4 0.8 %collective-permute-start.7 = (f32[11,16,256]{2,1,0:T(8,128)S(1)}, f32[11,16,256]{2,1,0:T(8,128)S(1)}, u32[]{:S(2)}, u32[]{:S(2)}) collective-permute-start(f32[11,16,256]{2,1,0:T(8,128)S(1)} %get-tuple-element.48), channel_id=1, source_target_pairs={{0,2},{1,3},{2,0},{3,1},{4,6},{5,7},{6,4},{7,5},{8,10},{9,11},{10,... | collective-permute-start | bytes 540680 | tf_op jit(solution)/shard_map/ppermute | solution.py:561
  20.2 1.5 %collective-permute-start.8 = (f32[11,16,256]{2,1,0:T(8,128)S(1)}, f32[11,16,256]{2,1,0:T(8,128)S(1)}, u32[]{:S(2)}, u32[]{:S(2)}) collective-permute-start(f32[11,16,256]{2,1,0:T(8,128)S(1)} %get-tuple-element.49), channel_id=1, source_target_pairs={{0,1},{1,0},{2,4},{3,5},{4,2},{5,3},{6,8},{7,9},{8,6},{9,7},{10,12... | collective-permute-start | bytes 540680 | tf_op jit(solution)/shard_map/ppermute | solution.py:562
  21.7 0.0 collective-permute-done.7.e
  21.7 1.4 %collective-permute-start.9 = (f32[1,256]{1,0:T(1,128)S(1)}, f32[1,256]{1,0:T(1,128)S(1)}, u32[]{:S(2)}, u32[]{:S(2)}) collective-permute-start(f32[1,256]{1,0:T(1,128)S(1)} %fusion), channel_id=1, source_target_pairs={{0,3},{1,2},{2,1},{3,0},{4,7},{5,6},{6,5},{7,4},{8,11},{9,10},{10,... | collective-permute-start | bytes 3080 | tf_op jit(solution)/shard_map/ppermute | solution.py:572
  23.1 1.6 %collective-permute-done.9 = f32[1,256]{1,0:T(1,128)S(1)} collective-permute-done((f32[1,256]{1,0:T(1,128)S(1)}, f32[1,256]{1,0:T(1,128)S(1)}, u32[]{:S(2)}, u32[]{:S(2)}) %collective-permute-start.9) | collective-permute-done | bytes 1056 | tf_op jit(solution)/shard_map/ppermute | solution.py:572
  24.8 2.2 %collective-permute-start.10 = (f32[1,256]{1,0:T(1,128)S(1)}, f32[1,256]{1,0:T(1,128)S(1)}, u32[]{:S(2)}, u32[]{:S(2)}) collective-permute-start(f32[1,256]{1,0:T(1,128)S(1)} %add.22), channel_id=1, source_target_pairs={{0,10},{1,11},{2,8},{3,9},{4,14},{5,15},{6,12},{7,13},{8,2},{9,3},... | collective-permute-start | bytes 3080 | tf_op jit(solution)/shard_map/ppermute | solution.py:572
  27.0 1.3 %collective-permute-done.10 = f32[1,256]{1,0:T(1,128)S(1)} collective-permute-done((f32[1,256]{1,0:T(1,128)S(1)}, f32[1,256]{1,0:T(1,128)S(1)}, u32[]{:S(2)}, u32[]{:S(2)}) %collective-permute-start.10) | collective-permute-done | bytes 1056 | tf_op jit(solution)/shard_map/ppermute | solution.py:572
  28.3 0.0 collective-permute-done.8.o
  28.3 2.7 %collective-permute-start.11 = (f32[1,256]{1,0:T(1,128)S(1)}, f32[1,256]{1,0:T(1,128)S(1)}, u32[]{:S(2)}, u32[]{:S(2)}) collective-permute-start(f32[1,256]{1,0:T(1,128)S(1)} %add.23), channel_id=1, source_target_pairs={{0,18},{1,19},{2,16},{3,17},{4,22},{5,23},{6,20},{7,21},{8,26},{9,... | collective-permute-start | bytes 3080 | tf_op jit(solution)/shard_map/ppermute | solution.py:572
  31.0 0.0 copy-done.1
  31.0 2.6 %shard_map.89 = (f32[19,2,16,256]{3,2,1,0:T(8,128)}, f32[19,2,16,256]{3,2,1,0:T(8,128)}, f32[2,16,256]{2,1,0:T(8,128)}) custom-call(s32[1]{0:T(128)} %bitcast.parity_ref, s32[1]{0:T(128)} %bitcast.1.real_ref, f32[19,2,16,256]{3,2,1,0:T(8,128)S(1)} %get-tuple-element.40.post, f32[19,2,16,256]{3,2,1,0:T(8,128)S(1)} %get-tuple-element.41.adj, ...), custom_call_target="tpu_custom_call" | custom-call | tf_op jit(solution)/shard_map/pallas_call | solution.py:522
  33.6 0.0 collective-permute-done.11
  33.6 0.5 %fusion.1 = f32[8]{0:T(128)} fusion(f32[1,256]{1,0:T(1,128)S(1)} %collective-permute-done.11, f32[1,256]{1,0:T(1,128)S(1)} %add.23), kind=kLoop, calls=%fused_computation.3 | loop fusion | flops 8 | bytes 96 | tf_op jit(solution)/shard_map/squeeze | solution.py:656
  (6 shorter events, 0.0 us)
Async XLA Ops:
  2.0 6.9 %collective-permute-start.2 = (f32[18,8,256]{2,1,0:T(8,128)S(1)}, f32[18,8,256]{2,1,0:T(8,128)S(1)}, u32[]{:S(2)}, u32[]{:S(2)}) collective-permute-start(f32[18,8,256]{2,1,0:T(8,128)S(1)} %get-tuple-element.39.t), channel_id=1, source_target_pairs={{0,1},{1,0},{2,3},{3,2},{4,5},{5,4},{6,7},{7,6},{8,9},{9,8},{10,11... | collective-permute-start | bytes 442376 | tf_op jit(solution)/shard_map/ppermute | solution.py:550
  5.9 6.9 %collective-permute-start = (f32[15,16,256]{2,1,0:T(8,128)S(1)}, f32[15,16,256]{2,1,0:T(8,128)S(1)}, u32[]{:S(2)}, u32[]{:S(2)}) collective-permute-start(f32[15,16,256]{2,1,0:T(8,128)S(1)} %get-tuple-element.37), channel_id=1, source_target_pairs={{0,2},{1,3},{2,0},{3,1},{4,6},{5,7},{6,4},{7,5},{8,10},{9,11},{10,... | collective-permute-start | bytes 737288 | tf_op jit(solution)/shard_map/ppermute | solution.py:561
  5.9 6.8 %copy-start = (f32[19,2,16,256]{3,2,1,0:T(8,128)S(1)}, f32[19,2,16,256]{3,2,1,0:T(8,128)}, u32[]{:S(2)}) copy-start(f32[19,2,16,256]{3,2,1,0:T(8,128)} %seed.1) | copy-start | bytes 1867780
  6.0 6.8 %copy-start.2 = (f32[2,16,256]{2,1,0:T(8,128)S(1)}, f32[2,16,256]{2,1,0:T(8,128)}, u32[]{:S(2)}) copy-start(f32[2,16,256]{2,1,0:T(8,128)} %porous.3) | copy-start | bytes 98308
  6.0 6.8 %copy-start.3 = (s32[2,16,256]{2,1,0:T(8,128)S(1)}, s32[2,16,256]{2,1,0:T(8,128)}, u32[]{:S(2)}) copy-start(s32[2,16,256]{2,1,0:T(8,128)} %types.3) | copy-start | bytes 98308
  6.0 6.8 %copy-start.4 = (s32[2,16,256]{2,1,0:T(8,128)S(1)}, s32[2,16,256]{2,1,0:T(8,128)}, u32[]{:S(2)}) copy-start(s32[2,16,256]{2,1,0:T(8,128)} %regions.3) | copy-start | bytes 98308
  6.0 6.8 %collective-permute-start.1 = (f32[15,16,256]{2,1,0:T(8,128)S(1)}, f32[15,16,256]{2,1,0:T(8,128)S(1)}, u32[]{:S(2)}, u32[]{:S(2)}) collective-permute-start(f32[15,16,256]{2,1,0:T(8,128)S(1)} %get-tuple-element.38), channel_id=1, source_target_pairs={{0,1},{1,0},{2,4},{3,5},{4,2},{5,3},{6,8},{7,9},{8,6},{9,7},{10,12... | collective-permute-start | bytes 737288 | tf_op jit(solution)/shard_map/ppermute | solution.py:562
  8.9 3.8 %collective-permute-start.4 = (f32[3,8,256]{2,1,0:T(8,128)S(1)}, f32[3,8,256]{2,1,0:T(8,128)S(1)}, u32[]{:S(2)}, u32[]{:S(2)}) collective-permute-start(f32[3,8,256]{2,1,0:T(8,128)S(1)} %shard_map.86), channel_id=1, source_target_pairs={{0,1},{1,0},{2,4},{3,5},{4,2},{5,3},{6,8},{7,9},{8,6},{9,7},{10,12... | collective-permute-start | bytes 73736 | tf_op jit(solution)/shard_map/ppermute | solution.py:562
  10.7 2.1 %collective-permute-start.3 = (f32[3,8,256]{2,1,0:T(8,128)S(1)}, f32[3,8,256]{2,1,0:T(8,128)S(1)}, u32[]{:S(2)}, u32[]{:S(2)}) collective-permute-start(f32[3,8,256]{2,1,0:T(8,128)S(1)} %shard_map.86), channel_id=1, source_target_pairs={{0,2},{1,3},{2,0},{3,1},{4,6},{5,7},{6,4},{7,5},{8,10},{9,11},{10,... | collective-permute-start | bytes 73736 | tf_op jit(solution)/shard_map/ppermute | solution.py:561
  12.8 18.2 %copy-start.1 = (f32[19,2,16,256]{3,2,1,0:T(8,128)S(1)}, f32[19,2,16,256]{3,2,1,0:T(8,128)}, u32[]{:S(2)}) copy-start(f32[19,2,16,256]{3,2,1,0:T(8,128)} %pops.1) | copy-start | bytes 1867780
  14.6 4.8 %collective-permute-start.5 = (f32[6,8,256]{2,1,0:T(8,128)S(1)}, f32[6,8,256]{2,1,0:T(8,128)S(1)}, u32[]{:S(2)}, u32[]{:S(2)}) collective-permute-start(f32[6,8,256]{2,1,0:T(8,128)S(1)} %get-tuple-element.46), channel_id=1, source_target_pairs={{0,1},{1,0},{2,3},{3,2},{4,5},{5,4},{6,7},{7,6},{8,9},{9,8},{10,11... | collective-permute-start | bytes 147464 | tf_op jit(solution)/shard_map/ppermute | solution.py:550
  16.4 3.0 %collective-permute-start.6 = (f32[1,256]{1,0:T(1,128)S(1)}, f32[1,256]{1,0:T(1,128)S(1)}, u32[]{:S(2)}, u32[]{:S(2)}) collective-permute-start(f32[1,256]{1,0:T(1,128)S(1)} %get-tuple-element.47), channel_id=1, source_target_pairs={{0,6},{1,7},{2,4},{3,5},{4,2},{5,3},{6,0},{7,1},{8,14},{9,15},{10,... | collective-permute-start | bytes 3080 | tf_op jit(solution)/shard_map/ppermute | solution.py:572
  19.4 2.3 %collective-permute-start.7 = (f32[11,16,256]{2,1,0:T(8,128)S(1)}, f32[11,16,256]{2,1,0:T(8,128)S(1)}, u32[]{:S(2)}, u32[]{:S(2)}) collective-permute-start(f32[11,16,256]{2,1,0:T(8,128)S(1)} %get-tuple-element.48), channel_id=1, source_target_pairs={{0,2},{1,3},{2,0},{3,1},{4,6},{5,7},{6,4},{7,5},{8,10},{9,11},{10,... | collective-permute-start | bytes 540680 | tf_op jit(solution)/shard_map/ppermute | solution.py:561
  20.2 8.1 %collective-permute-start.8 = (f32[11,16,256]{2,1,0:T(8,128)S(1)}, f32[11,16,256]{2,1,0:T(8,128)S(1)}, u32[]{:S(2)}, u32[]{:S(2)}) collective-permute-start(f32[11,16,256]{2,1,0:T(8,128)S(1)} %get-tuple-element.49), channel_id=1, source_target_pairs={{0,1},{1,0},{2,4},{3,5},{4,2},{5,3},{6,8},{7,9},{8,6},{9,7},{10,12... | collective-permute-start | bytes 540680 | tf_op jit(solution)/shard_map/ppermute | solution.py:562
  21.7 3.0 %collective-permute-start.9 = (f32[1,256]{1,0:T(1,128)S(1)}, f32[1,256]{1,0:T(1,128)S(1)}, u32[]{:S(2)}, u32[]{:S(2)}) collective-permute-start(f32[1,256]{1,0:T(1,128)S(1)} %fusion), channel_id=1, source_target_pairs={{0,3},{1,2},{2,1},{3,0},{4,7},{5,6},{6,5},{7,4},{8,11},{9,10},{10,... | collective-permute-start | bytes 3080 | tf_op jit(solution)/shard_map/ppermute | solution.py:572
  24.8 3.5 %collective-permute-start.10 = (f32[1,256]{1,0:T(1,128)S(1)}, f32[1,256]{1,0:T(1,128)S(1)}, u32[]{:S(2)}, u32[]{:S(2)}) collective-permute-start(f32[1,256]{1,0:T(1,128)S(1)} %add.22), channel_id=1, source_target_pairs={{0,10},{1,11},{2,8},{3,9},{4,14},{5,15},{6,12},{7,13},{8,2},{9,3},... | collective-permute-start | bytes 3080 | tf_op jit(solution)/shard_map/ppermute | solution.py:572
  28.3 5.3 %collective-permute-start.11 = (f32[1,256]{1,0:T(1,128)S(1)}, f32[1,256]{1,0:T(1,128)S(1)}, u32[]{:S(2)}, u32[]{:S(2)}) collective-permute-start(f32[1,256]{1,0:T(1,128)S(1)} %add.23), channel_id=1, source_target_pairs={{0,18},{1,19},{2,16},{3,17},{4,22},{5,23},{6,20},{7,21},{8,26},{9,... | collective-permute-start | bytes 3080 | tf_op jit(solution)/shard_map/ppermute | solution.py:572

commit v4 on v3

--- a/solution.py
+++ b/solution.py
@@ -57,7 +57,7 @@
 
 
 class Layout:
-    def __init__(self, kinds, extra, least_blocks=0):
+    def __init__(self, kinds, extra):
         self.ax = [face_fields(kinds, 0, side) for side in (LO, HI)]
         self.slot = [{key: i for i, key in enumerate(fields)} for fields in self.ax]
         self.fields = len(self.ax[LO])
@@ -70,12 +70,12 @@
                     (corner if kind == FLAG or leaves else rest).append(key)
         corner += extra
         self.corner_blocks = -(-len(corner) // 8)
-        self.blocks = max(self.corner_blocks + -(-len(rest) // 8), least_blocks)
+        self.blocks = self.corner_blocks + -(-len(rest) // 8)
         self.place = {key: (i // 8, i % 8) for i, key in enumerate(corner)}
         self.place.update({key: (self.corner_blocks + i // 8, i % 8) for i, key in enumerate(rest)})
 
 
-FIRST = Layout((POST, ADJ, FACTOR, FLAG), [(LO, "label"), (HI, "label"), (LO, "own")], 18)
+FIRST = Layout((POST, ADJ, FACTOR, FLAG), [(LO, "label"), (HI, "label")])
 SECOND = Layout((POST, ADJ), [(LO, "sum")])
 
 
@@ -204,10 +204,14 @@
     return result, sens
 
 
+def face_rows(slot):
+    return slice(16 * slot, 16 * slot + 16)
+
+
 class Fields:
-    def __init__(self, layout, own, parity, real, e, o, t, ec=None, oc=None):
+    def __init__(self, layout, own, parity, real, e, o, t, ed=None, od=None):
         self.layout, self.own = layout, own
-        self.e, self.o, self.t, self.ec, self.oc = e, o, t, ec, oc
+        self.e, self.o, self.t, self.ed, self.od = e, o, t, ed, od
         self.up_e = parity == 0
         self.o_real = real == 1
         self.rows_a = own[POST].shape[1]
@@ -218,8 +222,12 @@
         if kind == FACTOR:
             weight, *velocity = (self.row(MOTION, k, a) for k in range(4))
             return porosity_factor(q, weight, velocity)
-        slot = self.layout.slot[HI if a < 0 else LO][(kind, q)]
-        return self.beyond(kind, a, self.e[slot], self.o[slot])
+        rows = face_rows(self.layout.slot[HI if a < 0 else LO][(kind, q)])
+        return self.beyond(kind, a, self.e[rows, :], self.o[rows, :])
+
+    def row_label(self, a):
+        row = slice(16 * self.layout.fields, 16 * self.layout.fields + 1)
+        return self.beyond(None, a, self.e[row, :], self.o[row, :])
 
     def beyond(self, kind, a, e, o):
         if kind in (ADJ, FLAG):
@@ -228,14 +236,14 @@
 
     def message(self, key, a):
         block, i = self.layout.place[key]
-        rows = (block, slice(i, i + 1))
         if 0 <= a < self.rows_a:
-            return self.t[rows]
-        if self.ec is None:
-            rows = (self.layout.fields, slice(8 * block + i, 8 * block + i + 1))
-            e, o = self.e[rows], self.o[rows]
+            return self.t[block, i : i + 1, :]
+        if self.ed is None:
+            row = 16 * self.layout.fields + 8 * block + i
+            e, o = self.e[row : row + 1, :], self.o[row : row + 1, :]
         else:
-            e, o = self.ec[rows], self.oc[rows]
+            block = max(block - 1, 0)
+            e, o = self.ed[block, i : i + 1, :], self.od[block, i : i + 1, :]
         return self.beyond(key[1], a, e, o)
 
     def edge(self, side, kind, q, a):
@@ -275,8 +283,8 @@
     for slot in range(layout.fields):
         low = cells(own, *layout.ax[LO][slot], 0)[...]
         high = cells(own, *layout.ax[HI][slot], rows_a - 1)[...]
-        e_ref[slot] = jnp.where(even, high, low)
-        o_ref[slot] = jnp.where(even, low, high)
+        e_ref[face_rows(slot), :] = jnp.where(even, high, low)
+        o_ref[face_rows(slot), :] = jnp.where(even, low, high)
 
 
 def chunks(rows_a, shape, body):
@@ -331,62 +339,27 @@
     return result
 
 
-def edge_kernel(
-    pops_hbm, seed_hbm, porous_hbm, types_hbm, regions_hbm,
-    pops, seed, porous, types, regions, t_out, edge, edge_post, edge_factors, sems,
+def first_kernel(
+    parity_ref, pops_hbm, seed_hbm, porous_hbm, types_hbm, regions_hbm,
+    post, factors, e_out, o_out, t_out, ed_out, od_out, flags,
+    pops, seed, porous, types, regions, motion, sems,
 ):
-    rows_a, rows_t, rows_r = porous.shape
+    rows_a, _, rows_r = porous.shape
     pairs = [(types_hbm, types), (regions_hbm, regions), (porous_hbm, porous)]
-    pairs += [(pops_hbm, pops), (seed_hbm, seed)]
+    pairs += [(pops_hbm.at[:, a], pops.at[:, a]) for a in range(rows_a)] + [(seed_hbm, seed)]
     loads = [pltpu.make_async_copy(*pair, sems.at[i]) for i, pair in enumerate(pairs)]
     for copy in loads:
         copy.start()
     for copy in loads[:3]:
         copy.wait()
+    flags[...] = jnp.where(types[...] != 1, 1.0, 0.0)
     label = label_of(regions, rows_r)
-    for key in ((LO, "label"), (HI, "label"), (LO, "own")):
-        block, i = FIRST.place[key]
+    for side in (LO, HI):
+        block, i = FIRST.place[(side, "label")]
         t_out[block, i : i + 1, :] = label
-    columns = [(a, t) for a in range(rows_a) for t in (0, rows_t - 1)]
-
-    def gather(source, target):
-        for i, (a, t) in enumerate(columns):
-            target[i : i + 1, :] = source[a, t : t + 1, :]
-
-    gather(porous, edge.at[19])
-    gather_types = jnp.concatenate([types[a, t : t + 1, :] for a, t in columns] * 2)
-    gather_regions = jnp.concatenate([regions[a, t : t + 1, :] for a, t in columns] * 2)
-    for i in range(len(columns), edge.shape[1]):
-        edge[:, i, :] = jnp.ones((edge.shape[0], rows_r), jnp.float32)
-    loads[3].wait()
-    for q in range(19):
-        gather(pops.at[q], edge.at[q])
-    values = [edge[q] for q in range(19)]
-    lin = linearise(values, edge[19], gather_types, gather_regions)
-    post = collide(values, lin)
-    factors = porosity_factors(lin)
-    for q in range(19):
-        edge_post[q] = post[q]
-        edge_factors[q] = factors[q]
-    edge[0] = jnp.where(gather_types != 1, 1.0, 0.0)
-    loads[4].wait()
-    for key, (block, i) in FIRST.place.items():
-        if len(key) == 4:
-            side, kind, q, a = key
-            t = 0 if side == LO else rows_t - 1
-            k = columns.index((a, t))
-            if kind == ADJ:
-                row = seed[q, a, t : t + 1, :]
-            elif kind == FLAG:
-                row = edge[0, k : k + 1, :]
-            else:
-                row = (edge_post if kind == POST else edge_factors)[q, k : k + 1, :]
-            t_out[block, i : i + 1, :] = row
-
-
-def first_kernel(
-    parity_ref, real_ref, pops, seed, porous, types, regions, post, factors, e_out, o_out, flags, motion
-):
+    for out in (e_out, o_out):
+        out[16 * FIRST.fields : 16 * FIRST.fields + 8, :] = jnp.broadcast_to(label, (8, rows_r))
+
     def body(where):
         values = load(pops, where)
         lin = linearise(values, porous[where], types[where], regions[where])
@@ -395,25 +368,26 @@
         for k, value in enumerate([factor_weight(lin), *lin["u"]]):
             motion[(k,) + where] = value
 
-    chunks(range(porous.shape[0]), porous.shape, body)
-    flags[...] = jnp.where(types[...] != 1, 1.0, 0.0)
-    own = {POST: post, ADJ: seed, MOTION: motion, FLAG: flags}
+    for a in range(rows_a):
+        loads[3 + a].wait()
+        chunks([a], porous.shape, body)
+    loads[-1].wait()
+    own = {POST: post, ADJ: seed, FACTOR: factors, MOTION: motion, FLAG: flags}
+    even = parity_ref[0] == 0
     pack_axial(FIRST, own, parity_ref[0], e_out, o_out)
-
-
-def forward_kernel(t_near, t, corners):
-    for block in range(FIRST.corner_blocks):
-        corners[block] = t_near[block]
-    block, i = FIRST.place[(LO, "own")]
-    corners[block, i : i + 1, :] = t[block, i : i + 1, :]
+    pack_azimuthal(FIRST, own, t_out)
+    ed_out[0] = jnp.where(even, t_out[0], t_out[1])
+    od_out[0] = jnp.where(even, t_out[1], t_out[0])
+    for out in (ed_out, od_out):
+        out[1] = t_out[2]
 
 
 def second_kernel(
-    parity_ref, real_ref, post, seed, factors, flags, porous, types, regions, e, o, t, ec, oc,
+    parity_ref, real_ref, post, seed, factors, flags, porous, types, regions, e, o, t, ed, od,
     post_next, adj, sens, around, e_out, o_out, t_out, partial, state, back, parts,
 ):
     own = {POST: post, ADJ: seed, FACTOR: factors, FLAG: flags}
-    fields = Fields(FIRST, own, parity_ref[0], real_ref[0], e, o, t, ec, oc)
+    fields = Fields(FIRST, own, parity_ref[0], real_ref[0], e, o, t, ed, od)
     rows_a, rows_t, rows_r = porous.shape
     for a in range(rows_a):
         centre = flags[a]
@@ -455,7 +429,7 @@
         low, centre, high = (functools.reduce(jnp.add, sums[(beyond, st)]) for st in (-1, 0, 1))
         inner = centre + jnp.where(at_t == 0, 0.0, low) + jnp.where(at_t == rows_t - 1, 0.0, high)
         a = {-1: -1, 0: 0, 1: rows_a}[beyond]
-        label = fields.message((LO, "own"), a) if beyond else label_of(regions, rows_r)
+        label = fields.row_label(a) if beyond else label_of(regions, rows_r)
         rows.append((jnp.sum(inner, axis=0, keepdims=True), label))
         rows.append((high[rows_t - 1 : rows_t], fields.message((LO, "label"), a)))
         rows.append((low[0:1], fields.message((HI, "label"), a)))
@@ -470,11 +444,12 @@
 
 
 def corner_kernel(e, o, t, total, e_out, o_out):
-    slot, (row, i) = SECOND.fields, SECOND.place[(LO, "sum")]
+    block, i = SECOND.place[(LO, "sum")]
     for out in (e_out, o_out):
-        for block in range(SECOND.corner_blocks):
-            out[slot, 8 * block : 8 * block + 8, :] = t[block]
-        out[slot, 8 * row + i : 8 * row + i + 1, :] = total[...]
+        corners = out.at[16 * SECOND.fields : 16 * SECOND.fields + 16]
+        for k in range(SECOND.corner_blocks):
+            corners[8 * k : 8 * k + 8, :] = t[k]
+        corners[8 * block + i : 8 * block + i + 1, :] = total[...]
 
 
 def third_kernel(
@@ -531,45 +506,63 @@
     )(*arrays)
 
 
-def axial_pairs(flip):
+def axial_pairs(flip, shift_t=0):
     size_a, size_t = lax.axis_size("ax"), lax.axis_size("az")
     pairs = []
     for a in range(size_a):
         partner = ((a + flip) ^ 1) - flip
         for t in range(size_t):
             if 0 <= partner < size_a:
-                pairs.append((a * size_t + t, partner * size_t + t))
+                pairs.append((a * size_t + t, partner * size_t + (t + shift_t) % size_t))
+            elif shift_t:
+                pairs.append((a * size_t + t, a * size_t + (t + shift_t) % size_t))
             elif size_t % 2 == 0:
                 pairs.append((a * size_t + t, a * size_t + (t ^ 1)))
     return pairs
 
 
+def from_both_sectors(message, high_rows, send):
+    if lax.axis_size("az") == 2:
+        return send(message, 1)
+    return jnp.where(jnp.asarray(high_rows), send(message, 1), send(message, -1))
+
+
+def high_rows(layout):
+    rows = np.zeros((layout.blocks, 8, 1), bool)
+    for key, (block, i) in layout.place.items():
+        rows[block, i] = key[0] == HI
+    return rows
+
+
 def send_azimuthal(layout, message):
     size = lax.axis_size("az")
-    ring = [(i, (i + 1) % size) for i in range(size)]
-    t = lax.ppermute(message, "az", ring)
-    if size > 2:
-        from_high = np.zeros((layout.blocks, 8, 1), bool)
-        for key, (block, i) in layout.place.items():
-            from_high[block, i] = key[0] == HI
-        t_down = lax.ppermute(message, "az", [(j, i) for i, j in ring])
-        t = jnp.where(jnp.asarray(from_high), t, t_down)
-    return t
-
-
-def send_axial(e_message, o_message):
-    e = lax.ppermute(e_message, ("ax", "az"), axial_pairs(0))
-    return e, lax.ppermute(o_message, ("ax", "az"), axial_pairs(1))
-
-
-def add_partner(x, flip_a, flip_t=0):
+
+    def send(x, shift):
+        return lax.ppermute(x, "az", [(i, (i + shift) % size) for i in range(size)])
+
+    return from_both_sectors(message, high_rows(layout), send)
+
+
+def send_axial(message, flip):
+    return lax.ppermute(message, ("ax", "az"), axial_pairs(flip))
+
+
+def send_diagonal(message, flip):
+    def send(x, shift):
+        return lax.ppermute(x, ("ax", "az"), axial_pairs(flip, shift))
+
+    rows = high_rows(FIRST)
+    return from_both_sectors(message, np.stack([rows[0], rows[2]]), send)
+
+
+def from_partner(x, flip_a, flip_t):
     size_a, size_t = lax.axis_size("ax"), lax.axis_size("az")
     pairs = [
         (a * size_t + t, (a ^ flip_a) * size_t + (t ^ flip_t))
         for a in range(size_a)
         for t in range(size_t)
     ]
-    return x + lax.ppermute(x, ("ax", "az"), pairs)
+    return lax.ppermute(x, ("ax", "az"), pairs)
 
 
 def shards(initial, adjoint_seed, porosity, cell_type, region):
@@ -582,67 +575,57 @@
     real = (index != 0) & (index != size_a - 1)
     place = ((index % 2).astype(i32).reshape(1), real.astype(i32).reshape(1))
 
-    def axial(fields):
-        return [((fields,) + cells_[1:], f32, VMEM)] * 2
+    def axial(layout, more):
+        return [((16 * layout.fields + more, wide), f32, VMEM)] * 2
+
+    def azimuthal(layout):
+        return [((layout.blocks, 8, wide), f32, VMEM)]
 
     inputs = (initial, adjoint_seed, porosity, cell_type, region)
-    *near_inputs, t = call(
-        edge_kernel,
-        [HBM] * 5,
-        [(x.shape, x.dtype, VMEM) for x in inputs] + [((FIRST.blocks, 8, wide), f32, VMEM)],
-        [VMEM((20, 8, wide), f32), VMEM((19, 8, wide), f32), VMEM((19, 8, wide), f32)]
-        + [pltpu.SemaphoreType.DMA((5,))],
+    post, factors, e, o, t, ed, od, flags = call(
+        first_kernel,
+        [pltpu.SMEM] + [HBM] * 5,
+        [(pops, f32, VMEM), (pops, f32, VMEM)] + axial(FIRST, 8) + azimuthal(FIRST)
+        + [((2, 8, wide), f32, VMEM)] * 2 + [(cells_, f32, VMEM)],
+        [VMEM(x.shape, x.dtype) for x in inputs]
+        + [VMEM((4,) + cells_, f32), pltpu.SemaphoreType.DMA((4 + cells_[0],))],
+        place[0],
         *(pltpu.with_memory_space_constraint(x, HBM) for x in inputs),
     )
-    post, factors, e, o, flags = call(
-        first_kernel,
-        [pltpu.SMEM] * 2 + [VMEM] * 5,
-        [(pops, f32, VMEM), (pops, f32, VMEM)] + axial(FIRST.fields) + [(cells_, f32, VMEM)],
-        [VMEM((4,) + cells_, f32)],
-        *place, *near_inputs,
-    )
+    e, o = send_axial(e, 0), send_axial(o, 1)
     t_near = send_azimuthal(FIRST, t)
-    e, o = send_axial(e, o)
-    corners = call(
-        forward_kernel,
-        [VMEM] * 2,
-        [((FIRST.corner_blocks, 8, wide), f32, VMEM)],
-        [],
-        t_near, t,
-        cost=pl.CostEstimate(flops=1 << 30, bytes_accessed=40 << 20, transcendentals=0),
-    )[0]
-    ec, oc = send_axial(corners, corners)
+    ed, od = send_diagonal(ed, 0), send_diagonal(od, 1)
     post, adj, sens_one, around, e, o, t, total = call(
         second_kernel,
         [pltpu.SMEM] * 2 + [VMEM] * 12,
         [(pops, f32, VMEM), (pops, f32, VMEM), (cells_, f32, VMEM), ((18,) + cells_, f32, VMEM)]
-        + axial(SECOND.fields + 1)
-        + [((SECOND.blocks, 8, wide), f32, VMEM), ((1, wide), f32, VMEM)],
+        + axial(SECOND, 16) + azimuthal(SECOND) + [((1, wide), f32, VMEM)],
         [VMEM(pops, f32), VMEM(pops, f32), VMEM((2, 16, wide), f32)],
-        *place, post, adjoint_seed, factors, flags, porosity, cell_type, region, e, o, t_near, ec, oc,
+        *place, post, adjoint_seed, factors, flags, porosity, cell_type, region, e, o, t_near, ed, od,
     )
     t_near = send_azimuthal(SECOND, t)
+    block, i = SECOND.place[(LO, "sum")]
     halving = size_a >= 4 and not (size_a & (size_a - 1) or size_t & (size_t - 1))
+    flips = [((1 << k) | 1, 0) for k in range(2, size_a.bit_length() - 1)]
     if halving:
-        total = add_partner(total, 3)
+        total = total + from_partner(total, 3, 0)
+        flips = [(1, 1 << k) for k in range(size_t.bit_length() - 1)] + flips
     e, o = call(
         corner_kernel,
         [VMEM] * 4,
-        axial(SECOND.fields + 1),
+        axial(SECOND, 16),
         [],
         e, o, t_near, total,
         aliases={0: 0, 1: 1},
     )
-    e, o = send_axial(e, o)
+    e, o = send_axial(e, 0), send_axial(o, 1)
     if halving:
-        block, i = SECOND.place[(LO, "sum")]
-        totals = total + e[SECOND.fields, 8 * block + i : 8 * block + i + 1]
-        flips = [(1, 1 << k) for k in range(size_t.bit_length() - 1)]
-        flips += [((1 << k) | 1, 0) for k in range(2, size_a.bit_length() - 1)]
+        row = 16 * SECOND.fields + 8 * block + i
+        totals = total + e[row : row + 1]
         for flip in flips:
             if flip == flips[-1]:
                 totals, _ = lax.optimization_barrier((totals, o))
-            totals = add_partner(totals, *flip)
+            totals = totals + from_partner(totals, *flip)
     else:
         totals = lax.psum(total, ("ax", "az"))
     final, adjoint, sensitivity = call(

time: 34.3 us -> 33.4 us (0.974)
  waiting for transfers between devices: 10.5 us -> 9.51 us
  starting transfers between devices: 15.7 us -> 16.1 us
    ppermute x12, waiting for transfers between devices: 10.5 us -> 9.51 us  [the longest x4 5.91 us: from_partner(): return lax.ppermute(x, ('ax', 'az'), pairs)]
    ppermute x12, starting transfers between devices: 15.7 us -> 16.1 us  [the longest x4 6.37 us: from_partner(): return lax.ppermute(x, ('ax', 'az'), pairs)]
    pallas_call x6 -> x4, Pallas kernels: 6.58 us -> 6.33 us  [call(): pl.pallas_call(body, out_shape=[jax.ShapeDtypeStruct(shape, dtype) for sh...]
  transfers between devices with their start and end apart: 12 -> 12, of which waited for: 5 -> 5; matrix products, arithmetic and copies ran while one was open for 0% -> 0% of each run, Pallas kernels for 10% -> 8%
where the time goes in v4:
time: 33.4 us; the launch traced here: 33.3 us
  starting transfers between devices  16.1 us (48%)
  waiting for transfers between devices  9.51 us (28%)
  Pallas kernels  6.33 us (19%)
  between operations  0.76 us (2%)
  other arithmetic  0.53 us (2%)
    ppermute x4, starting transfers between devices, from_partner(): return lax.ppermute(x, ('ax', 'az'), pairs)  6.37 us
    pallas_call x4, Pallas kernels, call(): pl.pallas_call(body, out_shape=[jax.ShapeDtypeStruct(shape, dtype) for sh...  6.33 us
    ppermute x4, waiting for transfers between devices, from_partner(): return lax.ppermute(x, ('ax', 'az'), pairs)  5.91 us
    ppermute x4, starting transfers between devices, send_axial(): return lax.ppermute(message, ('ax', 'az'), axial_pairs(flip))  4.72 us
    ppermute x2, waiting for transfers between devices, send(): return lax.ppermute(x, ('ax', 'az'), axial_pairs(flip, shift))  3.59 us
    ppermute x2, starting transfers between devices, send(): return lax.ppermute(x, ('ax', 'az'), axial_pairs(flip, shift))  2.88 us
    ppermute x2, starting transfers between devices, send(): return lax.ppermute(x, 'az', [(i, (i + shift) % size) for i in range(size)])  2.13 us
  transfers between devices with their start and end apart: 12, of which 5 were waited for; matrix products, arithmetic and copies ran while one was open for 0% of the time, Pallas kernels for 8%

profile of v4, /device:TPU:0, one launch (start us, length us, event | category | flops | bytes accessed | tf_op | source)
XLA Modules:
  0.0 33.3 jit_solution(11992877409985665789)
XLA Ops:
  0.6 0.0 copy-start
  0.7 0.0 copy-start.2
  0.7 0.0 copy-start.3
  0.7 0.0 copy-start.4
  0.7 2.0 %shard_map.84 = (f32[19,2,16,256]{3,2,1,0:T(8,128)S(1)}, f32[19,2,16,256]{3,2,1,0:T(8,128)S(1)}, f32[248,256]{1,0:T(8,128)S(1)}, f32[248,256]{1,0:T(8,128)S(1)},...) custom-call(s32[1]{0:T(128)} %bitcast.parity_ref, ...), custom_call_target="tpu_custom_call" | custom-call | tf_op jit(solution)/shard_map/pallas_call | solution.py:497
  2.7 0.5 %collective-permute-start = (f32[248,256]{1,0:T(8,128)S(1)}, f32[248,256]{1,0:T(8,128)S(1)}, u32[]{:S(2)}, u32[]{:S(2)}) collective-permute-start(f32[248,256]{1,0:T(8,128)S(1)} %get-tuple-element.29), channel_id=1, source_target_pairs={{0,2},{1,3},{2,0},{3,1},{4,6},{5,7},{6,4},{7,5},{8,10},{9,11},{10,... | collective-permute-start | bytes 761864 | tf_op jit(solution)/shard_map/ppermute | solution.py:547
  3.2 2.6 %collective-permute-start.1 = (f32[248,256]{1,0:T(8,128)S(1)}, f32[248,256]{1,0:T(8,128)S(1)}, u32[]{:S(2)}, u32[]{:S(2)}) collective-permute-start(f32[248,256]{1,0:T(8,128)S(1)} %get-tuple-element.30), channel_id=1, source_target_pairs={{0,1},{1,0},{2,4},{3,5},{4,2},{5,3},{6,8},{7,9},{8,6},{9,7},{10,12... | collective-permute-start | bytes 761864 | tf_op jit(solution)/shard_map/ppermute | solution.py:547
  5.8 0.1 collective-permute-start.2
  5.8 1.4 %collective-permute-start.3 = (f32[2,8,256]{2,1,0:T(8,128)S(1)}, f32[2,8,256]{2,1,0:T(8,128)S(1)}, u32[]{:S(2)}, u32[]{:S(2)}) collective-permute-start(f32[2,8,256]{2,1,0:T(8,128)S(1)} %get-tuple-element.32), channel_id=1, source_target_pairs={{0,3},{1,2},{2,1},{3,0},{4,7},{5,6},{6,5},{7,4},{8,11},{9,10},{10,... | collective-permute-start | bytes 49160 | tf_op jit(solution)/shard_map/ppermute | solution.py:552
  7.2 1.5 %collective-permute-start.4 = (f32[2,8,256]{2,1,0:T(8,128)S(1)}, f32[2,8,256]{2,1,0:T(8,128)S(1)}, u32[]{:S(2)}, u32[]{:S(2)}) collective-permute-start(f32[2,8,256]{2,1,0:T(8,128)S(1)} %get-tuple-element.33), channel_id=1, source_target_pairs={{0,1},{1,0},{2,5},{3,4},{4,3},{5,2},{6,9},{7,8},{8,7},{9,6},{10,13... | collective-permute-start | bytes 49160 | tf_op jit(solution)/shard_map/ppermute | solution.py:552
  8.7 3.0 %collective-permute-done.3.ed = f32[2,8,256]{2,1,0:T(8,128)S(1)} collective-permute-done((f32[2,8,256]{2,1,0:T(8,128)S(1)}, f32[2,8,256]{2,1,0:T(8,128)S(1)}, u32[]{:S(2)}, u32[]{:S(2)}) %collective-permute-start.3) | collective-permute-done | bytes 16416 | tf_op jit(solution)/shard_map/ppermute | solution.py:552
  11.7 0.6 %collective-permute-done.4.od = f32[2,8,256]{2,1,0:T(8,128)S(1)} collective-permute-done((f32[2,8,256]{2,1,0:T(8,128)S(1)}, f32[2,8,256]{2,1,0:T(8,128)S(1)}, u32[]{:S(2)}, u32[]{:S(2)}) %collective-permute-start.4) | collective-permute-done | bytes 16416 | tf_op jit(solution)/shard_map/ppermute | solution.py:552
  12.3 0.0 collective-permute-done.2.t
  12.3 0.0 collective-permute-done.e
  12.3 0.0 collective-permute-done.1.o
  12.3 0.0 copy-done
  12.3 0.0 copy-done.2
  12.3 0.0 copy-done.3
  12.4 0.0 copy-done.4
  12.4 0.0 copy-start.1
  12.4 1.8 %shard_map.85 = (f32[19,2,16,256]{3,2,1,0:T(8,128)S(1)}, f32[19,2,16,256]{3,2,1,0:T(8,128)S(1)}, f32[2,16,256]{2,1,0:T(8,128)S(1)}, f32[18,2,16,256]{3,2,1,0:T(8...) custom-call(s32[1]{0:T(128)} %bitcast.parity_ref, ...), custom_call_target="tpu_custom_call" | custom-call | tf_op jit(solution)/shard_map/pallas_call | solution.py:497
  14.1 2.1 %collective-permute-start.5 = (f32[6,8,256]{2,1,0:T(8,128)S(1)}, f32[6,8,256]{2,1,0:T(8,128)S(1)}, u32[]{:S(2)}, u32[]{:S(2)}) collective-permute-start(f32[6,8,256]{2,1,0:T(8,128)S(1)} %get-tuple-element.40), channel_id=1, source_target_pairs={{0,1},{1,0},{2,3},{3,2},{4,5},{5,4},{6,7},{7,6},{8,9},{9,8},{10,11... | collective-permute-start | bytes 147464 | tf_op jit(solution)/shard_map/ppermute | solution.py:541
  16.2 0.0 collective-permute-start.6
  16.2 3.0 %collective-permute-done.6 = f32[1,256]{1,0:T(1,128)S(1)} collective-permute-done((f32[1,256]{1,0:T(1,128)S(1)}, f32[1,256]{1,0:T(1,128)S(1)}, u32[]{:S(2)}, u32[]{:S(2)}) %collective-permute-start.6) | collective-permute-done | bytes 1056 | tf_op jit(solution)/shard_map/ppermute | solution.py:565
  19.2 0.0 collective-permute-done.5.t
  19.2 0.2 collective-permute-start.7
  19.4 1.4 %collective-permute-start.8 = (f32[176,256]{1,0:T(8,128)S(1)}, f32[176,256]{1,0:T(8,128)S(1)}, u32[]{:S(2)}, u32[]{:S(2)}) collective-permute-start(f32[176,256]{1,0:T(8,128)S(1)} %get-tuple-element.43), channel_id=1, source_target_pairs={{0,1},{1,0},{2,4},{3,5},{4,2},{5,3},{6,8},{7,9},{8,6},{9,7},{10,12... | collective-permute-start | bytes 540680 | tf_op jit(solution)/shard_map/ppermute | solution.py:547
  20.8 0.0 collective-permute-done.7.e
  20.8 1.4 %collective-permute-start.9 = (f32[1,256]{1,0:T(1,128)S(1)}, f32[1,256]{1,0:T(1,128)S(1)}, u32[]{:S(2)}, u32[]{:S(2)}) collective-permute-start(f32[1,256]{1,0:T(1,128)S(1)} %slice_add_fusion), channel_id=1, source_target_pairs={{0,3},{1,2},{2,1},{3,0},{4,7},{5,6},{6,5},{7,4},{8,11},{9,10},{10,... | collective-permute-start | bytes 3080 | tf_op jit(solution)/shard_map/ppermute | solution.py:565
  22.3 1.6 %collective-permute-done.9 = f32[1,256]{1,0:T(1,128)S(1)} collective-permute-done((f32[1,256]{1,0:T(1,128)S(1)}, f32[1,256]{1,0:T(1,128)S(1)}, u32[]{:S(2)}, u32[]{:S(2)}) %collective-permute-start.9) | collective-permute-done | bytes 1056 | tf_op jit(solution)/shard_map/ppermute | solution.py:565
  23.9 2.2 %collective-permute-start.10 = (f32[1,256]{1,0:T(1,128)S(1)}, f32[1,256]{1,0:T(1,128)S(1)}, u32[]{:S(2)}, u32[]{:S(2)}) collective-permute-start(f32[1,256]{1,0:T(1,128)S(1)} %add.22), channel_id=1, source_target_pairs={{0,10},{1,11},{2,8},{3,9},{4,14},{5,15},{6,12},{7,13},{8,2},{9,3},... | collective-permute-start | bytes 3080 | tf_op jit(solution)/shard_map/ppermute | solution.py:565
  26.1 1.3 %collective-permute-done.10 = f32[1,256]{1,0:T(1,128)S(1)} collective-permute-done((f32[1,256]{1,0:T(1,128)S(1)}, f32[1,256]{1,0:T(1,128)S(1)}, u32[]{:S(2)}, u32[]{:S(2)}) %collective-permute-start.10) | collective-permute-done | bytes 1056 | tf_op jit(solution)/shard_map/ppermute | solution.py:565
  27.4 0.0 collective-permute-done.8.o
  27.4 2.7 %collective-permute-start.11 = (f32[1,256]{1,0:T(1,128)S(1)}, f32[1,256]{1,0:T(1,128)S(1)}, u32[]{:S(2)}, u32[]{:S(2)}) collective-permute-start(f32[1,256]{1,0:T(1,128)S(1)} %add.23), channel_id=1, source_target_pairs={{0,18},{1,19},{2,16},{3,17},{4,22},{5,23},{6,20},{7,21},{8,26},{9,... | collective-permute-start | bytes 3080 | tf_op jit(solution)/shard_map/ppermute | solution.py:565
  30.1 0.0 copy-done.1
  30.1 2.6 %shard_map.87 = (f32[19,2,16,256]{3,2,1,0:T(8,128)}, f32[19,2,16,256]{3,2,1,0:T(8,128)}, f32[2,16,256]{2,1,0:T(8,128)}) custom-call(s32[1]{0:T(128)} %bitcast.parity_ref, s32[1]{0:T(128)} %bitcast.1.real_ref, f32[19,2,16,256]{3,2,1,0:T(8,128)S(1)} %get-tuple-element.34.post, f32[19,2,16,256]{3,2,1,0:T(8,128)S(1)} %get-tuple-element.35.adj, ...), custom_call_target="tpu_custom_call" | custom-call | tf_op jit(solution)/shard_map/pallas_call | solution.py:497
  32.7 0.0 collective-permute-done.11
  32.7 0.5 %fusion = f32[8]{0:T(128)} fusion(f32[1,256]{1,0:T(1,128)S(1)} %collective-permute-done.11, f32[1,256]{1,0:T(1,128)S(1)} %add.23), kind=kLoop, calls=%fused_computation.2 | loop fusion | flops 8 | bytes 96 | tf_op jit(solution)/shard_map/squeeze | solution.py:639
  (5 shorter events, 0.0 us)
Async XLA Ops:
  0.6 11.7 %copy-start = (f32[19,2,16,256]{3,2,1,0:T(8,128)S(1)}, f32[19,2,16,256]{3,2,1,0:T(8,128)}, u32[]{:S(2)}) copy-start(f32[19,2,16,256]{3,2,1,0:T(8,128)} %seed.1) | copy-start | bytes 1867780
  0.7 11.7 %copy-start.2 = (f32[2,16,256]{2,1,0:T(8,128)S(1)}, f32[2,16,256]{2,1,0:T(8,128)}, u32[]{:S(2)}) copy-start(f32[2,16,256]{2,1,0:T(8,128)} %porous.3) | copy-start | bytes 98308
  0.7 11.7 %copy-start.3 = (s32[2,16,256]{2,1,0:T(8,128)S(1)}, s32[2,16,256]{2,1,0:T(8,128)}, u32[]{:S(2)}) copy-start(s32[2,16,256]{2,1,0:T(8,128)} %types.3) | copy-start | bytes 98308
  0.7 11.7 %copy-start.4 = (s32[2,16,256]{2,1,0:T(8,128)S(1)}, s32[2,16,256]{2,1,0:T(8,128)}, u32[]{:S(2)}) copy-start(s32[2,16,256]{2,1,0:T(8,128)} %regions.3) | copy-start | bytes 98308
  2.7 9.7 %collective-permute-start = (f32[248,256]{1,0:T(8,128)S(1)}, f32[248,256]{1,0:T(8,128)S(1)}, u32[]{:S(2)}, u32[]{:S(2)}) collective-permute-start(f32[248,256]{1,0:T(8,128)S(1)} %get-tuple-element.29), channel_id=1, source_target_pairs={{0,2},{1,3},{2,0},{3,1},{4,6},{5,7},{6,4},{7,5},{8,10},{9,11},{10,... | collective-permute-start | bytes 761864 | tf_op jit(solution)/shard_map/ppermute | solution.py:547
  3.2 9.1 %collective-permute-start.1 = (f32[248,256]{1,0:T(8,128)S(1)}, f32[248,256]{1,0:T(8,128)S(1)}, u32[]{:S(2)}, u32[]{:S(2)}) collective-permute-start(f32[248,256]{1,0:T(8,128)S(1)} %get-tuple-element.30), channel_id=1, source_target_pairs={{0,1},{1,0},{2,4},{3,5},{4,2},{5,3},{6,8},{7,9},{8,6},{9,7},{10,12... | collective-permute-start | bytes 761864 | tf_op jit(solution)/shard_map/ppermute | solution.py:547
  5.8 6.5 %collective-permute-start.2 = (f32[9,8,256]{2,1,0:T(8,128)S(1)}, f32[9,8,256]{2,1,0:T(8,128)S(1)}, u32[]{:S(2)}, u32[]{:S(2)}) collective-permute-start(f32[9,8,256]{2,1,0:T(8,128)S(1)} %get-tuple-element.31), channel_id=1, source_target_pairs={{0,1},{1,0},{2,3},{3,2},{4,5},{5,4},{6,7},{7,6},{8,9},{9,8},{10,11... | collective-permute-start | bytes 221192 | tf_op jit(solution)/shard_map/ppermute | solution.py:541
  5.8 5.8 %collective-permute-start.3 = (f32[2,8,256]{2,1,0:T(8,128)S(1)}, f32[2,8,256]{2,1,0:T(8,128)S(1)}, u32[]{:S(2)}, u32[]{:S(2)}) collective-permute-start(f32[2,8,256]{2,1,0:T(8,128)S(1)} %get-tuple-element.32), channel_id=1, source_target_pairs={{0,3},{1,2},{2,1},{3,0},{4,7},{5,6},{6,5},{7,4},{8,11},{9,10},{10,... | collective-permute-start | bytes 49160 | tf_op jit(solution)/shard_map/ppermute | solution.py:552
  7.2 5.1 %collective-permute-start.4 = (f32[2,8,256]{2,1,0:T(8,128)S(1)}, f32[2,8,256]{2,1,0:T(8,128)S(1)}, u32[]{:S(2)}, u32[]{:S(2)}) collective-permute-start(f32[2,8,256]{2,1,0:T(8,128)S(1)} %get-tuple-element.33), channel_id=1, source_target_pairs={{0,1},{1,0},{2,5},{3,4},{4,3},{5,2},{6,9},{7,8},{8,7},{9,6},{10,13... | collective-permute-start | bytes 49160 | tf_op jit(solution)/shard_map/ppermute | solution.py:552
  12.4 17.8 %copy-start.1 = (f32[19,2,16,256]{3,2,1,0:T(8,128)S(1)}, f32[19,2,16,256]{3,2,1,0:T(8,128)}, u32[]{:S(2)}) copy-start(f32[19,2,16,256]{3,2,1,0:T(8,128)} %pops.1) | copy-start | bytes 1867780
  14.1 5.1 %collective-permute-start.5 = (f32[6,8,256]{2,1,0:T(8,128)S(1)}, f32[6,8,256]{2,1,0:T(8,128)S(1)}, u32[]{:S(2)}, u32[]{:S(2)}) collective-permute-start(f32[6,8,256]{2,1,0:T(8,128)S(1)} %get-tuple-element.40), channel_id=1, source_target_pairs={{0,1},{1,0},{2,3},{3,2},{4,5},{5,4},{6,7},{7,6},{8,9},{9,8},{10,11... | collective-permute-start | bytes 147464 | tf_op jit(solution)/shard_map/ppermute | solution.py:541
  16.2 3.0 %collective-permute-start.6 = (f32[1,256]{1,0:T(1,128)S(1)}, f32[1,256]{1,0:T(1,128)S(1)}, u32[]{:S(2)}, u32[]{:S(2)}) collective-permute-start(f32[1,256]{1,0:T(1,128)S(1)} %get-tuple-element.41), channel_id=1, source_target_pairs={{0,6},{1,7},{2,4},{3,5},{4,2},{5,3},{6,0},{7,1},{8,14},{9,15},{10,... | collective-permute-start | bytes 3080 | tf_op jit(solution)/shard_map/ppermute | solution.py:565
  19.2 1.6 %collective-permute-start.7 = (f32[176,256]{1,0:T(8,128)S(1)}, f32[176,256]{1,0:T(8,128)S(1)}, u32[]{:S(2)}, u32[]{:S(2)}) collective-permute-start(f32[176,256]{1,0:T(8,128)S(1)} %get-tuple-element.42), channel_id=1, source_target_pairs={{0,2},{1,3},{2,0},{3,1},{4,6},{5,7},{6,4},{7,5},{8,10},{9,11},{10,... | collective-permute-start | bytes 540680 | tf_op jit(solution)/shard_map/ppermute | solution.py:547
  19.4 8.0 %collective-permute-start.8 = (f32[176,256]{1,0:T(8,128)S(1)}, f32[176,256]{1,0:T(8,128)S(1)}, u32[]{:S(2)}, u32[]{:S(2)}) collective-permute-start(f32[176,256]{1,0:T(8,128)S(1)} %get-tuple-element.43), channel_id=1, source_target_pairs={{0,1},{1,0},{2,4},{3,5},{4,2},{5,3},{6,8},{7,9},{8,6},{9,7},{10,12... | collective-permute-start | bytes 540680 | tf_op jit(solution)/shard_map/ppermute | solution.py:547
  20.8 3.0 %collective-permute-start.9 = (f32[1,256]{1,0:T(1,128)S(1)}, f32[1,256]{1,0:T(1,128)S(1)}, u32[]{:S(2)}, u32[]{:S(2)}) collective-permute-start(f32[1,256]{1,0:T(1,128)S(1)} %slice_add_fusion), channel_id=1, source_target_pairs={{0,3},{1,2},{2,1},{3,0},{4,7},{5,6},{6,5},{7,4},{8,11},{9,10},{10,... | collective-permute-start | bytes 3080 | tf_op jit(solution)/shard_map/ppermute | solution.py:565
  23.9 3.5 %collective-permute-start.10 = (f32[1,256]{1,0:T(1,128)S(1)}, f32[1,256]{1,0:T(1,128)S(1)}, u32[]{:S(2)}, u32[]{:S(2)}) collective-permute-start(f32[1,256]{1,0:T(1,128)S(1)} %add.22), channel_id=1, source_target_pairs={{0,10},{1,11},{2,8},{3,9},{4,14},{5,15},{6,12},{7,13},{8,2},{9,3},... | collective-permute-start | bytes 3080 | tf_op jit(solution)/shard_map/ppermute | solution.py:565
  27.4 5.3 %collective-permute-start.11 = (f32[1,256]{1,0:T(1,128)S(1)}, f32[1,256]{1,0:T(1,128)S(1)}, u32[]{:S(2)}, u32[]{:S(2)}) collective-permute-start(f32[1,256]{1,0:T(1,128)S(1)} %add.23), channel_id=1, source_target_pairs={{0,18},{1,19},{2,16},{3,17},{4,22},{5,23},{6,20},{7,21},{8,26},{9,... | collective-permute-start | bytes 3080 | tf_op jit(solution)/shard_map/ppermute | solution.py:565

commit v5 on v4

--- a/solution.py
+++ b/solution.py
@@ -208,13 +208,21 @@
     return slice(16 * slot, 16 * slot + 16)
 
 
+def by_parity(parity_ref, body):
+    for parity in (0, 1):
+        pl.when(parity_ref[0] == parity)(functools.partial(body, parity))
+
+
+def near_rows(parity, rows_a):
+    return (range(1, rows_a), 0) if parity == 0 else (range(rows_a - 1), rows_a - 1)
+
+
 class Fields:
-    def __init__(self, layout, own, parity, real, e, o, t, ed=None, od=None):
-        self.layout, self.own = layout, own
-        self.e, self.o, self.t, self.ed, self.od = e, o, t, ed, od
-        self.up_e = parity == 0
-        self.o_real = real == 1
+    def __init__(self, layout, own, parity, e=None, o=None, real=None, t=None, ed=None, od=None):
+        self.layout, self.own, self.t = layout, own, t
         self.rows_a = own[POST].shape[1]
+        sides = [(o, od, real), (e, ed, None)]
+        self.sides = sides if parity == 0 else sides[::-1]
 
     def row(self, kind, q, a):
         if 0 <= a < self.rows_a:
@@ -222,29 +230,28 @@
         if kind == FACTOR:
             weight, *velocity = (self.row(MOTION, k, a) for k in range(4))
             return porosity_factor(q, weight, velocity)
-        rows = face_rows(self.layout.slot[HI if a < 0 else LO][(kind, q)])
-        return self.beyond(kind, a, self.e[rows, :], self.o[rows, :])
+        message, _, real = self.sides[a >= 0]
+        slot = self.layout.slot[HI if a < 0 else LO][(kind, q)]
+        return self.masked(kind, message[face_rows(slot), :], real)
+
+    def masked(self, kind, value, real):
+        if real is None or kind not in (ADJ, FLAG):
+            return value
+        return jnp.where(real == 1, value, 0.0)
 
     def row_label(self, a):
-        row = slice(16 * self.layout.fields, 16 * self.layout.fields + 1)
-        return self.beyond(None, a, self.e[row, :], self.o[row, :])
-
-    def beyond(self, kind, a, e, o):
-        if kind in (ADJ, FLAG):
-            o = jnp.where(self.o_real, o, 0.0)
-        return jnp.where(self.up_e, o, e) if a < 0 else jnp.where(self.up_e, e, o)
+        row = 16 * self.layout.fields
+        return self.sides[a >= 0][0][row : row + 1, :]
 
     def message(self, key, a):
         block, i = self.layout.place[key]
         if 0 <= a < self.rows_a:
             return self.t[block, i : i + 1, :]
-        if self.ed is None:
+        axial, corners, real = self.sides[a >= 0]
+        if corners is None:
             row = 16 * self.layout.fields + 8 * block + i
-            e, o = self.e[row : row + 1, :], self.o[row : row + 1, :]
-        else:
-            block = max(block - 1, 0)
-            e, o = self.ed[block, i : i + 1, :], self.od[block, i : i + 1, :]
-        return self.beyond(key[1], a, e, o)
+            return self.masked(key[1], axial[row : row + 1, :], real)
+        return self.masked(key[1], corners[max(block - 1, 0), i : i + 1, :], real)
 
     def edge(self, side, kind, q, a):
         row = self.rows_a - 1 if a < 0 else 0 if a >= self.rows_a else a
@@ -268,6 +275,23 @@
     return own[FLAG].at[a] if kind == FLAG else own[kind].at[q, a]
 
 
+def stream_row(fields, a, around, result):
+    post = fields.own[POST]
+    result[0, a] = post[0, a]
+    for q in range(1, 19):
+        moved = fields.moved(POST, q, a, tuple(-c for c in VELOCITY[q]))
+        result[q, a] = jnp.where(around[q - 1, a] > 0, moved, post[OPPOSITE[q], a])
+
+
+def stream_adjoint_row(fields, a, centre, around, result):
+    adj = fields.own[ADJ]
+    result[0, a] = adj[0, a]
+    for q in range(1, 19):
+        opp = OPPOSITE[q]
+        ahead = centre * fields.moved(ADJ, opp, a, tuple(-c for c in VELOCITY[q]))
+        result[opp, a] = ahead + (1.0 - around[q - 1, a]) * adj[q, a]
+
+
 def pack_azimuthal(layout, own, t_ref):
     rows_t = own[POST].shape[2]
     for key, (block, i) in layout.place.items():
@@ -279,12 +303,10 @@
 
 def pack_axial(layout, own, parity, e_ref, o_ref):
     rows_a = own[POST].shape[1]
-    even = parity == 0
+    low_ref, high_ref = (o_ref, e_ref) if parity == 0 else (e_ref, o_ref)
     for slot in range(layout.fields):
-        low = cells(own, *layout.ax[LO][slot], 0)[...]
-        high = cells(own, *layout.ax[HI][slot], rows_a - 1)[...]
-        e_ref[face_rows(slot), :] = jnp.where(even, high, low)
-        o_ref[face_rows(slot), :] = jnp.where(even, low, high)
+        low_ref[face_rows(slot), :] = cells(own, *layout.ax[LO][slot], 0)[...]
+        high_ref[face_rows(slot), :] = cells(own, *layout.ax[HI][slot], rows_a - 1)[...]
 
 
 def chunks(rows_a, shape, body):
@@ -373,33 +395,26 @@
         chunks([a], porous.shape, body)
     loads[-1].wait()
     own = {POST: post, ADJ: seed, FACTOR: factors, MOTION: motion, FLAG: flags}
-    even = parity_ref[0] == 0
-    pack_axial(FIRST, own, parity_ref[0], e_out, o_out)
     pack_azimuthal(FIRST, own, t_out)
-    ed_out[0] = jnp.where(even, t_out[0], t_out[1])
-    od_out[0] = jnp.where(even, t_out[1], t_out[0])
-    for out in (ed_out, od_out):
-        out[1] = t_out[2]
-
-
-def second_kernel(
-    parity_ref, real_ref, post, seed, factors, flags, porous, types, regions, e, o, t, ed, od,
-    post_next, adj, sens, around, e_out, o_out, t_out, partial, state, back, parts,
-):
-    own = {POST: post, ADJ: seed, FACTOR: factors, FLAG: flags}
-    fields = Fields(FIRST, own, parity_ref[0], real_ref[0], e, o, t, ed, od)
-    rows_a, rows_t, rows_r = porous.shape
-    for a in range(rows_a):
-        centre = flags[a]
-        state[0, a] = post[0, a]
-        back[0, a] = seed[0, a]
+
+    def run(parity):
+        pack_axial(FIRST, own, parity, e_out, o_out)
+        for out, block in ((ed_out, parity), (od_out, 1 - parity)):
+            out[0] = t_out[block]
+            out[1] = t_out[2]
+
+    by_parity(parity_ref, run)
+
+
+def second_rows(fields, rows, cell_refs, results, scratch):
+    porous, types, regions = cell_refs
+    post_next, adj, sens, around = results
+    state, back = scratch
+    for a in rows:
         for q in range(1, 19):
-            behind = tuple(-c for c in VELOCITY[q])
-            open_ = fields.moved(FLAG, 0, a, behind)
-            around[q - 1, a] = open_
-            opp = OPPOSITE[q]
-            state[q, a] = jnp.where(open_ > 0, fields.moved(POST, q, a, behind), post[opp, a])
-            back[opp, a] = centre * fields.moved(ADJ, opp, a, behind) + (1.0 - open_) * seed[q, a]
+            around[q - 1, a] = fields.moved(FLAG, 0, a, tuple(-c for c in VELOCITY[q]))
+        stream_row(fields, a, around, state)
+        stream_adjoint_row(fields, a, fields.own[FLAG][a], around, back)
 
     def body(where):
         values = load(state, where)
@@ -409,9 +424,44 @@
         store(adj, where, result)
         sens[where] = partial_sens
 
-    chunks(range(rows_a), porous.shape, body)
-    pack_axial(SECOND, {POST: post_next, ADJ: adj}, parity_ref[0], e_out, o_out)
-    pack_azimuthal(SECOND, {POST: post_next, ADJ: adj}, t_out)
+    chunks(rows, porous.shape, body)
+
+
+def second_near_kernel(
+    parity_ref, post, seed, flags, porous, types, regions, e, t, ed,
+    post_next, adj, sens, around, state, back,
+):
+    def run(parity):
+        own = {POST: post, ADJ: seed, FLAG: flags}
+        fields = Fields(FIRST, own, parity, e=e, t=t, ed=ed)
+        rows, _ = near_rows(parity, porous.shape[0])
+        results = (post_next, adj, sens, around)
+        second_rows(fields, rows, (porous, types, regions), results, (state, back))
+
+    by_parity(parity_ref, run)
+
+
+def second_far_kernel(
+    parity_ref, real_ref, post_near, adj_near, sens_near, around_near,
+    post, seed, factors, flags, porous, types, regions, e, o, t, ed, od,
+    post_next, adj, sens, around, e_out, o_out, t_out, partial, state, back, parts,
+):
+    def run(parity):
+        own = {POST: post, ADJ: seed, FACTOR: factors, FLAG: flags}
+        fields = Fields(FIRST, own, parity, e, o, real_ref[0], t, ed, od)
+        _, row = near_rows(parity, porous.shape[0])
+        results = (post_next, adj, sens, around)
+        second_rows(fields, [row], (porous, types, regions), results, (state, back))
+        pack_axial(SECOND, {POST: post_next, ADJ: adj}, parity, e_out, o_out)
+        pack_azimuthal(SECOND, {POST: post_next, ADJ: adj}, t_out)
+        region_sums(fields, adj, sens, around, regions, parts, partial)
+
+    by_parity(parity_ref, run)
+
+
+def region_sums(fields, adj, sens, around, regions, parts, partial):
+    factors = fields.own[FACTOR]
+    rows_a, rows_t, rows_r = sens.shape
     sums = {(i, st): [] for i in (-1, 0, 1) for st in (-1, 0, 1)}
     for a in range(rows_a):
         sums[(0, 0)] += [sens[a], factors[0, a] * adj[0, a]]
@@ -452,20 +502,14 @@
         corners[8 * block + i : 8 * block + i + 1, :] = total[...]
 
 
-def third_kernel(
-    parity_ref, real_ref, post, adj, flags, around, pops, porous, types, regions, sens_one, e, o, t,
-    final_hbm, result_hbm, sens, final, result, back, sems,
-):
-    fields = Fields(SECOND, {POST: post, ADJ: adj}, parity_ref[0], real_ref[0], e, o, t)
-    rows_a = porous.shape[0]
+def third_rows(fields, rows, cell_refs, own_refs, hbm, sens, scratch, sems):
+    porous, types, regions = cell_refs
+    around, flags, pops, sens_one = own_refs
+    final, result, back = scratch
     stores = []
-    for a in range(rows_a):
-        final[0, a] = post[0, a]
-        for q in range(1, 19):
-            behind = tuple(-c for c in VELOCITY[q])
-            moved = fields.moved(POST, q, a, behind)
-            final[q, a] = jnp.where(around[q - 1, a] > 0, moved, post[OPPOSITE[q], a])
-        stores.append(pltpu.make_async_copy(final.at[:, a], final_hbm.at[:, a], sems.at[a]))
+
+    def send(source, target, a):
+        stores.append(pltpu.make_async_copy(source.at[:, a], target.at[:, a], sems.at[len(stores)]))
         stores[-1].start()
 
     def body(where):
@@ -475,19 +519,47 @@
         store(result, where, adjoint)
         sens[where] = partial_sens + sens_one[where]
 
-    for a in range(rows_a):
-        centre = flags[a]
-        back[0, a] = adj[0, a]
-        for q in range(1, 19):
-            behind = tuple(-c for c in VELOCITY[q])
-            opp = OPPOSITE[q]
-            ahead = centre * fields.moved(ADJ, opp, a, behind)
-            back[opp, a] = ahead + (1.0 - around[q - 1, a]) * adj[q, a]
+    for a in rows:
+        stream_row(fields, a, around, final)
+        send(final, hbm[0], a)
+        stream_adjoint_row(fields, a, flags[a], around, back)
         chunks([a], porous.shape, body)
-        stores.append(pltpu.make_async_copy(result.at[:, a], result_hbm.at[:, a], sems.at[rows_a + a]))
-        stores[-1].start()
+        send(result, hbm[1], a)
     for copy in stores:
         copy.wait()
+
+
+def third_near_kernel(
+    parity_ref, post, adj, flags, around, pops, porous, types, regions, sens_one, e, t,
+    final_hbm, result_hbm, sens, final, result, back, sems,
+):
+    def run(parity):
+        fields = Fields(SECOND, {POST: post, ADJ: adj}, parity, e=e, t=t)
+        rows, _ = near_rows(parity, porous.shape[0])
+        third_rows(
+            fields, rows, (porous, types, regions), (around, flags, pops, sens_one),
+            (final_hbm, result_hbm), sens, (final, result, back), sems,
+        )
+
+    by_parity(parity_ref, run)
+
+
+def third_far_kernel(
+    parity_ref, real_ref, final_near, result_near, sens_near,
+    post, adj, flags, around, pops, porous, types, regions, sens_one, o, t,
+    final_hbm, result_hbm, sens, final, result, back, sems,
+):
+    def run(parity):
+        fields = Fields(SECOND, {POST: post, ADJ: adj}, parity, o=o, real=real_ref[0], t=t)
+        rows, row = near_rows(parity, porous.shape[0])
+        for a in rows:
+            sens[a] = sens_near[a]
+        third_rows(
+            fields, [row], (porous, types, regions), (around, flags, pops, sens_one),
+            (final_hbm, result_hbm), sens, (final, result, back), sems,
+        )
+
+    by_parity(parity_ref, run)
 
 
 VMEM, HBM = pltpu.VMEM, pltpu.HBM
@@ -576,7 +648,7 @@
     place = ((index % 2).astype(i32).reshape(1), real.astype(i32).reshape(1))
 
     def axial(layout, more):
-        return [((16 * layout.fields + more, wide), f32, VMEM)] * 2
+        return ((16 * layout.fields + more, wide), f32, VMEM)
 
     def azimuthal(layout):
         return [((layout.blocks, 8, wide), f32, VMEM)]
@@ -585,7 +657,7 @@
     post, factors, e, o, t, ed, od, flags = call(
         first_kernel,
         [pltpu.SMEM] + [HBM] * 5,
-        [(pops, f32, VMEM), (pops, f32, VMEM)] + axial(FIRST, 8) + azimuthal(FIRST)
+        [(pops, f32, VMEM), (pops, f32, VMEM)] + [axial(FIRST, 8)] * 2 + azimuthal(FIRST)
         + [((2, 8, wide), f32, VMEM)] * 2 + [(cells_, f32, VMEM)],
         [VMEM(x.shape, x.dtype) for x in inputs]
         + [VMEM((4,) + cells_, f32), pltpu.SemaphoreType.DMA((4 + cells_[0],))],
@@ -595,13 +667,22 @@
     e, o = send_axial(e, 0), send_axial(o, 1)
     t_near = send_azimuthal(FIRST, t)
     ed, od = send_diagonal(ed, 0), send_diagonal(od, 1)
+    layers = [(pops, f32, VMEM), (pops, f32, VMEM), (cells_, f32, VMEM), ((18,) + cells_, f32, VMEM)]
+    inside = (flags, porosity, cell_type, region)
+    near = call(
+        second_near_kernel,
+        [pltpu.SMEM] + [VMEM] * 9,
+        layers,
+        [VMEM(pops, f32), VMEM(pops, f32)],
+        place[0], post, adjoint_seed, *inside, e, t_near, ed,
+    )
     post, adj, sens_one, around, e, o, t, total = call(
-        second_kernel,
-        [pltpu.SMEM] * 2 + [VMEM] * 12,
-        [(pops, f32, VMEM), (pops, f32, VMEM), (cells_, f32, VMEM), ((18,) + cells_, f32, VMEM)]
-        + axial(SECOND, 16) + azimuthal(SECOND) + [((1, wide), f32, VMEM)],
+        second_far_kernel,
+        [pltpu.SMEM] * 2 + [VMEM] * 16,
+        layers + [axial(SECOND, 16)] * 2 + azimuthal(SECOND) + [((1, wide), f32, VMEM)],
         [VMEM(pops, f32), VMEM(pops, f32), VMEM((2, 16, wide), f32)],
-        *place, post, adjoint_seed, factors, flags, porosity, cell_type, region, e, o, t_near, ed, od,
+        *place, *near, post, adjoint_seed, factors, *inside, e, o, t_near, ed, od,
+        aliases={2: 0, 3: 1, 4: 2, 5: 3},
     )
     t_near = send_azimuthal(SECOND, t)
     block, i = SECOND.place[(LO, "sum")]
@@ -613,28 +694,38 @@
     e, o = call(
         corner_kernel,
         [VMEM] * 4,
-        axial(SECOND, 16),
+        [axial(SECOND, 16)] * 2,
         [],
         e, o, t_near, total,
         aliases={0: 0, 1: 1},
     )
     e, o = send_axial(e, 0), send_axial(o, 1)
+    stored = [(pops, f32, HBM), (pops, f32, HBM), (cells_, f32, VMEM)]
+    third_scratch = [VMEM(pops, f32)] * 3 + [pltpu.SemaphoreType.DMA((2 * cells_[0],))]
+    inside = (post, adj, flags, around, initial, porosity, cell_type, region, sens_one)
+    near = call(
+        third_near_kernel,
+        [pltpu.SMEM] + [VMEM] * 11,
+        stored,
+        third_scratch,
+        place[0], *inside, e, t_near,
+    )
     if halving:
         row = 16 * SECOND.fields + 8 * block + i
         totals = total + e[row : row + 1]
         for flip in flips:
             if flip == flips[-1]:
-                totals, _ = lax.optimization_barrier((totals, o))
+                totals, _ = lax.optimization_barrier((totals, (o, near[2])))
             totals = totals + from_partner(totals, *flip)
     else:
         totals = lax.psum(total, ("ax", "az"))
     final, adjoint, sensitivity = call(
-        third_kernel,
-        [pltpu.SMEM] * 2 + [VMEM] * 12,
-        [(pops, f32, HBM), (pops, f32, HBM), (cells_, f32, VMEM)],
-        [VMEM(pops, f32), VMEM(pops, f32), VMEM(pops, f32)]
-        + [pltpu.SemaphoreType.DMA((2 * cells_[0],))],
-        *place, post, adj, flags, around, initial, porosity, cell_type, region, sens_one, e, o, t_near,
+        third_far_kernel,
+        [pltpu.SMEM] * 2 + [HBM] * 2 + [VMEM] * 12,
+        stored,
+        third_scratch,
+        *place, *near, *inside, o, t_near,
+        aliases={2: 0, 3: 1},
     )
     return final, adjoint, sensitivity, totals[0, : size_a * size_t // 4]
 

time: 33.4 us -> 32.1 us (0.961)
  waiting for transfers between devices: 9.51 us -> 8.16 us
  Pallas kernels: 6.33 us -> 7.17 us
  starting transfers between devices: 16.1 us -> 15.3 us
    ppermute x4, waiting for transfers between devices: 5.91 us -> 4.88 us  [from_partner(): return lax.ppermute(x, ('ax', 'az'), pairs)]
    pallas_call x4 -> x6, Pallas kernels: 6.33 us -> 7.17 us  [call(): pl.pallas_call(body, out_shape=[jax.ShapeDtypeStruct(shape, dtype) for sh...]
    ppermute x4, starting transfers between devices: 6.37 us -> 5.71 us  [from_partner(): return lax.ppermute(x, ('ax', 'az'), pairs)]
    ppermute x2, waiting for transfers between devices: 3.59 us -> 2.95 us  [send(): return lax.ppermute(x, ('ax', 'az'), axial_pairs(flip, shift))]
    ppermute x4, starting transfers between devices: 4.72 us -> 4.39 us  [send_axial(): return lax.ppermute(message, ('ax', 'az'), axial_pairs(flip))]
  transfers between devices with their start and end apart: 12 -> 12, of which waited for: 5 -> 5; matrix products, arithmetic and copies ran while one was open for 0% -> 0% of each run, Pallas kernels for 8% -> 13%
where the time goes in v5:
time: 32.1 us; the launch traced here: 32 us
  starting transfers between devices  15.3 us (48%)
  waiting for transfers between devices  8.16 us (25%)
  Pallas kernels  7.17 us (22%)
  between operations  0.8 us (2%)
  other arithmetic  0.53 us (2%)
    pallas_call x6, Pallas kernels, call(): pl.pallas_call(body, out_shape=[jax.ShapeDtypeStruct(shape, dtype) for sh...  7.17 us
    ppermute x4, starting transfers between devices, from_partner(): return lax.ppermute(x, ('ax', 'az'), pairs)  5.71 us
    ppermute x4, waiting for transfers between devices, from_partner(): return lax.ppermute(x, ('ax', 'az'), pairs)  4.88 us
    ppermute x4, starting transfers between devices, send_axial(): return lax.ppermute(message, ('ax', 'az'), axial_pairs(flip))  4.39 us
    ppermute x2, waiting for transfers between devices, send(): return lax.ppermute(x, ('ax', 'az'), axial_pairs(flip, shift))  2.95 us
    ppermute x2, starting transfers between devices, send(): return lax.ppermute(x, ('ax', 'az'), axial_pairs(flip, shift))  2.88 us
    ppermute x2, starting transfers between devices, send(): return lax.ppermute(x, 'az', [(i, (i + shift) % size) for i in range(size)])  2.31 us
  transfers between devices with their start and end apart: 12, of which 5 were waited for; matrix products, arithmetic and copies ran while one was open for 0% of the time, Pallas kernels for 13%

profile of v5, /device:TPU:0, one launch (start us, length us, event | category | flops | bytes accessed | tf_op | source)
XLA Modules:
  0.0 32.0 jit_solution(6963025146288708850)
XLA Ops:
  0.6 0.0 copy-start
  0.7 0.0 copy-start.2
  0.7 0.0 copy-start.3
  0.7 0.0 copy-start.4
  0.7 2.0 %shard_map.84 = (f32[19,2,16,256]{3,2,1,0:T(8,128)S(1)}, f32[19,2,16,256]{3,2,1,0:T(8,128)S(1)}, f32[248,256]{1,0:T(8,128)S(1)}, f32[248,256]{1,0:T(8,128)S(1)},...) custom-call(s32[1]{0:T(128)} %bitcast.parity_ref, ...), custom_call_target="tpu_custom_call" | custom-call | tf_op jit(solution)/shard_map/pallas_call | solution.py:569
  2.7 0.5 %collective-permute-start = (f32[248,256]{1,0:T(8,128)S(1)}, f32[248,256]{1,0:T(8,128)S(1)}, u32[]{:S(2)}, u32[]{:S(2)}) collective-permute-start(f32[248,256]{1,0:T(8,128)S(1)} %get-tuple-element.35), channel_id=1, source_target_pairs={{0,2},{1,3},{2,0},{3,1},{4,6},{5,7},{6,4},{7,5},{8,10},{9,11},{10,... | collective-permute-start | bytes 761864 | tf_op jit(solution)/shard_map/ppermute | solution.py:619
  3.2 2.6 %collective-permute-start.3 = (f32[248,256]{1,0:T(8,128)S(1)}, f32[248,256]{1,0:T(8,128)S(1)}, u32[]{:S(2)}, u32[]{:S(2)}) collective-permute-start(f32[248,256]{1,0:T(8,128)S(1)} %get-tuple-element.43), channel_id=1, source_target_pairs={{0,1},{1,0},{2,4},{3,5},{4,2},{5,3},{6,8},{7,9},{8,6},{9,7},{10,12... | collective-permute-start | bytes 761864 | tf_op jit(solution)/shard_map/ppermute | solution.py:619
  5.8 0.1 collective-permute-start.1
  5.8 1.4 %collective-permute-start.2 = (f32[2,8,256]{2,1,0:T(8,128)S(1)}, f32[2,8,256]{2,1,0:T(8,128)S(1)}, u32[]{:S(2)}, u32[]{:S(2)}) collective-permute-start(f32[2,8,256]{2,1,0:T(8,128)S(1)} %get-tuple-element.37), channel_id=1, source_target_pairs={{0,3},{1,2},{2,1},{3,0},{4,7},{5,6},{6,5},{7,4},{8,11},{9,10},{10,... | collective-permute-start | bytes 49160 | tf_op jit(solution)/shard_map/ppermute | solution.py:624
  7.2 1.5 %collective-permute-start.4 = (f32[2,8,256]{2,1,0:T(8,128)S(1)}, f32[2,8,256]{2,1,0:T(8,128)S(1)}, u32[]{:S(2)}, u32[]{:S(2)}) collective-permute-start(f32[2,8,256]{2,1,0:T(8,128)S(1)} %get-tuple-element.44), channel_id=1, source_target_pairs={{0,1},{1,0},{2,5},{3,4},{4,3},{5,2},{6,9},{7,8},{8,7},{9,6},{10,13... | collective-permute-start | bytes 49160 | tf_op jit(solution)/shard_map/ppermute | solution.py:624
  8.7 3.0 %collective-permute-done.2.ed = f32[2,8,256]{2,1,0:T(8,128)S(1)} collective-permute-done((f32[2,8,256]{2,1,0:T(8,128)S(1)}, f32[2,8,256]{2,1,0:T(8,128)S(1)}, u32[]{:S(2)}, u32[]{:S(2)}) %collective-permute-start.2) | collective-permute-done | bytes 16416 | tf_op jit(solution)/shard_map/ppermute | solution.py:624
  11.7 0.1 collective-permute-done.1.t
  11.8 0.0 collective-permute-done.e
  11.8 0.0 copy-done
  11.8 0.0 copy-done.2
  11.8 0.0 copy-done.3
  11.8 0.0 copy-done.4
  11.8 0.7 %shard_map.85 = (f32[19,2,16,256]{3,2,1,0:T(8,128)S(1)}, f32[19,2,16,256]{3,2,1,0:T(8,128)S(1)}, f32[2,16,256]{2,1,0:T(8,128)S(1)}, f32[18,2,16,256]{3,2,1,0:T(8,128)S(1)}) custom-call(s32[1]{0:T(128)} %bitcast.parity_ref, f32[19,2,16,256]{3,2,1,0:T(8,128)S(1)} %get-tuple-element.33.post, f32[19,2,16,256]{3,2,1,0:T(8,128)S(1)} %copy-done, ...), custom_call_target="tpu_custom_call" | custom-call | tf_op jit(solution)/shard_map/pallas_call | solution.py:569
  12.5 0.0 collective-permute-done.4.od
  12.5 0.0 collective-permute-done.3.o
  12.6 0.0 copy-start.1
  12.6 1.2 %shard_map.86 = (f32[19,2,16,256]{3,2,1,0:T(8,128)S(1)}, f32[19,2,16,256]{3,2,1,0:T(8,128)S(1)}, f32[2,16,256]{2,1,0:T(8,128)S(1)}, f32[18,2,16,256]{3,2,1,0:T(8...) custom-call(s32[1]{0:T(128)} %bitcast.parity_ref, ...), custom_call_target="tpu_custom_call", output_to_operand_aliasing={{0}: (2, {}), {1}: (3, {}), {2}: (4, {}), {3}: (5, {})} | custom-call | tf_op jit(solution)/shard_map/pallas_call | solution.py:569
  13.8 2.2 %collective-permute-start.5 = (f32[6,8,256]{2,1,0:T(8,128)S(1)}, f32[6,8,256]{2,1,0:T(8,128)S(1)}, u32[]{:S(2)}, u32[]{:S(2)}) collective-permute-start(f32[6,8,256]{2,1,0:T(8,128)S(1)} %get-tuple-element.51), channel_id=1, source_target_pairs={{0,1},{1,0},{2,3},{3,2},{4,5},{5,4},{6,7},{7,6},{8,9},{9,8},{10,11... | collective-permute-start | bytes 147464 | tf_op jit(solution)/shard_map/ppermute | solution.py:613
  16.0 0.0 collective-permute-start.6
  16.0 3.0 %collective-permute-done.6 = f32[1,256]{1,0:T(1,128)S(1)} collective-permute-done((f32[1,256]{1,0:T(1,128)S(1)}, f32[1,256]{1,0:T(1,128)S(1)}, u32[]{:S(2)}, u32[]{:S(2)}) %collective-permute-start.6) | collective-permute-done | bytes 1056 | tf_op jit(solution)/shard_map/ppermute | solution.py:637
  19.0 0.0 collective-permute-done.5.t
  19.0 0.2 collective-permute-start.7
  19.2 1.1 %collective-permute-start.8 = (f32[176,256]{1,0:T(8,128)S(1)}, f32[176,256]{1,0:T(8,128)S(1)}, u32[]{:S(2)}, u32[]{:S(2)}) collective-permute-start(f32[176,256]{1,0:T(8,128)S(1)} %get-tuple-element.57), channel_id=1, source_target_pairs={{0,1},{1,0},{2,4},{3,5},{4,2},{5,3},{6,8},{7,9},{8,6},{9,7},{10,12... | collective-permute-start | bytes 540680 | tf_op jit(solution)/shard_map/ppermute | solution.py:619
  20.3 0.2 collective-permute-done.7.e
  20.5 1.1 %collective-permute-start.9 = (f32[1,256]{1,0:T(1,128)S(1)}, f32[1,256]{1,0:T(1,128)S(1)}, u32[]{:S(2)}, u32[]{:S(2)}) collective-permute-start(f32[1,256]{1,0:T(1,128)S(1)} %slice_add_fusion), channel_id=1, source_target_pairs={{0,3},{1,2},{2,1},{3,0},{4,7},{5,6},{6,5},{7,4},{8,11},{9,10},{10,... | collective-permute-start | bytes 3080 | tf_op jit(solution)/shard_map/ppermute | solution.py:637
  21.6 1.9 %collective-permute-done.9 = f32[1,256]{1,0:T(1,128)S(1)} collective-permute-done((f32[1,256]{1,0:T(1,128)S(1)}, f32[1,256]{1,0:T(1,128)S(1)}, u32[]{:S(2)}, u32[]{:S(2)}) %collective-permute-start.9) | collective-permute-done | bytes 1056 | tf_op jit(solution)/shard_map/ppermute | solution.py:637
  23.5 2.0 %collective-permute-start.10 = (f32[1,256]{1,0:T(1,128)S(1)}, f32[1,256]{1,0:T(1,128)S(1)}, u32[]{:S(2)}, u32[]{:S(2)}) collective-permute-start(f32[1,256]{1,0:T(1,128)S(1)} %add.22), channel_id=1, source_target_pairs={{0,10},{1,11},{2,8},{3,9},{4,14},{5,15},{6,12},{7,13},{8,2},{9,3},... | collective-permute-start | bytes 3080 | tf_op jit(solution)/shard_map/ppermute | solution.py:637
  25.5 0.0 copy-done.1
  25.5 1.4 %shard_map.88 = (f32[19,2,16,256]{3,2,1,0:T(8,128)}, f32[19,2,16,256]{3,2,1,0:T(8,128)}, f32[2,16,256]{2,1,0:T(8,128)S(1)}) custom-call(s32[1]{0:T(128)} %bitcast.parity_ref, f32[19,2,16,256]{3,2,1,0:T(8,128)S(1)} %get-tuple-element.45.post, f32[19,2,16,256]{3,2,1,0:T(8,128)S(1)} %get-tuple-element.46.adj, f32[2,16,256]{2,1,0:T(8,128)S(1)} %get-tuple-element.34.flags, ...), custom_call_target="tpu_custom_call" | custom-call | tf_op jit(solution)/shard_map/pallas_call | solution.py:569
  26.8 0.0 collective-permute-done.10
  26.8 0.0 collective-permute-done.8.o
  26.8 2.6 %collective-permute-start.11 = (f32[1,256]{1,0:T(1,128)S(1)}, f32[1,256]{1,0:T(1,128)S(1)}, u32[]{:S(2)}, u32[]{:S(2)}) collective-permute-start(f32[1,256]{1,0:T(1,128)S(1)} %add.23), channel_id=1, source_target_pairs={{0,18},{1,19},{2,16},{3,17},{4,22},{5,23},{6,20},{7,21},{8,26},{9,... | collective-permute-start | bytes 3080 | tf_op jit(solution)/shard_map/ppermute | solution.py:637
  29.5 2.0 %shard_map.89 = (f32[19,2,16,256]{3,2,1,0:T(8,128)}, f32[19,2,16,256]{3,2,1,0:T(8,128)}, f32[2,16,256]{2,1,0:T(8,128)}) custom-call(s32[1]{0:T(128)} %bitcast.parity_ref, s32[1]{0:T(128)} %bitcast.1.real_ref, f32[19,2,16,256]{3,2,1,0:T(8,128)} %get-tuple-element.54.final_near, ...), custom_call_target="tpu_custom_call", output_to_operand_aliasing={{0}: (2, {}), {1}: (3, {})} | custom-call | tf_op jit(solution)/shard_map/pallas_call | solution.py:569
  31.4 0.0 collective-permute-done.11
  31.4 0.5 %fusion = f32[8]{0:T(128)} fusion(f32[1,256]{1,0:T(1,128)S(1)} %collective-permute-done.11, f32[1,256]{1,0:T(1,128)S(1)} %add.23), kind=kLoop, calls=%fused_computation.2 | loop fusion | flops 8 | bytes 96 | tf_op jit(solution)/shard_map/squeeze | solution.py:730
  (5 shorter events, 0.0 us)
Async XLA Ops:
  0.6 11.2 %copy-start = (f32[19,2,16,256]{3,2,1,0:T(8,128)S(1)}, f32[19,2,16,256]{3,2,1,0:T(8,128)}, u32[]{:S(2)}) copy-start(f32[19,2,16,256]{3,2,1,0:T(8,128)} %seed.3) | copy-start | bytes 1867780
  0.7 11.1 %copy-start.2 = (f32[2,16,256]{2,1,0:T(8,128)S(1)}, f32[2,16,256]{2,1,0:T(8,128)}, u32[]{:S(2)}) copy-start(f32[2,16,256]{2,1,0:T(8,128)} %porous.7) | copy-start | bytes 98308
  0.7 11.1 %copy-start.3 = (s32[2,16,256]{2,1,0:T(8,128)S(1)}, s32[2,16,256]{2,1,0:T(8,128)}, u32[]{:S(2)}) copy-start(s32[2,16,256]{2,1,0:T(8,128)} %types.7) | copy-start | bytes 98308
  0.7 11.1 %copy-start.4 = (s32[2,16,256]{2,1,0:T(8,128)S(1)}, s32[2,16,256]{2,1,0:T(8,128)}, u32[]{:S(2)}) copy-start(s32[2,16,256]{2,1,0:T(8,128)} %regions.7) | copy-start | bytes 98308
  2.7 9.1 %collective-permute-start = (f32[248,256]{1,0:T(8,128)S(1)}, f32[248,256]{1,0:T(8,128)S(1)}, u32[]{:S(2)}, u32[]{:S(2)}) collective-permute-start(f32[248,256]{1,0:T(8,128)S(1)} %get-tuple-element.35), channel_id=1, source_target_pairs={{0,2},{1,3},{2,0},{3,1},{4,6},{5,7},{6,4},{7,5},{8,10},{9,11},{10,... | collective-permute-start | bytes 761864 | tf_op jit(solution)/shard_map/ppermute | solution.py:619
  3.2 9.4 %collective-permute-start.3 = (f32[248,256]{1,0:T(8,128)S(1)}, f32[248,256]{1,0:T(8,128)S(1)}, u32[]{:S(2)}, u32[]{:S(2)}) collective-permute-start(f32[248,256]{1,0:T(8,128)S(1)} %get-tuple-element.43), channel_id=1, source_target_pairs={{0,1},{1,0},{2,4},{3,5},{4,2},{5,3},{6,8},{7,9},{8,6},{9,7},{10,12... | collective-permute-start | bytes 761864 | tf_op jit(solution)/shard_map/ppermute | solution.py:619
  5.8 6.0 %collective-permute-start.1 = (f32[9,8,256]{2,1,0:T(8,128)S(1)}, f32[9,8,256]{2,1,0:T(8,128)S(1)}, u32[]{:S(2)}, u32[]{:S(2)}) collective-permute-start(f32[9,8,256]{2,1,0:T(8,128)S(1)} %get-tuple-element.36), channel_id=1, source_target_pairs={{0,1},{1,0},{2,3},{3,2},{4,5},{5,4},{6,7},{7,6},{8,9},{9,8},{10,11... | collective-permute-start | bytes 221192 | tf_op jit(solution)/shard_map/ppermute | solution.py:613
  5.8 5.8 %collective-permute-start.2 = (f32[2,8,256]{2,1,0:T(8,128)S(1)}, f32[2,8,256]{2,1,0:T(8,128)S(1)}, u32[]{:S(2)}, u32[]{:S(2)}) collective-permute-start(f32[2,8,256]{2,1,0:T(8,128)S(1)} %get-tuple-element.37), channel_id=1, source_target_pairs={{0,3},{1,2},{2,1},{3,0},{4,7},{5,6},{6,5},{7,4},{8,11},{9,10},{10,... | collective-permute-start | bytes 49160 | tf_op jit(solution)/shard_map/ppermute | solution.py:624
  7.2 5.3 %collective-permute-start.4 = (f32[2,8,256]{2,1,0:T(8,128)S(1)}, f32[2,8,256]{2,1,0:T(8,128)S(1)}, u32[]{:S(2)}, u32[]{:S(2)}) collective-permute-start(f32[2,8,256]{2,1,0:T(8,128)S(1)} %get-tuple-element.44), channel_id=1, source_target_pairs={{0,1},{1,0},{2,5},{3,4},{4,3},{5,2},{6,9},{7,8},{8,7},{9,6},{10,13... | collective-permute-start | bytes 49160 | tf_op jit(solution)/shard_map/ppermute | solution.py:624
  12.6 12.9 %copy-start.1 = (f32[19,2,16,256]{3,2,1,0:T(8,128)S(1)}, f32[19,2,16,256]{3,2,1,0:T(8,128)}, u32[]{:S(2)}) copy-start(f32[19,2,16,256]{3,2,1,0:T(8,128)} %pops.3) | copy-start | bytes 1867780
  13.8 5.2 %collective-permute-start.5 = (f32[6,8,256]{2,1,0:T(8,128)S(1)}, f32[6,8,256]{2,1,0:T(8,128)S(1)}, u32[]{:S(2)}, u32[]{:S(2)}) collective-permute-start(f32[6,8,256]{2,1,0:T(8,128)S(1)} %get-tuple-element.51), channel_id=1, source_target_pairs={{0,1},{1,0},{2,3},{3,2},{4,5},{5,4},{6,7},{7,6},{8,9},{9,8},{10,11... | collective-permute-start | bytes 147464 | tf_op jit(solution)/shard_map/ppermute | solution.py:613
  16.0 3.0 %collective-permute-start.6 = (f32[1,256]{1,0:T(1,128)S(1)}, f32[1,256]{1,0:T(1,128)S(1)}, u32[]{:S(2)}, u32[]{:S(2)}) collective-permute-start(f32[1,256]{1,0:T(1,128)S(1)} %get-tuple-element.52), channel_id=1, source_target_pairs={{0,6},{1,7},{2,4},{3,5},{4,2},{5,3},{6,0},{7,1},{8,14},{9,15},{10,... | collective-permute-start | bytes 3080 | tf_op jit(solution)/shard_map/ppermute | solution.py:637
  19.0 1.5 %collective-permute-start.7 = (f32[176,256]{1,0:T(8,128)S(1)}, f32[176,256]{1,0:T(8,128)S(1)}, u32[]{:S(2)}, u32[]{:S(2)}) collective-permute-start(f32[176,256]{1,0:T(8,128)S(1)} %get-tuple-element.53), channel_id=1, source_target_pairs={{0,2},{1,3},{2,0},{3,1},{4,6},{5,7},{6,4},{7,5},{8,10},{9,11},{10,... | collective-permute-start | bytes 540680 | tf_op jit(solution)/shard_map/ppermute | solution.py:619
  19.2 7.7 %collective-permute-start.8 = (f32[176,256]{1,0:T(8,128)S(1)}, f32[176,256]{1,0:T(8,128)S(1)}, u32[]{:S(2)}, u32[]{:S(2)}) collective-permute-start(f32[176,256]{1,0:T(8,128)S(1)} %get-tuple-element.57), channel_id=1, source_target_pairs={{0,1},{1,0},{2,4},{3,5},{4,2},{5,3},{6,8},{7,9},{8,6},{9,7},{10,12... | collective-permute-start | bytes 540680 | tf_op jit(solution)/shard_map/ppermute | solution.py:619
  20.5 3.0 %collective-permute-start.9 = (f32[1,256]{1,0:T(1,128)S(1)}, f32[1,256]{1,0:T(1,128)S(1)}, u32[]{:S(2)}, u32[]{:S(2)}) collective-permute-start(f32[1,256]{1,0:T(1,128)S(1)} %slice_add_fusion), channel_id=1, source_target_pairs={{0,3},{1,2},{2,1},{3,0},{4,7},{5,6},{6,5},{7,4},{8,11},{9,10},{10,... | collective-permute-start | bytes 3080 | tf_op jit(solution)/shard_map/ppermute | solution.py:637
  23.5 3.3 %collective-permute-start.10 = (f32[1,256]{1,0:T(1,128)S(1)}, f32[1,256]{1,0:T(1,128)S(1)}, u32[]{:S(2)}, u32[]{:S(2)}) collective-permute-start(f32[1,256]{1,0:T(1,128)S(1)} %add.22), channel_id=1, source_target_pairs={{0,10},{1,11},{2,8},{3,9},{4,14},{5,15},{6,12},{7,13},{8,2},{9,3},... | collective-permute-start | bytes 3080 | tf_op jit(solution)/shard_map/ppermute | solution.py:637
  26.8 4.6 %collective-permute-start.11 = (f32[1,256]{1,0:T(1,128)S(1)}, f32[1,256]{1,0:T(1,128)S(1)}, u32[]{:S(2)}, u32[]{:S(2)}) collective-permute-start(f32[1,256]{1,0:T(1,128)S(1)} %add.23), channel_id=1, source_target_pairs={{0,18},{1,19},{2,16},{3,17},{4,22},{5,23},{6,20},{7,21},{8,26},{9,... | collective-permute-start | bytes 3080 | tf_op jit(solution)/shard_map/ppermute | solution.py:637

commit v6 on v5

--- a/solution.py
+++ b/solution.py
@@ -57,7 +57,7 @@
 
 
 class Layout:
-    def __init__(self, kinds, extra):
+    def __init__(self, kinds):
         self.ax = [face_fields(kinds, 0, side) for side in (LO, HI)]
         self.slot = [{key: i for i, key in enumerate(fields)} for fields in self.ax]
         self.fields = len(self.ax[LO])
@@ -68,15 +68,14 @@
                     leaves = VELOCITY[q][0] == (-sign if kind == ADJ else sign)
                     key = (side, kind, q, a)
                     (corner if kind == FLAG or leaves else rest).append(key)
-        corner += extra
         self.corner_blocks = -(-len(corner) // 8)
         self.blocks = self.corner_blocks + -(-len(rest) // 8)
         self.place = {key: (i // 8, i % 8) for i, key in enumerate(corner)}
         self.place.update({key: (self.corner_blocks + i // 8, i % 8) for i, key in enumerate(rest)})
 
 
-FIRST = Layout((POST, ADJ, FACTOR, FLAG), [(LO, "label"), (HI, "label")])
-SECOND = Layout((POST, ADJ), [(LO, "sum")])
+FIRST = Layout((POST, ADJ, FACTOR, FLAG))
+SECOND = Layout((POST, ADJ))
 
 
 def pairs_of(values):
@@ -240,8 +239,13 @@
         return jnp.where(real == 1, value, 0.0)
 
     def row_label(self, a):
-        row = 16 * self.layout.fields
-        return self.sides[a >= 0][0][row : row + 1, :]
+        row = 16 * self.layout.slot[HI if a < 0 else LO][(MOTION, 0)]
+        return self.sides[a >= 0][0][row : row + 1, 0:1]
+
+    def edge_label(self, side, a):
+        sa = 1 if a < 0 else -1 if a >= self.rows_a else 0
+        q = VELOCITY.index((sa, -1 if side == LO else 1, 0))
+        return self.edge(side, FACTOR, q, a)[:, 0:1]
 
     def message(self, key, a):
         block, i = self.layout.place[key]
@@ -251,7 +255,7 @@
         if corners is None:
             row = 16 * self.layout.fields + 8 * block + i
             return self.masked(key[1], axial[row : row + 1, :], real)
-        return self.masked(key[1], corners[max(block - 1, 0), i : i + 1, :], real)
+        return self.masked(key[1], corners[i : i + 1, :], real)
 
     def edge(self, side, kind, q, a):
         row = self.rows_a - 1 if a < 0 else 0 if a >= self.rows_a else a
@@ -292,21 +296,31 @@
         result[opp, a] = ahead + (1.0 - around[q - 1, a]) * adj[q, a]
 
 
-def pack_azimuthal(layout, own, t_ref):
+def labelled(value, label):
+    lanes = lax.broadcasted_iota(jnp.int32, value.shape, 1)
+    return jnp.where(lanes == 0, label, value)
+
+
+def pack_azimuthal(layout, own, rows, t_ref, label=None):
     rows_t = own[POST].shape[2]
-    for key, (block, i) in layout.place.items():
-        if len(key) == 4:
-            side, kind, q, a = key
+    for (side, kind, q, a), (block, i) in layout.place.items():
+        if a in rows:
             t = 0 if side == LO else rows_t - 1
-            t_ref[block, i : i + 1, :] = cells(own, kind, q, a)[t : t + 1, :]
-
-
-def pack_axial(layout, own, parity, e_ref, o_ref):
-    rows_a = own[POST].shape[1]
-    low_ref, high_ref = (o_ref, e_ref) if parity == 0 else (e_ref, o_ref)
-    for slot in range(layout.fields):
-        low_ref[face_rows(slot), :] = cells(own, *layout.ax[LO][slot], 0)[...]
-        high_ref[face_rows(slot), :] = cells(own, *layout.ax[HI][slot], rows_a - 1)[...]
+            row = cells(own, kind, q, a)[t : t + 1, :]
+            t_ref[block, i : i + 1, :] = labelled(row, label) if kind == FACTOR else row
+
+
+def pack_face(layout, own, side, message, label=None):
+    a = 0 if side == LO else own[POST].shape[1] - 1
+    for slot, (kind, q) in enumerate(layout.ax[side]):
+        value = cells(own, kind, q, a)[...]
+        if (kind, q) == (MOTION, 0):
+            value = labelled(value, label)
+        message[face_rows(slot), :] = value
+
+
+def near_side(parity):
+    return (HI, LO) if parity == 0 else (LO, HI)
 
 
 def chunks(rows_a, shape, body):
@@ -319,7 +333,7 @@
         body((a, pl.ds(t, 8), pl.ds(r, 128)))
         return carry
 
-    lax.fori_loop(0, counts[0] * counts[1] * counts[2], step, 0)
+    lax.fori_loop(0, counts[0] * counts[1] * counts[2], step, 0, unroll=4)
 
 
 def load(ref, where):
@@ -331,9 +345,9 @@
         ref[(q,) + where] = values[q]
 
 
-def label_of(regions, wide):
+def label_of(regions):
     label = jnp.max(jnp.max(regions[...], axis=0), axis=(0, 1), keepdims=True)
-    return jnp.broadcast_to(label.astype(jnp.float32), (1, wide))
+    return label.astype(jnp.float32)
 
 
 def porosity_factor(q, weight, velocity):
@@ -375,12 +389,7 @@
     for copy in loads[:3]:
         copy.wait()
     flags[...] = jnp.where(types[...] != 1, 1.0, 0.0)
-    label = label_of(regions, rows_r)
-    for side in (LO, HI):
-        block, i = FIRST.place[(side, "label")]
-        t_out[block, i : i + 1, :] = label
-    for out in (e_out, o_out):
-        out[16 * FIRST.fields : 16 * FIRST.fields + 8, :] = jnp.broadcast_to(label, (8, rows_r))
+    label = label_of(regions)
 
     def body(where):
         values = load(pops, where)
@@ -395,13 +404,14 @@
         chunks([a], porous.shape, body)
     loads[-1].wait()
     own = {POST: post, ADJ: seed, FACTOR: factors, MOTION: motion, FLAG: flags}
-    pack_azimuthal(FIRST, own, t_out)
+    pack_azimuthal(FIRST, own, range(rows_a), t_out, label)
 
     def run(parity):
-        pack_axial(FIRST, own, parity, e_out, o_out)
-        for out, block in ((ed_out, parity), (od_out, 1 - parity)):
-            out[0] = t_out[block]
-            out[1] = t_out[2]
+        near, far = near_side(parity)
+        pack_face(FIRST, own, near, e_out, label)
+        pack_face(FIRST, own, far, o_out, label)
+        ed_out[...] = t_out[parity]
+        od_out[...] = t_out[1 - parity]
 
     by_parity(parity_ref, run)
 
@@ -428,43 +438,49 @@
 
 
 def second_near_kernel(
-    parity_ref, post, seed, flags, porous, types, regions, e, t, ed,
-    post_next, adj, sens, around, state, back,
+    parity_ref, post, seed, factors, flags, porous, types, regions, e, t, ed,
+    post_next, adj, sens, around, e_out, t_out, partial, state, back, parts,
 ):
     def run(parity):
-        own = {POST: post, ADJ: seed, FLAG: flags}
+        own = {POST: post, ADJ: seed, FACTOR: factors, FLAG: flags}
         fields = Fields(FIRST, own, parity, e=e, t=t, ed=ed)
         rows, _ = near_rows(parity, porous.shape[0])
         results = (post_next, adj, sens, around)
         second_rows(fields, rows, (porous, types, regions), results, (state, back))
+        own = {POST: post_next, ADJ: adj}
+        pack_face(SECOND, own, near_side(parity)[0], e_out)
+        pack_azimuthal(SECOND, own, rows, t_out)
+        partial[...] = region_sums(fields, rows, adj, sens, around, regions, parts)
 
     by_parity(parity_ref, run)
 
 
 def second_far_kernel(
-    parity_ref, real_ref, post_near, adj_near, sens_near, around_near,
-    post, seed, factors, flags, porous, types, regions, e, o, t, ed, od,
-    post_next, adj, sens, around, e_out, o_out, t_out, partial, state, back, parts,
+    parity_ref, real_ref, post_near, adj_near, sens_near, around_near, t_near, partial_near,
+    post, seed, factors, flags, porous, types, regions, o, t, od,
+    post_next, adj, sens, around, t_out, o_out, partial, state, back, parts,
 ):
     def run(parity):
         own = {POST: post, ADJ: seed, FACTOR: factors, FLAG: flags}
-        fields = Fields(FIRST, own, parity, e, o, real_ref[0], t, ed, od)
+        fields = Fields(FIRST, own, parity, o=o, real=real_ref[0], t=t, od=od)
         _, row = near_rows(parity, porous.shape[0])
         results = (post_next, adj, sens, around)
         second_rows(fields, [row], (porous, types, regions), results, (state, back))
-        pack_axial(SECOND, {POST: post_next, ADJ: adj}, parity, e_out, o_out)
-        pack_azimuthal(SECOND, {POST: post_next, ADJ: adj}, t_out)
-        region_sums(fields, adj, sens, around, regions, parts, partial)
+        own = {POST: post_next, ADJ: adj}
+        pack_face(SECOND, own, near_side(parity)[1], o_out)
+        pack_azimuthal(SECOND, own, [row], t_out)
+        sums = region_sums(fields, [row], adj, sens, around, regions, parts)
+        partial[...] = partial_near[...] + sums
 
     by_parity(parity_ref, run)
 
 
-def region_sums(fields, adj, sens, around, regions, parts, partial):
+def region_sums(fields, rows, adj, sens, around, regions, parts):
     factors = fields.own[FACTOR]
     rows_a, rows_t, rows_r = sens.shape
-    sums = {(i, st): [] for i in (-1, 0, 1) for st in (-1, 0, 1)}
-    for a in range(rows_a):
-        sums[(0, 0)] += [sens[a], factors[0, a] * adj[0, a]]
+    sums = {}
+    for a in rows:
+        sums.setdefault((0, 0), []).extend([sens[a], factors[0, a] * adj[0, a]])
         for q in range(1, 19):
             behind = tuple(-c for c in VELOCITY[q])
             open_, value = around[q - 1, a], adj[q, a]
@@ -472,34 +488,33 @@
             term = jnp.where(open_ > 0, fields.moved(FACTOR, q, a, behind), 0.0) * value
             from_a = a + behind[0]
             beyond = -1 if from_a < 0 else 1 if from_a >= rows_a else 0
-            sums[(beyond, behind[1])].append(term)
+            sums.setdefault((beyond, behind[1]), []).append(term)
     at_t = lax.broadcasted_iota(jnp.int32, (rows_t, rows_r), 0)
-    rows = []
-    for beyond in (-1, 0, 1):
+    lines = []
+    for beyond in sorted({key[0] for key in sums}):
         low, centre, high = (functools.reduce(jnp.add, sums[(beyond, st)]) for st in (-1, 0, 1))
         inner = centre + jnp.where(at_t == 0, 0.0, low) + jnp.where(at_t == rows_t - 1, 0.0, high)
         a = {-1: -1, 0: 0, 1: rows_a}[beyond]
-        label = fields.row_label(a) if beyond else label_of(regions, rows_r)
-        rows.append((jnp.sum(inner, axis=0, keepdims=True), label))
-        rows.append((high[rows_t - 1 : rows_t], fields.message((LO, "label"), a)))
-        rows.append((low[0:1], fields.message((HI, "label"), a)))
+        label = fields.row_label(a) if beyond else label_of(regions)
+        lines.append((jnp.sum(inner, axis=0, keepdims=True), label))
+        a = a if beyond else rows[0]
+        lines.append((high[rows_t - 1 : rows_t], fields.edge_label(LO, a)))
+        lines.append((low[0:1], fields.edge_label(HI, a)))
     parts[...] = jnp.zeros_like(parts)
-    for i, (value, label) in enumerate(rows):
+    for i, (value, label) in enumerate(lines):
         parts[0, i : i + 1, :] = value
-        parts[1, i : i + 1, :] = label
+        parts[1, i : i + 1, :] = jnp.broadcast_to(label, (1, rows_r))
     lanes = lax.broadcasted_iota(jnp.int32, parts.shape[1:], 1) + 1
     total = jnp.sum(parts[0], axis=1, keepdims=True)
     chosen = jnp.where(lanes == parts[1].astype(jnp.int32), total, 0.0)
-    partial[...] = jnp.sum(chosen, axis=0, keepdims=True)
+    return jnp.sum(chosen, axis=0, keepdims=True)
 
 
 def corner_kernel(e, o, t, total, e_out, o_out):
-    block, i = SECOND.place[(LO, "sum")]
+    row = 16 * SECOND.fields
     for out in (e_out, o_out):
-        corners = out.at[16 * SECOND.fields : 16 * SECOND.fields + 16]
-        for k in range(SECOND.corner_blocks):
-            corners[8 * k : 8 * k + 8, :] = t[k]
-        corners[8 * block + i : 8 * block + i + 1, :] = total[...]
+        out[row : row + 8, :] = t[0]
+    e_out[row + 8 : row + 16, :] = jnp.broadcast_to(total[...], (8, e_out.shape[1]))
 
 
 def third_rows(fields, rows, cell_refs, own_refs, hbm, sens, scratch, sems):
@@ -623,8 +638,7 @@
     def send(x, shift):
         return lax.ppermute(x, ("ax", "az"), axial_pairs(flip, shift))
 
-    rows = high_rows(FIRST)
-    return from_both_sectors(message, np.stack([rows[0], rows[2]]), send)
+    return from_both_sectors(message, high_rows(FIRST)[0], send)
 
 
 def from_partner(x, flip_a, flip_t):
@@ -657,8 +671,8 @@
     post, factors, e, o, t, ed, od, flags = call(
         first_kernel,
         [pltpu.SMEM] + [HBM] * 5,
-        [(pops, f32, VMEM), (pops, f32, VMEM)] + [axial(FIRST, 8)] * 2 + azimuthal(FIRST)
-        + [((2, 8, wide), f32, VMEM)] * 2 + [(cells_, f32, VMEM)],
+        [(pops, f32, VMEM), (pops, f32, VMEM)] + [axial(FIRST, 0)] * 2 + azimuthal(FIRST)
+        + [((8, wide), f32, VMEM)] * 2 + [(cells_, f32, VMEM)],
         [VMEM(x.shape, x.dtype) for x in inputs]
         + [VMEM((4,) + cells_, f32), pltpu.SemaphoreType.DMA((4 + cells_[0],))],
         place[0],
@@ -668,33 +682,34 @@
     t_near = send_azimuthal(FIRST, t)
     ed, od = send_diagonal(ed, 0), send_diagonal(od, 1)
     layers = [(pops, f32, VMEM), (pops, f32, VMEM), (cells_, f32, VMEM), ((18,) + cells_, f32, VMEM)]
-    inside = (flags, porosity, cell_type, region)
-    near = call(
+    inside = (post, adjoint_seed, factors, flags, porosity, cell_type, region)
+    row = [((1, wide), f32, VMEM)]
+    scratch = [VMEM(pops, f32), VMEM(pops, f32), VMEM((2, 8, wide), f32)]
+    *near, e, t, total = call(
         second_near_kernel,
-        [pltpu.SMEM] + [VMEM] * 9,
-        layers,
-        [VMEM(pops, f32), VMEM(pops, f32)],
-        place[0], post, adjoint_seed, *inside, e, t_near, ed,
+        [pltpu.SMEM] + [VMEM] * 10,
+        layers + [axial(SECOND, 16)] + azimuthal(SECOND) + row,
+        scratch,
+        place[0], *inside, e, t_near, ed,
     )
-    post, adj, sens_one, around, e, o, t, total = call(
+    post, adj, sens_one, around, t, o, total = call(
         second_far_kernel,
         [pltpu.SMEM] * 2 + [VMEM] * 16,
-        layers + [axial(SECOND, 16)] * 2 + azimuthal(SECOND) + [((1, wide), f32, VMEM)],
-        [VMEM(pops, f32), VMEM(pops, f32), VMEM((2, 16, wide), f32)],
-        *place, *near, post, adjoint_seed, factors, *inside, e, o, t_near, ed, od,
-        aliases={2: 0, 3: 1, 4: 2, 5: 3},
+        layers + azimuthal(SECOND) + [axial(SECOND, 8)] + row,
+        scratch,
+        *place, *near, t, total, *inside, o, t_near, od,
+        aliases={2: 0, 3: 1, 4: 2, 5: 3, 6: 4},
     )
     t_near = send_azimuthal(SECOND, t)
-    block, i = SECOND.place[(LO, "sum")]
     halving = size_a >= 4 and not (size_a & (size_a - 1) or size_t & (size_t - 1))
-    flips = [((1 << k) | 1, 0) for k in range(2, size_a.bit_length() - 1)]
+    flips = [((1 << k) | 1, 0) for k in range(size_a.bit_length() - 3, 0, -1)]
     if halving:
-        total = total + from_partner(total, 3, 0)
+        total = total + from_partner(total, size_a // 2 | 1, 0)
         flips = [(1, 1 << k) for k in range(size_t.bit_length() - 1)] + flips
     e, o = call(
         corner_kernel,
         [VMEM] * 4,
-        [axial(SECOND, 16)] * 2,
+        [axial(SECOND, 16), axial(SECOND, 8)],
         [],
         e, o, t_near, total,
         aliases={0: 0, 1: 1},
@@ -711,7 +726,7 @@
         place[0], *inside, e, t_near,
     )
     if halving:
-        row = 16 * SECOND.fields + 8 * block + i
+        row = 16 * SECOND.fields + 8
         totals = total + e[row : row + 1]
         for flip in flips:
             if flip == flips[-1]:

time: 32.1 us -> 30.8 us (0.960); the launches traced: 32 us -> 30.3 us
  waiting for transfers between devices: 8.16 us -> 6.98 us
  Pallas kernels: 7.17 us -> 6.4 us
    ppermute x4, waiting for transfers between devices: 4.88 us -> 3.9 us  [from_partner(): return lax.ppermute(x, ('ax', 'az'), pairs)]
    pallas_call x6, Pallas kernels: 7.17 us -> 6.4 us  [call(): pl.pallas_call(body, out_shape=[jax.ShapeDtypeStruct(shape, dtype) for sh...]
    ppermute x2, waiting for transfers between devices: 2.95 us -> 2.43 us  [send(): return lax.ppermute(x, ('ax', 'az'), axial_pairs(flip, shift))]
    ppermute x4, starting transfers between devices: 5.71 us -> 6.23 us  [from_partner(): return lax.ppermute(x, ('ax', 'az'), pairs)]
  transfers between devices with their start and end apart: 12 -> 12, of which waited for: 5 -> 6; matrix products, arithmetic and copies ran while one was open for 0% -> 0% of each run, Pallas kernels for 13% -> 13%
where the time goes in v6:
time: 30.8 us; the launch traced here: 30.3 us
  starting transfers between devices  15.6 us (51%)
  waiting for transfers between devices  6.98 us (23%)
  Pallas kernels  6.4 us (21%)
  between operations  0.75 us (2%)
  other arithmetic  0.53 us (2%)
    pallas_call x6, Pallas kernels, call(): pl.pallas_call(body, out_shape=[jax.ShapeDtypeStruct(shape, dtype) for sh...  6.4 us
    ppermute x4, starting transfers between devices, from_partner(): return lax.ppermute(x, ('ax', 'az'), pairs)  6.23 us
    ppermute x4, starting transfers between devices, send_axial(): return lax.ppermute(message, ('ax', 'az'), axial_pairs(flip))  4.24 us
    ppermute x4, waiting for transfers between devices, from_partner(): return lax.ppermute(x, ('ax', 'az'), pairs)  3.9 us
    ppermute x2, starting transfers between devices, send(): return lax.ppermute(x, ('ax', 'az'), axial_pairs(flip, shift))  2.88 us
    ppermute x2, waiting for transfers between devices, send(): return lax.ppermute(x, ('ax', 'az'), axial_pairs(flip, shift))  2.43 us
    ppermute x2, starting transfers between devices, send(): return lax.ppermute(x, 'az', [(i, (i + shift) % size) for i in range(size)])  2.23 us
  transfers between devices with their start and end apart: 12, of which 6 were waited for; matrix products, arithmetic and copies ran while one was open for 0% of the time, Pallas kernels for 13%

profile of v6, /device:TPU:0, one launch (start us, length us, event | category | flops | bytes accessed | tf_op | source)
XLA Modules:
  0.0 30.3 jit_solution(11589327317634145748)
XLA Ops:
  0.6 0.0 copy-start.1
  0.7 0.0 copy-start.2
  0.7 0.0 copy-start.3
  0.7 0.0 copy-start.4
  0.7 1.7 %shard_map.84 = (f32[19,2,16,256]{3,2,1,0:T(8,128)S(1)}, f32[19,2,16,256]{3,2,1,0:T(8,128)S(1)}, f32[240,256]{1,0:T(8,128)S(1)}, f32[240,256]{1,0:T(8,128)S(1)},...) custom-call(s32[1]{0:T(128)} %bitcast.parity_ref, ...), custom_call_target="tpu_custom_call" | custom-call | tf_op jit(solution)/shard_map/pallas_call | solution.py:584
  2.4 0.5 %collective-permute-start = (f32[240,256]{1,0:T(8,128)S(1)}, f32[240,256]{1,0:T(8,128)S(1)}, u32[]{:S(2)}, u32[]{:S(2)}) collective-permute-start(f32[240,256]{1,0:T(8,128)S(1)} %get-tuple-element.38), channel_id=1, source_target_pairs={{0,2},{1,3},{2,0},{3,1},{4,6},{5,7},{6,4},{7,5},{8,10},{9,11},{10,... | collective-permute-start | bytes 737288 | tf_op jit(solution)/shard_map/ppermute | solution.py:634
  2.9 2.6 %collective-permute-start.3 = (f32[240,256]{1,0:T(8,128)S(1)}, f32[240,256]{1,0:T(8,128)S(1)}, u32[]{:S(2)}, u32[]{:S(2)}) collective-permute-start(f32[240,256]{1,0:T(8,128)S(1)} %get-tuple-element.47), channel_id=1, source_target_pairs={{0,1},{1,0},{2,4},{3,5},{4,2},{5,3},{6,8},{7,9},{8,6},{9,7},{10,12... | collective-permute-start | bytes 737288 | tf_op jit(solution)/shard_map/ppermute | solution.py:634
  5.5 0.1 collective-permute-start.1
  5.5 1.4 %collective-permute-start.2 = (f32[8,256]{1,0:T(8,128)S(1)}, f32[8,256]{1,0:T(8,128)S(1)}, u32[]{:S(2)}, u32[]{:S(2)}) collective-permute-start(f32[8,256]{1,0:T(8,128)S(1)} %get-tuple-element.40), channel_id=1, source_target_pairs={{0,3},{1,2},{2,1},{3,0},{4,7},{5,6},{6,5},{7,4},{8,11},{9,10},{10,... | collective-permute-start | bytes 24584 | tf_op jit(solution)/shard_map/ppermute | solution.py:639
  6.9 1.5 %collective-permute-start.4 = (f32[8,256]{1,0:T(8,128)S(1)}, f32[8,256]{1,0:T(8,128)S(1)}, u32[]{:S(2)}, u32[]{:S(2)}) collective-permute-start(f32[8,256]{1,0:T(8,128)S(1)} %get-tuple-element.48), channel_id=1, source_target_pairs={{0,1},{1,0},{2,5},{3,4},{4,3},{5,2},{6,9},{7,8},{8,7},{9,6},{10,13... | collective-permute-start | bytes 24584 | tf_op jit(solution)/shard_map/ppermute | solution.py:639
  8.4 2.4 %collective-permute-done.2.ed = f32[8,256]{1,0:T(8,128)S(1)} collective-permute-done((f32[8,256]{1,0:T(8,128)S(1)}, f32[8,256]{1,0:T(8,128)S(1)}, u32[]{:S(2)}, u32[]{:S(2)}) %collective-permute-start.2) | collective-permute-done | bytes 8224 | tf_op jit(solution)/shard_map/ppermute | solution.py:639
  10.9 0.3 collective-permute-done.1.t
  11.1 0.0 collective-permute-done.e
  11.1 0.0 copy-done.1
  11.1 0.0 copy-done.2
  11.2 0.0 copy-done.3
  11.2 0.0 copy-done.4
  11.2 0.8 %shard_map.85 = (f32[19,2,16,256]{3,2,1,0:T(8,128)S(1)}, f32[19,2,16,256]{3,2,1,0:T(8,128)S(1)}, f32[2,16,256]{2,1,0:T(8,128)S(1)}, f32[18,2,16,256]{3,2,1,0:T(8...) custom-call(s32[1]{0:T(128)} %bitcast.parity_ref, ...), custom_call_target="tpu_custom_call" | custom-call | tf_op jit(solution)/shard_map/pallas_call | solution.py:584
  12.0 0.0 collective-permute-done.4.od
  12.0 0.0 collective-permute-done.3.o
  12.0 0.0 copy-start
  12.0 0.8 %shard_map.86 = (f32[19,2,16,256]{3,2,1,0:T(8,128)S(1)}, f32[19,2,16,256]{3,2,1,0:T(8,128)S(1)}, f32[2,16,256]{2,1,0:T(8,128)S(1)}, f32[18,2,16,256]{3,2,1,0:T(8...) custom-call(s32[1]{0:T(128)} %bitcast.parity_ref, ...), custom_call_target="tpu_custom_call", output_to_operand_aliasing={{0}: (2, {}), {1}: (3, {}), {2}: (4, {}), {3}: (5, {}), {4}... | custom-call | tf_op jit(solution)/shard_map/pallas_call | solution.py:584
  12.8 2.1 %collective-permute-start.5 = (f32[5,8,256]{2,1,0:T(8,128)S(1)}, f32[5,8,256]{2,1,0:T(8,128)S(1)}, u32[]{:S(2)}, u32[]{:S(2)}) collective-permute-start(f32[5,8,256]{2,1,0:T(8,128)S(1)} %get-tuple-element.55), channel_id=1, source_target_pairs={{0,1},{1,0},{2,3},{3,2},{4,5},{5,4},{6,7},{7,6},{8,9},{9,8},{10,11... | collective-permute-start | bytes 122888 | tf_op jit(solution)/shard_map/ppermute | solution.py:628
  15.0 2.1 %collective-permute-start.6 = (f32[1,256]{1,0:T(1,128)S(1)}, f32[1,256]{1,0:T(1,128)S(1)}, u32[]{:S(2)}, u32[]{:S(2)}) collective-permute-start(f32[1,256]{1,0:T(1,128)S(1)} %get-tuple-element.56), channel_id=1, source_target_pairs={{0,18},{1,19},{2,16},{3,17},{4,22},{5,23},{6,20},{7,21},{8,26},{9,... | collective-permute-start | bytes 3080 | tf_op jit(solution)/shard_map/ppermute | solution.py:651
  17.0 1.8 %collective-permute-done.6 = f32[1,256]{1,0:T(1,128)S(1)} collective-permute-done((f32[1,256]{1,0:T(1,128)S(1)}, f32[1,256]{1,0:T(1,128)S(1)}, u32[]{:S(2)}, u32[]{:S(2)}) %collective-permute-start.6) | collective-permute-done | bytes 1056 | tf_op jit(solution)/shard_map/ppermute | solution.py:651
  18.9 0.0 collective-permute-done.5.t
  18.9 0.2 collective-permute-start.7
  19.1 0.9 %collective-permute-start.8 = (f32[168,256]{1,0:T(8,128)S(1)}, f32[168,256]{1,0:T(8,128)S(1)}, u32[]{:S(2)}, u32[]{:S(2)}) collective-permute-start(f32[168,256]{1,0:T(8,128)S(1)} %get-tuple-element.61), channel_id=1, source_target_pairs={{0,1},{1,0},{2,4},{3,5},{4,2},{5,3},{6,8},{7,9},{8,6},{9,7},{10,12... | collective-permute-start | bytes 516104 | tf_op jit(solution)/shard_map/ppermute | solution.py:634
  20.0 0.4 %collective-permute-done.7.e = f32[176,256]{1,0:T(8,128)S(1)} collective-permute-done((f32[176,256]{1,0:T(8,128)S(1)}, f32[176,256]{1,0:T(8,128)S(1)}, u32[]{:S(2)}, u32[]{:S(2)}) %collective-permute-start.7) | collective-permute-done | bytes 180256 | tf_op jit(solution)/shard_map/ppermute | solution.py:634
  20.4 1.2 %collective-permute-start.9 = (f32[1,256]{1,0:T(1,128)S(1)}, f32[1,256]{1,0:T(1,128)S(1)}, u32[]{:S(2)}, u32[]{:S(2)}) collective-permute-start(f32[1,256]{1,0:T(1,128)S(1)} %slice_add_fusion), channel_id=1, source_target_pairs={{0,3},{1,2},{2,1},{3,0},{4,7},{5,6},{6,5},{7,4},{8,11},{9,10},{10,... | collective-permute-start | bytes 3080 | tf_op jit(solution)/shard_map/ppermute | solution.py:651
  21.5 1.8 %collective-permute-done.9 = f32[1,256]{1,0:T(1,128)S(1)} collective-permute-done((f32[1,256]{1,0:T(1,128)S(1)}, f32[1,256]{1,0:T(1,128)S(1)}, u32[]{:S(2)}, u32[]{:S(2)}) %collective-permute-start.9) | collective-permute-done | bytes 1056 | tf_op jit(solution)/shard_map/ppermute | solution.py:651
  23.4 1.5 %collective-permute-start.10 = (f32[1,256]{1,0:T(1,128)S(1)}, f32[1,256]{1,0:T(1,128)S(1)}, u32[]{:S(2)}, u32[]{:S(2)}) collective-permute-start(f32[1,256]{1,0:T(1,128)S(1)} %add.22), channel_id=1, source_target_pairs={{0,10},{1,11},{2,8},{3,9},{4,14},{5,15},{6,12},{7,13},{8,2},{9,3},... | collective-permute-start | bytes 3080 | tf_op jit(solution)/shard_map/ppermute | solution.py:651
  24.9 0.0 copy-done
  24.9 1.2 %shard_map.88 = (f32[19,2,16,256]{3,2,1,0:T(8,128)}, f32[19,2,16,256]{3,2,1,0:T(8,128)}, f32[2,16,256]{2,1,0:T(8,128)S(1)}) custom-call(s32[1]{0:T(128)} %bitcast.parity_ref, f32[19,2,16,256]{3,2,1,0:T(8,128)S(1)} %get-tuple-element.49.post, f32[19,2,16,256]{3,2,1,0:T(8,128)S(1)} %get-tuple-element.50.adj, f32[2,16,256]{2,1,0:T(8,128)S(1)} %get-tuple-element.37.flags, ...), custom_call_target="tpu_custom_call" | custom-call | tf_op jit(solution)/shard_map/pallas_call | solution.py:584
  26.1 0.2 collective-permute-done.10
  26.4 0.0 collective-permute-done.8.o
  26.4 1.5 %collective-permute-start.11 = (f32[1,256]{1,0:T(1,128)S(1)}, f32[1,256]{1,0:T(1,128)S(1)}, u32[]{:S(2)}, u32[]{:S(2)}) collective-permute-start(f32[1,256]{1,0:T(1,128)S(1)} %add.23), channel_id=1, source_target_pairs={{0,6},{1,7},{2,4},{3,5},{4,2},{5,3},{6,0},{7,1},{8,14},{9,15},{10,... | collective-permute-start | bytes 3080 | tf_op jit(solution)/shard_map/ppermute | solution.py:651
  27.9 1.9 %shard_map.89 = (f32[19,2,16,256]{3,2,1,0:T(8,128)}, f32[19,2,16,256]{3,2,1,0:T(8,128)}, f32[2,16,256]{2,1,0:T(8,128)}) custom-call(s32[1]{0:T(128)} %bitcast.parity_ref, s32[1]{0:T(128)} %bitcast.1.real_ref, f32[19,2,16,256]{3,2,1,0:T(8,128)} %get-tuple-element.58.final_near, ...), custom_call_target="tpu_custom_call", output_to_operand_aliasing={{0}: (2, {}), {1}: (3, {})} | custom-call | tf_op jit(solution)/shard_map/pallas_call | solution.py:584
  29.7 0.0 collective-permute-done.11
  29.7 0.5 %fusion = f32[8]{0:T(128)} fusion(f32[1,256]{1,0:T(1,128)S(1)} %collective-permute-done.11, f32[1,256]{1,0:T(1,128)S(1)} %add.23), kind=kLoop, calls=%fused_computation.2 | loop fusion | flops 8 | bytes 96 | tf_op jit(solution)/shard_map/squeeze | solution.py:745
  (5 shorter events, 0.0 us)
Async XLA Ops:
  0.6 10.5 %copy-start.1 = (f32[19,2,16,256]{3,2,1,0:T(8,128)S(1)}, f32[19,2,16,256]{3,2,1,0:T(8,128)}, u32[]{:S(2)}) copy-start(f32[19,2,16,256]{3,2,1,0:T(8,128)} %seed.3) | copy-start | bytes 1867780
  0.7 10.5 %copy-start.2 = (f32[2,16,256]{2,1,0:T(8,128)S(1)}, f32[2,16,256]{2,1,0:T(8,128)}, u32[]{:S(2)}) copy-start(f32[2,16,256]{2,1,0:T(8,128)} %porous.7) | copy-start | bytes 98308
  0.7 10.5 %copy-start.3 = (s32[2,16,256]{2,1,0:T(8,128)S(1)}, s32[2,16,256]{2,1,0:T(8,128)}, u32[]{:S(2)}) copy-start(s32[2,16,256]{2,1,0:T(8,128)} %types.7) | copy-start | bytes 98308
  0.7 10.5 %copy-start.4 = (s32[2,16,256]{2,1,0:T(8,128)S(1)}, s32[2,16,256]{2,1,0:T(8,128)}, u32[]{:S(2)}) copy-start(s32[2,16,256]{2,1,0:T(8,128)} %regions.7) | copy-start | bytes 98308
  2.4 8.8 %collective-permute-start = (f32[240,256]{1,0:T(8,128)S(1)}, f32[240,256]{1,0:T(8,128)S(1)}, u32[]{:S(2)}, u32[]{:S(2)}) collective-permute-start(f32[240,256]{1,0:T(8,128)S(1)} %get-tuple-element.38), channel_id=1, source_target_pairs={{0,2},{1,3},{2,0},{3,1},{4,6},{5,7},{6,4},{7,5},{8,10},{9,11},{10,... | collective-permute-start | bytes 737288 | tf_op jit(solution)/shard_map/ppermute | solution.py:634
  2.9 9.1 %collective-permute-start.3 = (f32[240,256]{1,0:T(8,128)S(1)}, f32[240,256]{1,0:T(8,128)S(1)}, u32[]{:S(2)}, u32[]{:S(2)}) collective-permute-start(f32[240,256]{1,0:T(8,128)S(1)} %get-tuple-element.47), channel_id=1, source_target_pairs={{0,1},{1,0},{2,4},{3,5},{4,2},{5,3},{6,8},{7,9},{8,6},{9,7},{10,12... | collective-permute-start | bytes 737288 | tf_op jit(solution)/shard_map/ppermute | solution.py:634
  5.5 5.7 %collective-permute-start.1 = (f32[8,8,256]{2,1,0:T(8,128)S(1)}, f32[8,8,256]{2,1,0:T(8,128)S(1)}, u32[]{:S(2)}, u32[]{:S(2)}) collective-permute-start(f32[8,8,256]{2,1,0:T(8,128)S(1)} %get-tuple-element.39), channel_id=1, source_target_pairs={{0,1},{1,0},{2,3},{3,2},{4,5},{5,4},{6,7},{7,6},{8,9},{9,8},{10,11... | collective-permute-start | bytes 196616 | tf_op jit(solution)/shard_map/ppermute | solution.py:628
  5.5 5.3 %collective-permute-start.2 = (f32[8,256]{1,0:T(8,128)S(1)}, f32[8,256]{1,0:T(8,128)S(1)}, u32[]{:S(2)}, u32[]{:S(2)}) collective-permute-start(f32[8,256]{1,0:T(8,128)S(1)} %get-tuple-element.40), channel_id=1, source_target_pairs={{0,3},{1,2},{2,1},{3,0},{4,7},{5,6},{6,5},{7,4},{8,11},{9,10},{10,... | collective-permute-start | bytes 24584 | tf_op jit(solution)/shard_map/ppermute | solution.py:639
  6.9 5.1 %collective-permute-start.4 = (f32[8,256]{1,0:T(8,128)S(1)}, f32[8,256]{1,0:T(8,128)S(1)}, u32[]{:S(2)}, u32[]{:S(2)}) collective-permute-start(f32[8,256]{1,0:T(8,128)S(1)} %get-tuple-element.48), channel_id=1, source_target_pairs={{0,1},{1,0},{2,5},{3,4},{4,3},{5,2},{6,9},{7,8},{8,7},{9,6},{10,13... | collective-permute-start | bytes 24584 | tf_op jit(solution)/shard_map/ppermute | solution.py:639
  12.0 12.9 %copy-start = (f32[19,2,16,256]{3,2,1,0:T(8,128)S(1)}, f32[19,2,16,256]{3,2,1,0:T(8,128)}, u32[]{:S(2)}) copy-start(f32[19,2,16,256]{3,2,1,0:T(8,128)} %pops.3) | copy-start | bytes 1867780
  12.8 6.0 %collective-permute-start.5 = (f32[5,8,256]{2,1,0:T(8,128)S(1)}, f32[5,8,256]{2,1,0:T(8,128)S(1)}, u32[]{:S(2)}, u32[]{:S(2)}) collective-permute-start(f32[5,8,256]{2,1,0:T(8,128)S(1)} %get-tuple-element.55), channel_id=1, source_target_pairs={{0,1},{1,0},{2,3},{3,2},{4,5},{5,4},{6,7},{7,6},{8,9},{9,8},{10,11... | collective-permute-start | bytes 122888 | tf_op jit(solution)/shard_map/ppermute | solution.py:628
  15.0 3.9 %collective-permute-start.6 = (f32[1,256]{1,0:T(1,128)S(1)}, f32[1,256]{1,0:T(1,128)S(1)}, u32[]{:S(2)}, u32[]{:S(2)}) collective-permute-start(f32[1,256]{1,0:T(1,128)S(1)} %get-tuple-element.56), channel_id=1, source_target_pairs={{0,18},{1,19},{2,16},{3,17},{4,22},{5,23},{6,20},{7,21},{8,26},{9,... | collective-permute-start | bytes 3080 | tf_op jit(solution)/shard_map/ppermute | solution.py:651
  18.9 1.5 %collective-permute-start.7 = (f32[176,256]{1,0:T(8,128)S(1)}, f32[176,256]{1,0:T(8,128)S(1)}, u32[]{:S(2)}, u32[]{:S(2)}) collective-permute-start(f32[176,256]{1,0:T(8,128)S(1)} %get-tuple-element.57), channel_id=1, source_target_pairs={{0,2},{1,3},{2,0},{3,1},{4,6},{5,7},{6,4},{7,5},{8,10},{9,11},{10,... | collective-permute-start | bytes 540680 | tf_op jit(solution)/shard_map/ppermute | solution.py:634
  19.1 7.3 %collective-permute-start.8 = (f32[168,256]{1,0:T(8,128)S(1)}, f32[168,256]{1,0:T(8,128)S(1)}, u32[]{:S(2)}, u32[]{:S(2)}) collective-permute-start(f32[168,256]{1,0:T(8,128)S(1)} %get-tuple-element.61), channel_id=1, source_target_pairs={{0,1},{1,0},{2,4},{3,5},{4,2},{5,3},{6,8},{7,9},{8,6},{9,7},{10,12... | collective-permute-start | bytes 516104 | tf_op jit(solution)/shard_map/ppermute | solution.py:634
  20.4 3.0 %collective-permute-start.9 = (f32[1,256]{1,0:T(1,128)S(1)}, f32[1,256]{1,0:T(1,128)S(1)}, u32[]{:S(2)}, u32[]{:S(2)}) collective-permute-start(f32[1,256]{1,0:T(1,128)S(1)} %slice_add_fusion), channel_id=1, source_target_pairs={{0,3},{1,2},{2,1},{3,0},{4,7},{5,6},{6,5},{7,4},{8,11},{9,10},{10,... | collective-permute-start | bytes 3080 | tf_op jit(solution)/shard_map/ppermute | solution.py:651
  23.4 3.0 %collective-permute-start.10 = (f32[1,256]{1,0:T(1,128)S(1)}, f32[1,256]{1,0:T(1,128)S(1)}, u32[]{:S(2)}, u32[]{:S(2)}) collective-permute-start(f32[1,256]{1,0:T(1,128)S(1)} %add.22), channel_id=1, source_target_pairs={{0,10},{1,11},{2,8},{3,9},{4,14},{5,15},{6,12},{7,13},{8,2},{9,3},... | collective-permute-start | bytes 3080 | tf_op jit(solution)/shard_map/ppermute | solution.py:651
  26.4 3.4 %collective-permute-start.11 = (f32[1,256]{1,0:T(1,128)S(1)}, f32[1,256]{1,0:T(1,128)S(1)}, u32[]{:S(2)}, u32[]{:S(2)}) collective-permute-start(f32[1,256]{1,0:T(1,128)S(1)} %add.23), channel_id=1, source_target_pairs={{0,6},{1,7},{2,4},{3,5},{4,2},{5,3},{6,0},{7,1},{8,14},{9,15},{10,... | collective-permute-start | bytes 3080 | tf_op jit(solution)/shard_map/ppermute | solution.py:651

commit v7 on v6

--- a/solution.py
+++ b/solution.py
@@ -702,10 +702,12 @@
     )
     t_near = send_azimuthal(SECOND, t)
     halving = size_a >= 4 and not (size_a & (size_a - 1) or size_t & (size_t - 1))
-    flips = [((1 << k) | 1, 0) for k in range(size_a.bit_length() - 3, 0, -1)]
+    flips, last = [(1, 1 << k) for k in range(size_t.bit_length() - 1)], []
     if halving:
         total = total + from_partner(total, size_a // 2 | 1, 0)
-        flips = [(1, 1 << k) for k in range(size_t.bit_length() - 1)] + flips
+        left = [(1 << k) | 1 for k in range(size_a.bit_length() - 3, 0, -1)]
+        last = left[-2:] if len(left) > 1 else []
+        flips += [(flip, 0) for flip in left[: len(left) - len(last)]]
     e, o = call(
         corner_kernel,
         [VMEM] * 4,
@@ -729,9 +731,12 @@
         row = 16 * SECOND.fields + 8
         totals = total + e[row : row + 1]
         for flip in flips:
-            if flip == flips[-1]:
-                totals, _ = lax.optimization_barrier((totals, (o, near[2])))
             totals = totals + from_partner(totals, *flip)
+        if last:
+            totals, _ = lax.optimization_barrier((totals, near[2]))
+            one, two = last
+            pair = totals + from_partner(totals, one, 0)
+            totals = pair + (from_partner(totals, two, 0) + from_partner(totals, one ^ two, 0))
     else:
         totals = lax.psum(total, ("ax", "az"))
     final, adjoint, sensitivity = call(

time: 30.8 us -> 29.7 us (0.964); the launches traced: 30.3 us -> 29.6 us
  waiting for transfers between devices: 6.98 us -> 6.09 us
    ppermute x4 -> x5, waiting for transfers between devices: 3.9 us -> 3.02 us  [from_partner(): return lax.ppermute(x, ('ax', 'az'), pairs)]
    ppermute x4 -> x5, starting transfers between devices: 6.23 us -> 6.43 us  [from_partner(): return lax.ppermute(x, ('ax', 'az'), pairs)]
  transfers between devices with their start and end apart: 12 -> 13, of which waited for: 6 -> 7; matrix products, arithmetic and copies ran while one was open for 0% -> 0% of each run, Pallas kernels for 13% -> 13%
where the time goes in v7:
time: 29.7 us; the launch traced here: 29.6 us
  starting transfers between devices  15.8 us (53%)
  Pallas kernels  6.4 us (22%)
  waiting for transfers between devices  6.09 us (21%)
  between operations  0.75 us (3%)
  other arithmetic  0.52 us (2%)
    ppermute x5, starting transfers between devices, from_partner(): return lax.ppermute(x, ('ax', 'az'), pairs)  6.43 us
    pallas_call x6, Pallas kernels, call(): pl.pallas_call(body, out_shape=[jax.ShapeDtypeStruct(shape, dtype) for sh...  6.4 us
    ppermute x4, starting transfers between devices, send_axial(): return lax.ppermute(message, ('ax', 'az'), axial_pairs(flip))  4.24 us
    ppermute x5, waiting for transfers between devices, from_partner(): return lax.ppermute(x, ('ax', 'az'), pairs)  3.02 us
    ppermute x2, starting transfers between devices, send(): return lax.ppermute(x, ('ax', 'az'), axial_pairs(flip, shift))  2.88 us
    ppermute x2, waiting for transfers between devices, send(): return lax.ppermute(x, ('ax', 'az'), axial_pairs(flip, shift))  2.43 us
    ppermute x2, starting transfers between devices, send(): return lax.ppermute(x, 'az', [(i, (i + shift) % size) for i in range(size)])  2.23 us
  transfers between devices with their start and end apart: 13, of which 7 were waited for; matrix products, arithmetic and copies ran while one was open for 0% of the time, Pallas kernels for 13%

profile of v7, /device:TPU:0, one launch (start us, length us, event | category | flops | bytes accessed | tf_op | source)
XLA Modules:
  0.0 29.6 jit_solution(6999705045920500057)
XLA Ops:
  0.6 0.0 copy-start.1
  0.7 0.0 copy-start.2
  0.7 0.0 copy-start.3
  0.7 0.0 copy-start.4
  0.7 1.7 %shard_map.84 = (f32[19,2,16,256]{3,2,1,0:T(8,128)S(1)}, f32[19,2,16,256]{3,2,1,0:T(8,128)S(1)}, f32[240,256]{1,0:T(8,128)S(1)}, f32[240,256]{1,0:T(8,128)S(1)},...) custom-call(s32[1]{0:T(128)} %bitcast.parity_ref, ...), custom_call_target="tpu_custom_call" | custom-call | tf_op jit(solution)/shard_map/pallas_call | solution.py:584
  2.4 0.5 %collective-permute-start = (f32[240,256]{1,0:T(8,128)S(1)}, f32[240,256]{1,0:T(8,128)S(1)}, u32[]{:S(2)}, u32[]{:S(2)}) collective-permute-start(f32[240,256]{1,0:T(8,128)S(1)} %get-tuple-element.38), channel_id=1, source_target_pairs={{0,2},{1,3},{2,0},{3,1},{4,6},{5,7},{6,4},{7,5},{8,10},{9,11},{10,... | collective-permute-start | bytes 737288 | tf_op jit(solution)/shard_map/ppermute | solution.py:634
  2.9 2.6 %collective-permute-start.3 = (f32[240,256]{1,0:T(8,128)S(1)}, f32[240,256]{1,0:T(8,128)S(1)}, u32[]{:S(2)}, u32[]{:S(2)}) collective-permute-start(f32[240,256]{1,0:T(8,128)S(1)} %get-tuple-element.47), channel_id=1, source_target_pairs={{0,1},{1,0},{2,4},{3,5},{4,2},{5,3},{6,8},{7,9},{8,6},{9,7},{10,12... | collective-permute-start | bytes 737288 | tf_op jit(solution)/shard_map/ppermute | solution.py:634
  5.5 0.1 collective-permute-start.1
  5.5 1.4 %collective-permute-start.2 = (f32[8,256]{1,0:T(8,128)S(1)}, f32[8,256]{1,0:T(8,128)S(1)}, u32[]{:S(2)}, u32[]{:S(2)}) collective-permute-start(f32[8,256]{1,0:T(8,128)S(1)} %get-tuple-element.40), channel_id=1, source_target_pairs={{0,3},{1,2},{2,1},{3,0},{4,7},{5,6},{6,5},{7,4},{8,11},{9,10},{10,... | collective-permute-start | bytes 24584 | tf_op jit(solution)/shard_map/ppermute | solution.py:639
  6.9 1.5 %collective-permute-start.4 = (f32[8,256]{1,0:T(8,128)S(1)}, f32[8,256]{1,0:T(8,128)S(1)}, u32[]{:S(2)}, u32[]{:S(2)}) collective-permute-start(f32[8,256]{1,0:T(8,128)S(1)} %get-tuple-element.48), channel_id=1, source_target_pairs={{0,1},{1,0},{2,5},{3,4},{4,3},{5,2},{6,9},{7,8},{8,7},{9,6},{10,13... | collective-permute-start | bytes 24584 | tf_op jit(solution)/shard_map/ppermute | solution.py:639
  8.4 2.4 %collective-permute-done.2.ed = f32[8,256]{1,0:T(8,128)S(1)} collective-permute-done((f32[8,256]{1,0:T(8,128)S(1)}, f32[8,256]{1,0:T(8,128)S(1)}, u32[]{:S(2)}, u32[]{:S(2)}) %collective-permute-start.2) | collective-permute-done | bytes 8224 | tf_op jit(solution)/shard_map/ppermute | solution.py:639
  10.9 0.3 collective-permute-done.1.t
  11.1 0.0 collective-permute-done.e
  11.1 0.0 copy-done.1
  11.1 0.0 copy-done.2
  11.2 0.0 copy-done.3
  11.2 0.0 copy-done.4
  11.2 0.8 %shard_map.85 = (f32[19,2,16,256]{3,2,1,0:T(8,128)S(1)}, f32[19,2,16,256]{3,2,1,0:T(8,128)S(1)}, f32[2,16,256]{2,1,0:T(8,128)S(1)}, f32[18,2,16,256]{3,2,1,0:T(8...) custom-call(s32[1]{0:T(128)} %bitcast.parity_ref, ...), custom_call_target="tpu_custom_call" | custom-call | tf_op jit(solution)/shard_map/pallas_call | solution.py:584
  12.0 0.0 collective-permute-done.4.od
  12.0 0.0 collective-permute-done.3.o
  12.0 0.0 copy-start
  12.0 0.8 %shard_map.86 = (f32[19,2,16,256]{3,2,1,0:T(8,128)S(1)}, f32[19,2,16,256]{3,2,1,0:T(8,128)S(1)}, f32[2,16,256]{2,1,0:T(8,128)S(1)}, f32[18,2,16,256]{3,2,1,0:T(8...) custom-call(s32[1]{0:T(128)} %bitcast.parity_ref, ...), custom_call_target="tpu_custom_call", output_to_operand_aliasing={{0}: (2, {}), {1}: (3, {}), {2}: (4, {}), {3}: (5, {}), {4}... | custom-call | tf_op jit(solution)/shard_map/pallas_call | solution.py:584
  12.8 2.1 %collective-permute-start.5 = (f32[5,8,256]{2,1,0:T(8,128)S(1)}, f32[5,8,256]{2,1,0:T(8,128)S(1)}, u32[]{:S(2)}, u32[]{:S(2)}) collective-permute-start(f32[5,8,256]{2,1,0:T(8,128)S(1)} %get-tuple-element.55), channel_id=1, source_target_pairs={{0,1},{1,0},{2,3},{3,2},{4,5},{5,4},{6,7},{7,6},{8,9},{9,8},{10,11... | collective-permute-start | bytes 122888 | tf_op jit(solution)/shard_map/ppermute | solution.py:628
  15.0 2.1 %collective-permute-start.6 = (f32[1,256]{1,0:T(1,128)S(1)}, f32[1,256]{1,0:T(1,128)S(1)}, u32[]{:S(2)}, u32[]{:S(2)}) collective-permute-start(f32[1,256]{1,0:T(1,128)S(1)} %get-tuple-element.56), channel_id=1, source_target_pairs={{0,18},{1,19},{2,16},{3,17},{4,22},{5,23},{6,20},{7,21},{8,26},{9,... | collective-permute-start | bytes 3080 | tf_op jit(solution)/shard_map/ppermute | solution.py:651
  17.0 1.8 %collective-permute-done.6 = f32[1,256]{1,0:T(1,128)S(1)} collective-permute-done((f32[1,256]{1,0:T(1,128)S(1)}, f32[1,256]{1,0:T(1,128)S(1)}, u32[]{:S(2)}, u32[]{:S(2)}) %collective-permute-start.6) | collective-permute-done | bytes 1056 | tf_op jit(solution)/shard_map/ppermute | solution.py:651
  18.9 0.0 collective-permute-done.5.t
  18.9 0.2 collective-permute-start.7
  19.1 0.9 %collective-permute-start.8 = (f32[168,256]{1,0:T(8,128)S(1)}, f32[168,256]{1,0:T(8,128)S(1)}, u32[]{:S(2)}, u32[]{:S(2)}) collective-permute-start(f32[168,256]{1,0:T(8,128)S(1)} %get-tuple-element.61), channel_id=1, source_target_pairs={{0,1},{1,0},{2,4},{3,5},{4,2},{5,3},{6,8},{7,9},{8,6},{9,7},{10,12... | collective-permute-start | bytes 516104 | tf_op jit(solution)/shard_map/ppermute | solution.py:634
  20.0 0.4 %collective-permute-done.7.e = f32[176,256]{1,0:T(8,128)S(1)} collective-permute-done((f32[176,256]{1,0:T(8,128)S(1)}, f32[176,256]{1,0:T(8,128)S(1)}, u32[]{:S(2)}, u32[]{:S(2)}) %collective-permute-start.7) | collective-permute-done | bytes 180256 | tf_op jit(solution)/shard_map/ppermute | solution.py:634
  20.4 1.2 %collective-permute-start.9 = (f32[1,256]{1,0:T(1,128)S(1)}, f32[1,256]{1,0:T(1,128)S(1)}, u32[]{:S(2)}, u32[]{:S(2)}) collective-permute-start(f32[1,256]{1,0:T(1,128)S(1)} %slice_add_fusion), channel_id=1, source_target_pairs={{0,3},{1,2},{2,1},{3,0},{4,7},{5,6},{6,5},{7,4},{8,11},{9,10},{10,... | collective-permute-start | bytes 3080 | tf_op jit(solution)/shard_map/ppermute | solution.py:651
  21.5 0.0 copy-done
  21.5 1.2 %shard_map.88 = (f32[19,2,16,256]{3,2,1,0:T(8,128)}, f32[19,2,16,256]{3,2,1,0:T(8,128)}, f32[2,16,256]{2,1,0:T(8,128)S(1)}) custom-call(s32[1]{0:T(128)} %bitcast.parity_ref, f32[19,2,16,256]{3,2,1,0:T(8,128)S(1)} %get-tuple-element.49.post, f32[19,2,16,256]{3,2,1,0:T(8,128)S(1)} %get-tuple-element.50.adj, f32[2,16,256]{2,1,0:T(8,128)S(1)} %get-tuple-element.37.flags, ...), custom_call_target="tpu_custom_call" | custom-call | tf_op jit(solution)/shard_map/pallas_call | solution.py:584
  22.8 0.6 %collective-permute-done.9 = f32[1,256]{1,0:T(1,128)S(1)} collective-permute-done((f32[1,256]{1,0:T(1,128)S(1)}, f32[1,256]{1,0:T(1,128)S(1)}, u32[]{:S(2)}, u32[]{:S(2)}) %collective-permute-start.9) | collective-permute-done | bytes 1056 | tf_op jit(solution)/shard_map/ppermute | solution.py:651
  23.4 2.3 %collective-permute-start.12 = (f32[1,256]{1,0:T(1,128)S(1)}, f32[1,256]{1,0:T(1,128)S(1)}, u32[]{:S(2)}, u32[]{:S(2)}) collective-permute-start(f32[1,256]{1,0:T(1,128)S(1)} %add.25), channel_id=1, source_target_pairs={{0,12},{1,13},{2,14},{3,15},{4,8},{5,9},{6,10},{7,11},{8,4},{9,5},... | collective-permute-start | bytes 3080 | tf_op jit(solution)/shard_map/ppermute | solution.py:651
  25.6 0.4 %collective-permute-start.11 = (f32[1,256]{1,0:T(1,128)S(1)}, f32[1,256]{1,0:T(1,128)S(1)}, u32[]{:S(2)}, u32[]{:S(2)}) collective-permute-start(f32[1,256]{1,0:T(1,128)S(1)} %add.25), channel_id=1, source_target_pairs={{0,6},{1,7},{2,4},{3,5},{4,2},{5,3},{6,0},{7,1},{8,14},{9,15},{10,... | collective-permute-start | bytes 3080 | tf_op jit(solution)/shard_map/ppermute | solution.py:651
  26.1 0.5 %collective-permute-start.10 = (f32[1,256]{1,0:T(1,128)S(1)}, f32[1,256]{1,0:T(1,128)S(1)}, u32[]{:S(2)}, u32[]{:S(2)}) collective-permute-start(f32[1,256]{1,0:T(1,128)S(1)} %add.25), channel_id=1, source_target_pairs={{0,10},{1,11},{2,8},{3,9},{4,14},{5,15},{6,12},{7,13},{8,2},{9,3},... | collective-permute-start | bytes 3080 | tf_op jit(solution)/shard_map/ppermute | solution.py:651
  26.6 0.0 collective-permute-done.8.o
  26.6 1.9 %shard_map.89 = (f32[19,2,16,256]{3,2,1,0:T(8,128)}, f32[19,2,16,256]{3,2,1,0:T(8,128)}, f32[2,16,256]{2,1,0:T(8,128)}) custom-call(s32[1]{0:T(128)} %bitcast.parity_ref, s32[1]{0:T(128)} %bitcast.1.real_ref, f32[19,2,16,256]{3,2,1,0:T(8,128)} %get-tuple-element.58.final_near, ...), custom_call_target="tpu_custom_call", output_to_operand_aliasing={{0}: (2, {}), {1}: (3, {})} | custom-call | tf_op jit(solution)/shard_map/pallas_call | solution.py:584
  28.4 0.0 collective-permute-done.12
  28.4 0.2 collective-permute-done.11
  28.6 0.4 %collective-permute-done.10 = f32[1,256]{1,0:T(1,128)S(1)} collective-permute-done((f32[1,256]{1,0:T(1,128)S(1)}, f32[1,256]{1,0:T(1,128)S(1)}, u32[]{:S(2)}, u32[]{:S(2)}) %collective-permute-start.10) | collective-permute-done | bytes 1056 | tf_op jit(solution)/shard_map/ppermute | solution.py:651
  29.1 0.5 %fusion.1 = f32[8]{0:T(128)} fusion(f32[1,256]{1,0:T(1,128)S(1)} %collective-permute-done.12, f32[1,256]{1,0:T(1,128)S(1)} %collective-permute-done.11, f32[1,256]{1,0:T(1,128)S(1)} %collective-permute-done.10, f32[1,256]{1,0:T(1,128)S(1)} %add.25), kind=kLoop, calls=%fused_computation.4 | loop fusion | flops 24 | bytes 160 | tf_op jit(solution)/shard_map/squeeze | solution.py:750
  (4 shorter events, 0.0 us)
Async XLA Ops:
  0.6 10.5 %copy-start.1 = (f32[19,2,16,256]{3,2,1,0:T(8,128)S(1)}, f32[19,2,16,256]{3,2,1,0:T(8,128)}, u32[]{:S(2)}) copy-start(f32[19,2,16,256]{3,2,1,0:T(8,128)} %seed.3) | copy-start | bytes 1867780
  0.7 10.5 %copy-start.2 = (f32[2,16,256]{2,1,0:T(8,128)S(1)}, f32[2,16,256]{2,1,0:T(8,128)}, u32[]{:S(2)}) copy-start(f32[2,16,256]{2,1,0:T(8,128)} %porous.7) | copy-start | bytes 98308
  0.7 10.5 %copy-start.3 = (s32[2,16,256]{2,1,0:T(8,128)S(1)}, s32[2,16,256]{2,1,0:T(8,128)}, u32[]{:S(2)}) copy-start(s32[2,16,256]{2,1,0:T(8,128)} %types.7) | copy-start | bytes 98308
  0.7 10.5 %copy-start.4 = (s32[2,16,256]{2,1,0:T(8,128)S(1)}, s32[2,16,256]{2,1,0:T(8,128)}, u32[]{:S(2)}) copy-start(s32[2,16,256]{2,1,0:T(8,128)} %regions.7) | copy-start | bytes 98308
  2.4 8.8 %collective-permute-start = (f32[240,256]{1,0:T(8,128)S(1)}, f32[240,256]{1,0:T(8,128)S(1)}, u32[]{:S(2)}, u32[]{:S(2)}) collective-permute-start(f32[240,256]{1,0:T(8,128)S(1)} %get-tuple-element.38), channel_id=1, source_target_pairs={{0,2},{1,3},{2,0},{3,1},{4,6},{5,7},{6,4},{7,5},{8,10},{9,11},{10,... | collective-permute-start | bytes 737288 | tf_op jit(solution)/shard_map/ppermute | solution.py:634
  2.9 9.1 %collective-permute-start.3 = (f32[240,256]{1,0:T(8,128)S(1)}, f32[240,256]{1,0:T(8,128)S(1)}, u32[]{:S(2)}, u32[]{:S(2)}) collective-permute-start(f32[240,256]{1,0:T(8,128)S(1)} %get-tuple-element.47), channel_id=1, source_target_pairs={{0,1},{1,0},{2,4},{3,5},{4,2},{5,3},{6,8},{7,9},{8,6},{9,7},{10,12... | collective-permute-start | bytes 737288 | tf_op jit(solution)/shard_map/ppermute | solution.py:634
  5.5 5.7 %collective-permute-start.1 = (f32[8,8,256]{2,1,0:T(8,128)S(1)}, f32[8,8,256]{2,1,0:T(8,128)S(1)}, u32[]{:S(2)}, u32[]{:S(2)}) collective-permute-start(f32[8,8,256]{2,1,0:T(8,128)S(1)} %get-tuple-element.39), channel_id=1, source_target_pairs={{0,1},{1,0},{2,3},{3,2},{4,5},{5,4},{6,7},{7,6},{8,9},{9,8},{10,11... | collective-permute-start | bytes 196616 | tf_op jit(solution)/shard_map/ppermute | solution.py:628
  5.5 5.3 %collective-permute-start.2 = (f32[8,256]{1,0:T(8,128)S(1)}, f32[8,256]{1,0:T(8,128)S(1)}, u32[]{:S(2)}, u32[]{:S(2)}) collective-permute-start(f32[8,256]{1,0:T(8,128)S(1)} %get-tuple-element.40), channel_id=1, source_target_pairs={{0,3},{1,2},{2,1},{3,0},{4,7},{5,6},{6,5},{7,4},{8,11},{9,10},{10,... | collective-permute-start | bytes 24584 | tf_op jit(solution)/shard_map/ppermute | solution.py:639
  6.9 5.1 %collective-permute-start.4 = (f32[8,256]{1,0:T(8,128)S(1)}, f32[8,256]{1,0:T(8,128)S(1)}, u32[]{:S(2)}, u32[]{:S(2)}) collective-permute-start(f32[8,256]{1,0:T(8,128)S(1)} %get-tuple-element.48), channel_id=1, source_target_pairs={{0,1},{1,0},{2,5},{3,4},{4,3},{5,2},{6,9},{7,8},{8,7},{9,6},{10,13... | collective-permute-start | bytes 24584 | tf_op jit(solution)/shard_map/ppermute | solution.py:639
  12.0 9.5 %copy-start = (f32[19,2,16,256]{3,2,1,0:T(8,128)S(1)}, f32[19,2,16,256]{3,2,1,0:T(8,128)}, u32[]{:S(2)}) copy-start(f32[19,2,16,256]{3,2,1,0:T(8,128)} %pops.3) | copy-start | bytes 1867780
  12.8 6.0 %collective-permute-start.5 = (f32[5,8,256]{2,1,0:T(8,128)S(1)}, f32[5,8,256]{2,1,0:T(8,128)S(1)}, u32[]{:S(2)}, u32[]{:S(2)}) collective-permute-start(f32[5,8,256]{2,1,0:T(8,128)S(1)} %get-tuple-element.55), channel_id=1, source_target_pairs={{0,1},{1,0},{2,3},{3,2},{4,5},{5,4},{6,7},{7,6},{8,9},{9,8},{10,11... | collective-permute-start | bytes 122888 | tf_op jit(solution)/shard_map/ppermute | solution.py:628
  15.0 3.9 %collective-permute-start.6 = (f32[1,256]{1,0:T(1,128)S(1)}, f32[1,256]{1,0:T(1,128)S(1)}, u32[]{:S(2)}, u32[]{:S(2)}) collective-permute-start(f32[1,256]{1,0:T(1,128)S(1)} %get-tuple-element.56), channel_id=1, source_target_pairs={{0,18},{1,19},{2,16},{3,17},{4,22},{5,23},{6,20},{7,21},{8,26},{9,... | collective-permute-start | bytes 3080 | tf_op jit(solution)/shard_map/ppermute | solution.py:651
  18.9 1.5 %collective-permute-start.7 = (f32[176,256]{1,0:T(8,128)S(1)}, f32[176,256]{1,0:T(8,128)S(1)}, u32[]{:S(2)}, u32[]{:S(2)}) collective-permute-start(f32[176,256]{1,0:T(8,128)S(1)} %get-tuple-element.57), channel_id=1, source_target_pairs={{0,2},{1,3},{2,0},{3,1},{4,6},{5,7},{6,4},{7,5},{8,10},{9,11},{10,... | collective-permute-start | bytes 540680 | tf_op jit(solution)/shard_map/ppermute | solution.py:634
  19.1 7.5 %collective-permute-start.8 = (f32[168,256]{1,0:T(8,128)S(1)}, f32[168,256]{1,0:T(8,128)S(1)}, u32[]{:S(2)}, u32[]{:S(2)}) collective-permute-start(f32[168,256]{1,0:T(8,128)S(1)} %get-tuple-element.61), channel_id=1, source_target_pairs={{0,1},{1,0},{2,4},{3,5},{4,2},{5,3},{6,8},{7,9},{8,6},{9,7},{10,12... | collective-permute-start | bytes 516104 | tf_op jit(solution)/shard_map/ppermute | solution.py:634
  20.4 3.0 %collective-permute-start.9 = (f32[1,256]{1,0:T(1,128)S(1)}, f32[1,256]{1,0:T(1,128)S(1)}, u32[]{:S(2)}, u32[]{:S(2)}) collective-permute-start(f32[1,256]{1,0:T(1,128)S(1)} %slice_add_fusion), channel_id=1, source_target_pairs={{0,3},{1,2},{2,1},{3,0},{4,7},{5,6},{6,5},{7,4},{8,11},{9,10},{10,... | collective-permute-start | bytes 3080 | tf_op jit(solution)/shard_map/ppermute | solution.py:651
  23.4 5.1 %collective-permute-start.12 = (f32[1,256]{1,0:T(1,128)S(1)}, f32[1,256]{1,0:T(1,128)S(1)}, u32[]{:S(2)}, u32[]{:S(2)}) collective-permute-start(f32[1,256]{1,0:T(1,128)S(1)} %add.25), channel_id=1, source_target_pairs={{0,12},{1,13},{2,14},{3,15},{4,8},{5,9},{6,10},{7,11},{8,4},{9,5},... | collective-permute-start | bytes 3080 | tf_op jit(solution)/shard_map/ppermute | solution.py:651
  25.6 3.0 %collective-permute-start.11 = (f32[1,256]{1,0:T(1,128)S(1)}, f32[1,256]{1,0:T(1,128)S(1)}, u32[]{:S(2)}, u32[]{:S(2)}) collective-permute-start(f32[1,256]{1,0:T(1,128)S(1)} %add.25), channel_id=1, source_target_pairs={{0,6},{1,7},{2,4},{3,5},{4,2},{5,3},{6,0},{7,1},{8,14},{9,15},{10,... | collective-permute-start | bytes 3080 | tf_op jit(solution)/shard_map/ppermute | solution.py:651
  26.1 3.0 %collective-permute-start.10 = (f32[1,256]{1,0:T(1,128)S(1)}, f32[1,256]{1,0:T(1,128)S(1)}, u32[]{:S(2)}, u32[]{:S(2)}) collective-permute-start(f32[1,256]{1,0:T(1,128)S(1)} %add.25), channel_id=1, source_target_pairs={{0,10},{1,11},{2,8},{3,9},{4,14},{5,15},{6,12},{7,13},{8,2},{9,3},... | collective-permute-start | bytes 3080 | tf_op jit(solution)/shard_map/ppermute | solution.py:651

commit v8 on v7

--- a/solution.py
+++ b/solution.py
@@ -540,8 +540,7 @@
         stream_adjoint_row(fields, a, flags[a], around, back)
         chunks([a], porous.shape, body)
         send(result, hbm[1], a)
-    for copy in stores:
-        copy.wait()
+    return stores
 
 
 def third_near_kernel(
@@ -551,10 +550,12 @@
     def run(parity):
         fields = Fields(SECOND, {POST: post, ADJ: adj}, parity, e=e, t=t)
         rows, _ = near_rows(parity, porous.shape[0])
-        third_rows(
+        stores = third_rows(
             fields, rows, (porous, types, regions), (around, flags, pops, sens_one),
             (final_hbm, result_hbm), sens, (final, result, back), sems,
         )
+        for copy in stores:
+            copy.wait()
 
     by_parity(parity_ref, run)
 
@@ -562,17 +563,21 @@
 def third_far_kernel(
     parity_ref, real_ref, final_near, result_near, sens_near,
     post, adj, flags, around, pops, porous, types, regions, sens_one, o, t,
-    final_hbm, result_hbm, sens, final, result, back, sems,
+    final_hbm, result_hbm, sens_hbm, final, result, back, sems, sens,
 ):
     def run(parity):
         fields = Fields(SECOND, {POST: post, ADJ: adj}, parity, o=o, real=real_ref[0], t=t)
         rows, row = near_rows(parity, porous.shape[0])
         for a in rows:
             sens[a] = sens_near[a]
-        third_rows(
+        stores = third_rows(
             fields, [row], (porous, types, regions), (around, flags, pops, sens_one),
             (final_hbm, result_hbm), sens, (final, result, back), sems,
         )
+        stores.append(pltpu.make_async_copy(sens, sens_hbm, sems.at[len(stores)]))
+        stores[-1].start()
+        for copy in stores:
+            copy.wait()
 
     by_parity(parity_ref, run)
 
@@ -671,7 +676,7 @@
     post, factors, e, o, t, ed, od, flags = call(
         first_kernel,
         [pltpu.SMEM] + [HBM] * 5,
-        [(pops, f32, VMEM), (pops, f32, VMEM)] + [axial(FIRST, 0)] * 2 + azimuthal(FIRST)
+        [(pops, f32, VMEM), (pops, f32, VMEM)] + [axial(FIRST, 0), axial(FIRST, 8)] + azimuthal(FIRST)
         + [((8, wide), f32, VMEM)] * 2 + [(cells_, f32, VMEM)],
         [VMEM(x.shape, x.dtype) for x in inputs]
         + [VMEM((4,) + cells_, f32), pltpu.SemaphoreType.DMA((4 + cells_[0],))],
@@ -734,7 +739,7 @@
             totals = totals + from_partner(totals, *flip)
         if last:
             totals, _ = lax.optimization_barrier((totals, near[2]))
-            one, two = last
+            two, one = last
             pair = totals + from_partner(totals, one, 0)
             totals = pair + (from_partner(totals, two, 0) + from_partner(totals, one ^ two, 0))
     else:
@@ -742,8 +747,8 @@
     final, adjoint, sensitivity = call(
         third_far_kernel,
         [pltpu.SMEM] * 2 + [HBM] * 2 + [VMEM] * 12,
-        stored,
-        third_scratch,
+        stored[:2] + [(cells_, f32, HBM)],
+        third_scratch + [VMEM(cells_, f32)],
         *place, *near, *inside, o, t_near,
         aliases={2: 0, 3: 1},
     )

time: 29.7 us -> 29.5 us (level)
  waiting for transfers between devices: 6.09 us -> 7.28 us
  starting transfers between devices: 15.8 us -> 15.1 us
  Pallas kernels: 6.4 us -> 5.71 us
    ppermute x2, starting transfers between devices: 2.88 us -> 1.35 us  [send(): return lax.ppermute(x, ('ax', 'az'), axial_pairs(flip, shift))]
    ppermute x2, starting transfers between devices: 2.23 us -> 3.58 us  [send(): return lax.ppermute(x, 'az', [(i, (i + shift) % size) for i in range(size)])]
    ppermute x5, waiting for transfers between devices: 3.02 us -> 3.75 us  [from_partner(): return lax.ppermute(x, ('ax', 'az'), pairs)]
    pallas_call x6, Pallas kernels: 6.4 us -> 5.71 us  [call(): pl.pallas_call(body, out_shape=[jax.ShapeDtypeStruct(shape, dtype) for sh...]
    ppermute x4, waiting for transfers between devices: 0.36 us -> 0.73 us  [send_axial(): return lax.ppermute(message, ('ax', 'az'), axial_pairs(flip))]
    ppermute x4, starting transfers between devices: 4.24 us -> 3.88 us  [send_axial(): return lax.ppermute(message, ('ax', 'az'), axial_pairs(flip))]
  transfers between devices with their start and end apart: 13 -> 13, of which waited for: 7 -> 7; matrix products, arithmetic and copies ran while one was open for 0% -> 0% of each run, Pallas kernels for 13% -> 11%
where the time goes in v8:
time: 29.5 us; the launch traced here: 29.3 us
  starting transfers between devices  15.1 us (51%)
  waiting for transfers between devices  7.28 us (25%)
  Pallas kernels  5.71 us (19%)
  between operations  0.75 us (3%)
  other arithmetic  0.52 us (2%)
    ppermute x5, starting transfers between devices, from_partner(): return lax.ppermute(x, ('ax', 'az'), pairs)  6.25 us
    pallas_call x6, Pallas kernels, call(): pl.pallas_call(body, out_shape=[jax.ShapeDtypeStruct(shape, dtype) for sh...  5.71 us
    ppermute x4, starting transfers between devices, send_axial(): return lax.ppermute(message, ('ax', 'az'), axial_pairs(flip))  3.88 us
    ppermute x5, waiting for transfers between devices, from_partner(): return lax.ppermute(x, ('ax', 'az'), pairs)  3.75 us
    ppermute x2, starting transfers between devices, send(): return lax.ppermute(x, 'az', [(i, (i + shift) % size) for i in range(size)])  3.58 us
    ppermute x2, waiting for transfers between devices, send(): return lax.ppermute(x, ('ax', 'az'), axial_pairs(flip, shift))  2.42 us
    ppermute x2, starting transfers between devices, send(): return lax.ppermute(x, ('ax', 'az'), axial_pairs(flip, shift))  1.35 us
    ppermute x4, waiting for transfers between devices, send_axial(): return lax.ppermute(message, ('ax', 'az'), axial_pairs(flip))  0.73 us
  transfers between devices with their start and end apart: 13, of which 7 were waited for; matrix products, arithmetic and copies ran while one was open for 0% of the time, Pallas kernels for 11%

profile of v8, /device:TPU:0, one launch (start us, length us, event | category | flops | bytes accessed | tf_op | source)
XLA Modules:
  0.0 29.3 jit_solution(13241084787200104738)
XLA Ops:
  0.6 0.0 copy-start.1
  0.7 0.0 copy-start.2
  0.7 0.0 copy-start.3
  0.7 0.0 copy-start.4
  0.7 1.7 %shard_map.84 = (f32[19,2,16,256]{3,2,1,0:T(8,128)S(1)}, f32[19,2,16,256]{3,2,1,0:T(8,128)S(1)}, f32[240,256]{1,0:T(8,128)S(1)}, f32[248,256]{1,0:T(8,128)S(1)},...) custom-call(s32[1]{0:T(128)} %bitcast.parity_ref, ...), custom_call_target="tpu_custom_call" | custom-call | tf_op jit(solution)/shard_map/pallas_call | solution.py:589
  2.4 3.0 %collective-permute-start.3 = (f32[248,256]{1,0:T(8,128)S(1)}, f32[248,256]{1,0:T(8,128)S(1)}, u32[]{:S(2)}, u32[]{:S(2)}) collective-permute-start(f32[248,256]{1,0:T(8,128)S(1)} %get-tuple-element.47), channel_id=1, source_target_pairs={{0,1},{1,0},{2,4},{3,5},{4,2},{5,3},{6,8},{7,9},{8,6},{9,7},{10,12... | collective-permute-start | bytes 761864 | tf_op jit(solution)/shard_map/ppermute | solution.py:639
  5.4 0.1 collective-permute-start
  5.5 1.5 %collective-permute-start.1 = (f32[8,8,256]{2,1,0:T(8,128)S(1)}, f32[8,8,256]{2,1,0:T(8,128)S(1)}, u32[]{:S(2)}, u32[]{:S(2)}) collective-permute-start(f32[8,8,256]{2,1,0:T(8,128)S(1)} %get-tuple-element.39), channel_id=1, source_target_pairs={{0,1},{1,0},{2,3},{3,2},{4,5},{5,4},{6,7},{7,6},{8,9},{9,8},{10,11... | collective-permute-start | bytes 196616 | tf_op jit(solution)/shard_map/ppermute | solution.py:633
  7.0 0.3 collective-permute-start.2
  7.3 1.1 %collective-permute-start.4 = (f32[8,256]{1,0:T(8,128)S(1)}, f32[8,256]{1,0:T(8,128)S(1)}, u32[]{:S(2)}, u32[]{:S(2)}) collective-permute-start(f32[8,256]{1,0:T(8,128)S(1)} %get-tuple-element.48), channel_id=1, source_target_pairs={{0,1},{1,0},{2,5},{3,4},{4,3},{5,2},{6,9},{7,8},{8,7},{9,6},{10,13... | collective-permute-start | bytes 24584 | tf_op jit(solution)/shard_map/ppermute | solution.py:644
  8.4 2.4 %collective-permute-done.2.ed = f32[8,256]{1,0:T(8,128)S(1)} collective-permute-done((f32[8,256]{1,0:T(8,128)S(1)}, f32[8,256]{1,0:T(8,128)S(1)}, u32[]{:S(2)}, u32[]{:S(2)}) %collective-permute-start.2) | collective-permute-done | bytes 8224 | tf_op jit(solution)/shard_map/ppermute | solution.py:644
  10.8 0.4 %collective-permute-done.1.t = f32[8,8,256]{2,1,0:T(8,128)S(1)} collective-permute-done((f32[8,8,256]{2,1,0:T(8,128)S(1)}, f32[8,8,256]{2,1,0:T(8,128)S(1)}, u32[]{:S(2)}, u32[]{:S(2)}) %collective-permute-start.1) | collective-permute-done | bytes 65568 | tf_op jit(solution)/shard_map/ppermute | solution.py:633
  11.1 0.0 collective-permute-done.e
  11.2 0.0 copy-done.1
  11.2 0.0 copy-done.2
  11.2 0.0 copy-done.3
  11.2 0.0 copy-done.4
  11.2 0.8 %shard_map.85 = (f32[19,2,16,256]{3,2,1,0:T(8,128)S(1)}, f32[19,2,16,256]{3,2,1,0:T(8,128)S(1)}, f32[2,16,256]{2,1,0:T(8,128)S(1)}, f32[18,2,16,256]{3,2,1,0:T(8...) custom-call(s32[1]{0:T(128)} %bitcast.parity_ref, ...), custom_call_target="tpu_custom_call" | custom-call | tf_op jit(solution)/shard_map/pallas_call | solution.py:589
  12.0 0.0 collective-permute-done.4.od
  12.0 0.0 collective-permute-done.3.o
  12.0 0.0 copy-start
  12.0 0.8 %shard_map.86 = (f32[19,2,16,256]{3,2,1,0:T(8,128)S(1)}, f32[19,2,16,256]{3,2,1,0:T(8,128)S(1)}, f32[2,16,256]{2,1,0:T(8,128)S(1)}, f32[18,2,16,256]{3,2,1,0:T(8...) custom-call(s32[1]{0:T(128)} %bitcast.parity_ref, ...), custom_call_target="tpu_custom_call", output_to_operand_aliasing={{0}: (2, {}), {1}: (3, {}), {2}: (4, {}), {3}: (5, {}), {4}... | custom-call | tf_op jit(solution)/shard_map/pallas_call | solution.py:589
  12.8 2.1 %collective-permute-start.5 = (f32[5,8,256]{2,1,0:T(8,128)S(1)}, f32[5,8,256]{2,1,0:T(8,128)S(1)}, u32[]{:S(2)}, u32[]{:S(2)}) collective-permute-start(f32[5,8,256]{2,1,0:T(8,128)S(1)} %get-tuple-element.55), channel_id=1, source_target_pairs={{0,1},{1,0},{2,3},{3,2},{4,5},{5,4},{6,7},{7,6},{8,9},{9,8},{10,11... | collective-permute-start | bytes 122888 | tf_op jit(solution)/shard_map/ppermute | solution.py:633
  14.8 1.7 %collective-permute-start.6 = (f32[1,256]{1,0:T(1,128)S(1)}, f32[1,256]{1,0:T(1,128)S(1)}, u32[]{:S(2)}, u32[]{:S(2)}) collective-permute-start(f32[1,256]{1,0:T(1,128)S(1)} %get-tuple-element.56), channel_id=1, source_target_pairs={{0,18},{1,19},{2,16},{3,17},{4,22},{5,23},{6,20},{7,21},{8,26},{9,... | collective-permute-start | bytes 3080 | tf_op jit(solution)/shard_map/ppermute | solution.py:656
  16.5 2.2 %collective-permute-done.6 = f32[1,256]{1,0:T(1,128)S(1)} collective-permute-done((f32[1,256]{1,0:T(1,128)S(1)}, f32[1,256]{1,0:T(1,128)S(1)}, u32[]{:S(2)}, u32[]{:S(2)}) %collective-permute-start.6) | collective-permute-done | bytes 1056 | tf_op jit(solution)/shard_map/ppermute | solution.py:656
  18.7 0.0 collective-permute-done.5.t
  18.8 0.2 collective-permute-start.7
  18.9 0.6 %collective-permute-start.8 = (f32[168,256]{1,0:T(8,128)S(1)}, f32[168,256]{1,0:T(8,128)S(1)}, u32[]{:S(2)}, u32[]{:S(2)}) collective-permute-start(f32[168,256]{1,0:T(8,128)S(1)} %get-tuple-element.61), channel_id=1, source_target_pairs={{0,1},{1,0},{2,4},{3,5},{4,2},{5,3},{6,8},{7,9},{8,6},{9,7},{10,12... | collective-permute-start | bytes 516104 | tf_op jit(solution)/shard_map/ppermute | solution.py:639
  19.5 0.7 %collective-permute-done.7.e = f32[176,256]{1,0:T(8,128)S(1)} collective-permute-done((f32[176,256]{1,0:T(8,128)S(1)}, f32[176,256]{1,0:T(8,128)S(1)}, u32[]{:S(2)}, u32[]{:S(2)}) %collective-permute-start.7) | collective-permute-done | bytes 180256 | tf_op jit(solution)/shard_map/ppermute | solution.py:639
  20.2 1.4 %collective-permute-start.9 = (f32[1,256]{1,0:T(1,128)S(1)}, f32[1,256]{1,0:T(1,128)S(1)}, u32[]{:S(2)}, u32[]{:S(2)}) collective-permute-start(f32[1,256]{1,0:T(1,128)S(1)} %slice_add_fusion), channel_id=1, source_target_pairs={{0,3},{1,2},{2,1},{3,0},{4,7},{5,6},{6,5},{7,4},{8,11},{9,10},{10,... | collective-permute-start | bytes 3080 | tf_op jit(solution)/shard_map/ppermute | solution.py:656
  21.6 0.0 copy-done
  21.6 1.2 %shard_map.88 = (f32[19,2,16,256]{3,2,1,0:T(8,128)}, f32[19,2,16,256]{3,2,1,0:T(8,128)}, f32[2,16,256]{2,1,0:T(8,128)S(1)}) custom-call(s32[1]{0:T(128)} %bitcast.parity_ref, f32[19,2,16,256]{3,2,1,0:T(8,128)S(1)} %get-tuple-element.49.post, f32[19,2,16,256]{3,2,1,0:T(8,128)S(1)} %get-tuple-element.50.adj, f32[2,16,256]{2,1,0:T(8,128)S(1)} %get-tuple-element.37.flags, ...), custom_call_target="tpu_custom_call" | custom-call | tf_op jit(solution)/shard_map/pallas_call | solution.py:589
  22.8 0.4 %collective-permute-done.9 = f32[1,256]{1,0:T(1,128)S(1)} collective-permute-done((f32[1,256]{1,0:T(1,128)S(1)}, f32[1,256]{1,0:T(1,128)S(1)}, u32[]{:S(2)}, u32[]{:S(2)}) %collective-permute-start.9) | collective-permute-done | bytes 1056 | tf_op jit(solution)/shard_map/ppermute | solution.py:656
  23.2 2.4 %collective-permute-start.12 = (f32[1,256]{1,0:T(1,128)S(1)}, f32[1,256]{1,0:T(1,128)S(1)}, u32[]{:S(2)}, u32[]{:S(2)}) collective-permute-start(f32[1,256]{1,0:T(1,128)S(1)} %add.25), channel_id=1, source_target_pairs={{0,12},{1,13},{2,14},{3,15},{4,8},{5,9},{6,10},{7,11},{8,4},{9,5},... | collective-permute-start | bytes 3080 | tf_op jit(solution)/shard_map/ppermute | solution.py:656
  25.6 0.2 collective-permute-start.11
  25.8 0.6 %collective-permute-start.10 = (f32[1,256]{1,0:T(1,128)S(1)}, f32[1,256]{1,0:T(1,128)S(1)}, u32[]{:S(2)}, u32[]{:S(2)}) collective-permute-start(f32[1,256]{1,0:T(1,128)S(1)} %add.25), channel_id=1, source_target_pairs={{0,6},{1,7},{2,4},{3,5},{4,2},{5,3},{6,0},{7,1},{8,14},{9,15},{10,... | collective-permute-start | bytes 3080 | tf_op jit(solution)/shard_map/ppermute | solution.py:656
  26.5 0.0 collective-permute-done.8.o
  26.5 1.2 %shard_map.89 = (f32[19,2,16,256]{3,2,1,0:T(8,128)}, f32[19,2,16,256]{3,2,1,0:T(8,128)}, f32[2,16,256]{2,1,0:T(8,128)}) custom-call(s32[1]{0:T(128)} %bitcast.parity_ref, s32[1]{0:T(128)} %bitcast.1.real_ref, f32[19,2,16,256]{3,2,1,0:T(8,128)} %get-tuple-element.58.final_near, ...), custom_call_target="tpu_custom_call", output_to_operand_aliasing={{0}: (2, {}), {1}: (3, {})} | custom-call | tf_op jit(solution)/shard_map/pallas_call | solution.py:589
  27.7 0.0 collective-permute-done.12
  27.7 0.9 %collective-permute-done.11 = f32[1,256]{1,0:T(1,128)S(1)} collective-permute-done((f32[1,256]{1,0:T(1,128)S(1)}, f32[1,256]{1,0:T(1,128)S(1)}, u32[]{:S(2)}, u32[]{:S(2)}) %collective-permute-start.11) | collective-permute-done | bytes 1056 | tf_op jit(solution)/shard_map/ppermute | solution.py:656
  28.6 0.2 collective-permute-done.10
  28.8 0.5 %fusion.1 = f32[8]{0:T(128)} fusion(f32[1,256]{1,0:T(1,128)S(1)} %collective-permute-done.12, f32[1,256]{1,0:T(1,128)S(1)} %collective-permute-done.11, f32[1,256]{1,0:T(1,128)S(1)} %collective-permute-done.10, f32[1,256]{1,0:T(1,128)S(1)} %add.25), kind=kLoop, calls=%fused_computation.4 | loop fusion | flops 24 | bytes 160 | tf_op jit(solution)/shard_map/squeeze | solution.py:755
  (4 shorter events, 0.0 us)
Async XLA Ops:
  0.6 10.5 %copy-start.1 = (f32[19,2,16,256]{3,2,1,0:T(8,128)S(1)}, f32[19,2,16,256]{3,2,1,0:T(8,128)}, u32[]{:S(2)}) copy-start(f32[19,2,16,256]{3,2,1,0:T(8,128)} %seed.3) | copy-start | bytes 1867780
  0.7 10.5 %copy-start.2 = (f32[2,16,256]{2,1,0:T(8,128)S(1)}, f32[2,16,256]{2,1,0:T(8,128)}, u32[]{:S(2)}) copy-start(f32[2,16,256]{2,1,0:T(8,128)} %porous.7) | copy-start | bytes 98308
  0.7 10.5 %copy-start.3 = (s32[2,16,256]{2,1,0:T(8,128)S(1)}, s32[2,16,256]{2,1,0:T(8,128)}, u32[]{:S(2)}) copy-start(s32[2,16,256]{2,1,0:T(8,128)} %types.7) | copy-start | bytes 98308
  0.7 10.5 %copy-start.4 = (s32[2,16,256]{2,1,0:T(8,128)S(1)}, s32[2,16,256]{2,1,0:T(8,128)}, u32[]{:S(2)}) copy-start(s32[2,16,256]{2,1,0:T(8,128)} %regions.7) | copy-start | bytes 98308
  2.4 9.6 %collective-permute-start.3 = (f32[248,256]{1,0:T(8,128)S(1)}, f32[248,256]{1,0:T(8,128)S(1)}, u32[]{:S(2)}, u32[]{:S(2)}) collective-permute-start(f32[248,256]{1,0:T(8,128)S(1)} %get-tuple-element.47), channel_id=1, source_target_pairs={{0,1},{1,0},{2,4},{3,5},{4,2},{5,3},{6,8},{7,9},{8,6},{9,7},{10,12... | collective-permute-start | bytes 761864 | tf_op jit(solution)/shard_map/ppermute | solution.py:639
  5.4 5.8 %collective-permute-start = (f32[240,256]{1,0:T(8,128)S(1)}, f32[240,256]{1,0:T(8,128)S(1)}, u32[]{:S(2)}, u32[]{:S(2)}) collective-permute-start(f32[240,256]{1,0:T(8,128)S(1)} %get-tuple-element.38), channel_id=1, source_target_pairs={{0,2},{1,3},{2,0},{3,1},{4,6},{5,7},{6,4},{7,5},{8,10},{9,11},{10,... | collective-permute-start | bytes 737288 | tf_op jit(solution)/shard_map/ppermute | solution.py:639
  5.5 5.7 %collective-permute-start.1 = (f32[8,8,256]{2,1,0:T(8,128)S(1)}, f32[8,8,256]{2,1,0:T(8,128)S(1)}, u32[]{:S(2)}, u32[]{:S(2)}) collective-permute-start(f32[8,8,256]{2,1,0:T(8,128)S(1)} %get-tuple-element.39), channel_id=1, source_target_pairs={{0,1},{1,0},{2,3},{3,2},{4,5},{5,4},{6,7},{7,6},{8,9},{9,8},{10,11... | collective-permute-start | bytes 196616 | tf_op jit(solution)/shard_map/ppermute | solution.py:633
  7.0 3.8 %collective-permute-start.2 = (f32[8,256]{1,0:T(8,128)S(1)}, f32[8,256]{1,0:T(8,128)S(1)}, u32[]{:S(2)}, u32[]{:S(2)}) collective-permute-start(f32[8,256]{1,0:T(8,128)S(1)} %get-tuple-element.40), channel_id=1, source_target_pairs={{0,3},{1,2},{2,1},{3,0},{4,7},{5,6},{6,5},{7,4},{8,11},{9,10},{10,... | collective-permute-start | bytes 24584 | tf_op jit(solution)/shard_map/ppermute | solution.py:644
  7.3 4.7 %collective-permute-start.4 = (f32[8,256]{1,0:T(8,128)S(1)}, f32[8,256]{1,0:T(8,128)S(1)}, u32[]{:S(2)}, u32[]{:S(2)}) collective-permute-start(f32[8,256]{1,0:T(8,128)S(1)} %get-tuple-element.48), channel_id=1, source_target_pairs={{0,1},{1,0},{2,5},{3,4},{4,3},{5,2},{6,9},{7,8},{8,7},{9,6},{10,13... | collective-permute-start | bytes 24584 | tf_op jit(solution)/shard_map/ppermute | solution.py:644
  12.0 9.6 %copy-start = (f32[19,2,16,256]{3,2,1,0:T(8,128)S(1)}, f32[19,2,16,256]{3,2,1,0:T(8,128)}, u32[]{:S(2)}) copy-start(f32[19,2,16,256]{3,2,1,0:T(8,128)} %pops.3) | copy-start | bytes 1867780
  12.8 6.0 %collective-permute-start.5 = (f32[5,8,256]{2,1,0:T(8,128)S(1)}, f32[5,8,256]{2,1,0:T(8,128)S(1)}, u32[]{:S(2)}, u32[]{:S(2)}) collective-permute-start(f32[5,8,256]{2,1,0:T(8,128)S(1)} %get-tuple-element.55), channel_id=1, source_target_pairs={{0,1},{1,0},{2,3},{3,2},{4,5},{5,4},{6,7},{7,6},{8,9},{9,8},{10,11... | collective-permute-start | bytes 122888 | tf_op jit(solution)/shard_map/ppermute | solution.py:633
  14.8 3.9 %collective-permute-start.6 = (f32[1,256]{1,0:T(1,128)S(1)}, f32[1,256]{1,0:T(1,128)S(1)}, u32[]{:S(2)}, u32[]{:S(2)}) collective-permute-start(f32[1,256]{1,0:T(1,128)S(1)} %get-tuple-element.56), channel_id=1, source_target_pairs={{0,18},{1,19},{2,16},{3,17},{4,22},{5,23},{6,20},{7,21},{8,26},{9,... | collective-permute-start | bytes 3080 | tf_op jit(solution)/shard_map/ppermute | solution.py:656
  18.8 1.5 %collective-permute-start.7 = (f32[176,256]{1,0:T(8,128)S(1)}, f32[176,256]{1,0:T(8,128)S(1)}, u32[]{:S(2)}, u32[]{:S(2)}) collective-permute-start(f32[176,256]{1,0:T(8,128)S(1)} %get-tuple-element.57), channel_id=1, source_target_pairs={{0,2},{1,3},{2,0},{3,1},{4,6},{5,7},{6,4},{7,5},{8,10},{9,11},{10,... | collective-permute-start | bytes 540680 | tf_op jit(solution)/shard_map/ppermute | solution.py:639
  18.9 7.5 %collective-permute-start.8 = (f32[168,256]{1,0:T(8,128)S(1)}, f32[168,256]{1,0:T(8,128)S(1)}, u32[]{:S(2)}, u32[]{:S(2)}) collective-permute-start(f32[168,256]{1,0:T(8,128)S(1)} %get-tuple-element.61), channel_id=1, source_target_pairs={{0,1},{1,0},{2,4},{3,5},{4,2},{5,3},{6,8},{7,9},{8,6},{9,7},{10,12... | collective-permute-start | bytes 516104 | tf_op jit(solution)/shard_map/ppermute | solution.py:639
  20.2 3.0 %collective-permute-start.9 = (f32[1,256]{1,0:T(1,128)S(1)}, f32[1,256]{1,0:T(1,128)S(1)}, u32[]{:S(2)}, u32[]{:S(2)}) collective-permute-start(f32[1,256]{1,0:T(1,128)S(1)} %slice_add_fusion), channel_id=1, source_target_pairs={{0,3},{1,2},{2,1},{3,0},{4,7},{5,6},{6,5},{7,4},{8,11},{9,10},{10,... | collective-permute-start | bytes 3080 | tf_op jit(solution)/shard_map/ppermute | solution.py:656
  23.2 4.5 %collective-permute-start.12 = (f32[1,256]{1,0:T(1,128)S(1)}, f32[1,256]{1,0:T(1,128)S(1)}, u32[]{:S(2)}, u32[]{:S(2)}) collective-permute-start(f32[1,256]{1,0:T(1,128)S(1)} %add.25), channel_id=1, source_target_pairs={{0,12},{1,13},{2,14},{3,15},{4,8},{5,9},{6,10},{7,11},{8,4},{9,5},... | collective-permute-start | bytes 3080 | tf_op jit(solution)/shard_map/ppermute | solution.py:656
  25.6 3.0 %collective-permute-start.11 = (f32[1,256]{1,0:T(1,128)S(1)}, f32[1,256]{1,0:T(1,128)S(1)}, u32[]{:S(2)}, u32[]{:S(2)}) collective-permute-start(f32[1,256]{1,0:T(1,128)S(1)} %add.25), channel_id=1, source_target_pairs={{0,10},{1,11},{2,8},{3,9},{4,14},{5,15},{6,12},{7,13},{8,2},{9,3},... | collective-permute-start | bytes 3080 | tf_op jit(solution)/shard_map/ppermute | solution.py:656
  25.8 3.0 %collective-permute-start.10 = (f32[1,256]{1,0:T(1,128)S(1)}, f32[1,256]{1,0:T(1,128)S(1)}, u32[]{:S(2)}, u32[]{:S(2)}) collective-permute-start(f32[1,256]{1,0:T(1,128)S(1)} %add.25), channel_id=1, source_target_pairs={{0,6},{1,7},{2,4},{3,5},{4,2},{5,3},{6,0},{7,1},{8,14},{9,15},{10,... | collective-permute-start | bytes 3080 | tf_op jit(solution)/shard_map/ppermute | solution.py:656

commit v9 on v8

--- a/solution.py
+++ b/solution.py
@@ -388,9 +388,6 @@
         copy.start()
     for copy in loads[:3]:
         copy.wait()
-    flags[...] = jnp.where(types[...] != 1, 1.0, 0.0)
-    label = label_of(regions)
-
     def body(where):
         values = load(pops, where)
         lin = linearise(values, porous[where], types[where], regions[where])
@@ -402,6 +399,8 @@
     for a in range(rows_a):
         loads[3 + a].wait()
         chunks([a], porous.shape, body)
+    flags[...] = jnp.where(types[...] != 1, 1.0, 0.0)
+    label = label_of(regions)
     loads[-1].wait()
     own = {POST: post, ADJ: seed, FACTOR: factors, MOTION: motion, FLAG: flags}
     pack_azimuthal(FIRST, own, range(rows_a), t_out, label)

time: 29.5 us -> 29.6 us (level)
  no operation moved by 1% of the time
where the time goes in v9:
time: 29.6 us; the launch traced here: 29.4 us
  starting transfers between devices  15.1 us (51%)
  waiting for transfers between devices  7.28 us (25%)
  Pallas kernels  5.77 us (19%)
  between operations  0.75 us (3%)
  other arithmetic  0.52 us (2%)
    ppermute x5, starting transfers between devices, from_partner(): return lax.ppermute(x, ('ax', 'az'), pairs)  6.25 us
    pallas_call x6, Pallas kernels, call(): pl.pallas_call(body, out_shape=[jax.ShapeDtypeStruct(shape, dtype) for sh...  5.77 us
    ppermute x4, starting transfers between devices, send_axial(): return lax.ppermute(message, ('ax', 'az'), axial_pairs(flip))  3.88 us
    ppermute x5, waiting for transfers between devices, from_partner(): return lax.ppermute(x, ('ax', 'az'), pairs)  3.75 us
    ppermute x2, starting transfers between devices, send(): return lax.ppermute(x, 'az', [(i, (i + shift) % size) for i in range(size)])  3.58 us
    ppermute x2, waiting for transfers between devices, send(): return lax.ppermute(x, ('ax', 'az'), axial_pairs(flip, shift))  2.42 us
    ppermute x2, starting transfers between devices, send(): return lax.ppermute(x, ('ax', 'az'), axial_pairs(flip, shift))  1.35 us
    ppermute x4, waiting for transfers between devices, send_axial(): return lax.ppermute(message, ('ax', 'az'), axial_pairs(flip))  0.73 us
  transfers between devices with their start and end apart: 13, of which 7 were waited for; matrix products, arithmetic and copies ran while one was open for 0% of the time, Pallas kernels for 11%

profile of v9, /device:TPU:0, one launch (start us, length us, event | category | flops | bytes accessed | tf_op | source)
XLA Modules:
  0.0 29.4 jit_solution(15684501540602359902)
XLA Ops:
  0.6 0.0 copy-start.1
  0.7 0.0 copy-start.2
  0.7 0.0 copy-start.3
  0.7 0.0 copy-start.4
  0.7 1.7 %shard_map.84 = (f32[19,2,16,256]{3,2,1,0:T(8,128)S(1)}, f32[19,2,16,256]{3,2,1,0:T(8,128)S(1)}, f32[240,256]{1,0:T(8,128)S(1)}, f32[248,256]{1,0:T(8,128)S(1)},...) custom-call(s32[1]{0:T(128)} %bitcast.parity_ref, ...), custom_call_target="tpu_custom_call" | custom-call | tf_op jit(solution)/shard_map/pallas_call | solution.py:588
  2.4 3.0 %collective-permute-start.3 = (f32[248,256]{1,0:T(8,128)S(1)}, f32[248,256]{1,0:T(8,128)S(1)}, u32[]{:S(2)}, u32[]{:S(2)}) collective-permute-start(f32[248,256]{1,0:T(8,128)S(1)} %get-tuple-element.47), channel_id=1, source_target_pairs={{0,1},{1,0},{2,4},{3,5},{4,2},{5,3},{6,8},{7,9},{8,6},{9,7},{10,12... | collective-permute-start | bytes 761864 | tf_op jit(solution)/shard_map/ppermute | solution.py:638
  5.5 0.1 collective-permute-start
  5.5 1.5 %collective-permute-start.1 = (f32[8,8,256]{2,1,0:T(8,128)S(1)}, f32[8,8,256]{2,1,0:T(8,128)S(1)}, u32[]{:S(2)}, u32[]{:S(2)}) collective-permute-start(f32[8,8,256]{2,1,0:T(8,128)S(1)} %get-tuple-element.39), channel_id=1, source_target_pairs={{0,1},{1,0},{2,3},{3,2},{4,5},{5,4},{6,7},{7,6},{8,9},{9,8},{10,11... | collective-permute-start | bytes 196616 | tf_op jit(solution)/shard_map/ppermute | solution.py:632
  7.1 0.3 collective-permute-start.2
  7.3 1.1 %collective-permute-start.4 = (f32[8,256]{1,0:T(8,128)S(1)}, f32[8,256]{1,0:T(8,128)S(1)}, u32[]{:S(2)}, u32[]{:S(2)}) collective-permute-start(f32[8,256]{1,0:T(8,128)S(1)} %get-tuple-element.48), channel_id=1, source_target_pairs={{0,1},{1,0},{2,5},{3,4},{4,3},{5,2},{6,9},{7,8},{8,7},{9,6},{10,13... | collective-permute-start | bytes 24584 | tf_op jit(solution)/shard_map/ppermute | solution.py:643
  8.4 2.4 %collective-permute-done.2.ed = f32[8,256]{1,0:T(8,128)S(1)} collective-permute-done((f32[8,256]{1,0:T(8,128)S(1)}, f32[8,256]{1,0:T(8,128)S(1)}, u32[]{:S(2)}, u32[]{:S(2)}) %collective-permute-start.2) | collective-permute-done | bytes 8224 | tf_op jit(solution)/shard_map/ppermute | solution.py:643
  10.8 0.4 %collective-permute-done.1.t = f32[8,8,256]{2,1,0:T(8,128)S(1)} collective-permute-done((f32[8,8,256]{2,1,0:T(8,128)S(1)}, f32[8,8,256]{2,1,0:T(8,128)S(1)}, u32[]{:S(2)}, u32[]{:S(2)}) %collective-permute-start.1) | collective-permute-done | bytes 65568 | tf_op jit(solution)/shard_map/ppermute | solution.py:632
  11.2 0.0 collective-permute-done.e
  11.2 0.0 copy-done.1
  11.2 0.0 copy-done.2
  11.2 0.0 copy-done.3
  11.2 0.0 copy-done.4
  11.2 0.8 %shard_map.85 = (f32[19,2,16,256]{3,2,1,0:T(8,128)S(1)}, f32[19,2,16,256]{3,2,1,0:T(8,128)S(1)}, f32[2,16,256]{2,1,0:T(8,128)S(1)}, f32[18,2,16,256]{3,2,1,0:T(8...) custom-call(s32[1]{0:T(128)} %bitcast.parity_ref, ...), custom_call_target="tpu_custom_call" | custom-call | tf_op jit(solution)/shard_map/pallas_call | solution.py:588
  12.0 0.0 collective-permute-done.4.od
  12.0 0.0 collective-permute-done.3.o
  12.0 0.0 copy-start
  12.1 0.8 %shard_map.86 = (f32[19,2,16,256]{3,2,1,0:T(8,128)S(1)}, f32[19,2,16,256]{3,2,1,0:T(8,128)S(1)}, f32[2,16,256]{2,1,0:T(8,128)S(1)}, f32[18,2,16,256]{3,2,1,0:T(8...) custom-call(s32[1]{0:T(128)} %bitcast.parity_ref, ...), custom_call_target="tpu_custom_call", output_to_operand_aliasing={{0}: (2, {}), {1}: (3, {}), {2}: (4, {}), {3}: (5, {}), {4}... | custom-call | tf_op jit(solution)/shard_map/pallas_call | solution.py:588
  12.8 2.1 %collective-permute-start.5 = (f32[5,8,256]{2,1,0:T(8,128)S(1)}, f32[5,8,256]{2,1,0:T(8,128)S(1)}, u32[]{:S(2)}, u32[]{:S(2)}) collective-permute-start(f32[5,8,256]{2,1,0:T(8,128)S(1)} %get-tuple-element.55), channel_id=1, source_target_pairs={{0,1},{1,0},{2,3},{3,2},{4,5},{5,4},{6,7},{7,6},{8,9},{9,8},{10,11... | collective-permute-start | bytes 122888 | tf_op jit(solution)/shard_map/ppermute | solution.py:632
  14.9 1.7 %collective-permute-start.6 = (f32[1,256]{1,0:T(1,128)S(1)}, f32[1,256]{1,0:T(1,128)S(1)}, u32[]{:S(2)}, u32[]{:S(2)}) collective-permute-start(f32[1,256]{1,0:T(1,128)S(1)} %get-tuple-element.56), channel_id=1, source_target_pairs={{0,18},{1,19},{2,16},{3,17},{4,22},{5,23},{6,20},{7,21},{8,26},{9,... | collective-permute-start | bytes 3080 | tf_op jit(solution)/shard_map/ppermute | solution.py:655
  16.6 2.2 %collective-permute-done.6 = f32[1,256]{1,0:T(1,128)S(1)} collective-permute-done((f32[1,256]{1,0:T(1,128)S(1)}, f32[1,256]{1,0:T(1,128)S(1)}, u32[]{:S(2)}, u32[]{:S(2)}) %collective-permute-start.6) | collective-permute-done | bytes 1056 | tf_op jit(solution)/shard_map/ppermute | solution.py:655
  18.8 0.0 collective-permute-done.5.t
  18.8 0.2 collective-permute-start.7
  19.0 0.6 %collective-permute-start.8 = (f32[168,256]{1,0:T(8,128)S(1)}, f32[168,256]{1,0:T(8,128)S(1)}, u32[]{:S(2)}, u32[]{:S(2)}) collective-permute-start(f32[168,256]{1,0:T(8,128)S(1)} %get-tuple-element.61), channel_id=1, source_target_pairs={{0,1},{1,0},{2,4},{3,5},{4,2},{5,3},{6,8},{7,9},{8,6},{9,7},{10,12... | collective-permute-start | bytes 516104 | tf_op jit(solution)/shard_map/ppermute | solution.py:638
  19.6 0.7 %collective-permute-done.7.e = f32[176,256]{1,0:T(8,128)S(1)} collective-permute-done((f32[176,256]{1,0:T(8,128)S(1)}, f32[176,256]{1,0:T(8,128)S(1)}, u32[]{:S(2)}, u32[]{:S(2)}) %collective-permute-start.7) | collective-permute-done | bytes 180256 | tf_op jit(solution)/shard_map/ppermute | solution.py:638
  20.3 1.4 %collective-permute-start.9 = (f32[1,256]{1,0:T(1,128)S(1)}, f32[1,256]{1,0:T(1,128)S(1)}, u32[]{:S(2)}, u32[]{:S(2)}) collective-permute-start(f32[1,256]{1,0:T(1,128)S(1)} %slice_add_fusion), channel_id=1, source_target_pairs={{0,3},{1,2},{2,1},{3,0},{4,7},{5,6},{6,5},{7,4},{8,11},{9,10},{10,... | collective-permute-start | bytes 3080 | tf_op jit(solution)/shard_map/ppermute | solution.py:655
  21.7 0.0 copy-done
  21.7 1.2 %shard_map.88 = (f32[19,2,16,256]{3,2,1,0:T(8,128)}, f32[19,2,16,256]{3,2,1,0:T(8,128)}, f32[2,16,256]{2,1,0:T(8,128)S(1)}) custom-call(s32[1]{0:T(128)} %bitcast.parity_ref, f32[19,2,16,256]{3,2,1,0:T(8,128)S(1)} %get-tuple-element.49.post, f32[19,2,16,256]{3,2,1,0:T(8,128)S(1)} %get-tuple-element.50.adj, f32[2,16,256]{2,1,0:T(8,128)S(1)} %get-tuple-element.37.flags, ...), custom_call_target="tpu_custom_call" | custom-call | tf_op jit(solution)/shard_map/pallas_call | solution.py:588
  22.9 0.4 %collective-permute-done.9 = f32[1,256]{1,0:T(1,128)S(1)} collective-permute-done((f32[1,256]{1,0:T(1,128)S(1)}, f32[1,256]{1,0:T(1,128)S(1)}, u32[]{:S(2)}, u32[]{:S(2)}) %collective-permute-start.9) | collective-permute-done | bytes 1056 | tf_op jit(solution)/shard_map/ppermute | solution.py:655
  23.3 2.4 %collective-permute-start.12 = (f32[1,256]{1,0:T(1,128)S(1)}, f32[1,256]{1,0:T(1,128)S(1)}, u32[]{:S(2)}, u32[]{:S(2)}) collective-permute-start(f32[1,256]{1,0:T(1,128)S(1)} %add.25), channel_id=1, source_target_pairs={{0,12},{1,13},{2,14},{3,15},{4,8},{5,9},{6,10},{7,11},{8,4},{9,5},... | collective-permute-start | bytes 3080 | tf_op jit(solution)/shard_map/ppermute | solution.py:655
  25.7 0.2 collective-permute-start.11
  25.9 0.6 %collective-permute-start.10 = (f32[1,256]{1,0:T(1,128)S(1)}, f32[1,256]{1,0:T(1,128)S(1)}, u32[]{:S(2)}, u32[]{:S(2)}) collective-permute-start(f32[1,256]{1,0:T(1,128)S(1)} %add.25), channel_id=1, source_target_pairs={{0,6},{1,7},{2,4},{3,5},{4,2},{5,3},{6,0},{7,1},{8,14},{9,15},{10,... | collective-permute-start | bytes 3080 | tf_op jit(solution)/shard_map/ppermute | solution.py:655
  26.5 0.0 collective-permute-done.8.o
  26.5 1.2 %shard_map.89 = (f32[19,2,16,256]{3,2,1,0:T(8,128)}, f32[19,2,16,256]{3,2,1,0:T(8,128)}, f32[2,16,256]{2,1,0:T(8,128)}) custom-call(s32[1]{0:T(128)} %bitcast.parity_ref, s32[1]{0:T(128)} %bitcast.1.real_ref, f32[19,2,16,256]{3,2,1,0:T(8,128)} %get-tuple-element.58.final_near, ...), custom_call_target="tpu_custom_call", output_to_operand_aliasing={{0}: (2, {}), {1}: (3, {})} | custom-call | tf_op jit(solution)/shard_map/pallas_call | solution.py:588
  27.7 0.0 collective-permute-done.12
  27.8 0.9 %collective-permute-done.11 = f32[1,256]{1,0:T(1,128)S(1)} collective-permute-done((f32[1,256]{1,0:T(1,128)S(1)}, f32[1,256]{1,0:T(1,128)S(1)}, u32[]{:S(2)}, u32[]{:S(2)}) %collective-permute-start.11) | collective-permute-done | bytes 1056 | tf_op jit(solution)/shard_map/ppermute | solution.py:655
  28.7 0.2 collective-permute-done.10
  28.9 0.5 %fusion.1 = f32[8]{0:T(128)} fusion(f32[1,256]{1,0:T(1,128)S(1)} %collective-permute-done.12, f32[1,256]{1,0:T(1,128)S(1)} %collective-permute-done.11, f32[1,256]{1,0:T(1,128)S(1)} %collective-permute-done.10, f32[1,256]{1,0:T(1,128)S(1)} %add.25), kind=kLoop, calls=%fused_computation.4 | loop fusion | flops 24 | bytes 160 | tf_op jit(solution)/shard_map/squeeze | solution.py:754
  (4 shorter events, 0.0 us)
Async XLA Ops:
  0.6 10.6 %copy-start.1 = (f32[19,2,16,256]{3,2,1,0:T(8,128)S(1)}, f32[19,2,16,256]{3,2,1,0:T(8,128)}, u32[]{:S(2)}) copy-start(f32[19,2,16,256]{3,2,1,0:T(8,128)} %seed.3) | copy-start | bytes 1867780
  0.7 10.6 %copy-start.2 = (f32[2,16,256]{2,1,0:T(8,128)S(1)}, f32[2,16,256]{2,1,0:T(8,128)}, u32[]{:S(2)}) copy-start(f32[2,16,256]{2,1,0:T(8,128)} %porous.7) | copy-start | bytes 98308
  0.7 10.6 %copy-start.3 = (s32[2,16,256]{2,1,0:T(8,128)S(1)}, s32[2,16,256]{2,1,0:T(8,128)}, u32[]{:S(2)}) copy-start(s32[2,16,256]{2,1,0:T(8,128)} %types.7) | copy-start | bytes 98308
  0.7 10.6 %copy-start.4 = (s32[2,16,256]{2,1,0:T(8,128)S(1)}, s32[2,16,256]{2,1,0:T(8,128)}, u32[]{:S(2)}) copy-start(s32[2,16,256]{2,1,0:T(8,128)} %regions.7) | copy-start | bytes 98308
  2.4 9.6 %collective-permute-start.3 = (f32[248,256]{1,0:T(8,128)S(1)}, f32[248,256]{1,0:T(8,128)S(1)}, u32[]{:S(2)}, u32[]{:S(2)}) collective-permute-start(f32[248,256]{1,0:T(8,128)S(1)} %get-tuple-element.47), channel_id=1, source_target_pairs={{0,1},{1,0},{2,4},{3,5},{4,2},{5,3},{6,8},{7,9},{8,6},{9,7},{10,12... | collective-permute-start | bytes 761864 | tf_op jit(solution)/shard_map/ppermute | solution.py:638
  5.5 5.8 %collective-permute-start = (f32[240,256]{1,0:T(8,128)S(1)}, f32[240,256]{1,0:T(8,128)S(1)}, u32[]{:S(2)}, u32[]{:S(2)}) collective-permute-start(f32[240,256]{1,0:T(8,128)S(1)} %get-tuple-element.38), channel_id=1, source_target_pairs={{0,2},{1,3},{2,0},{3,1},{4,6},{5,7},{6,4},{7,5},{8,10},{9,11},{10,... | collective-permute-start | bytes 737288 | tf_op jit(solution)/shard_map/ppermute | solution.py:638
  5.5 5.7 %collective-permute-start.1 = (f32[8,8,256]{2,1,0:T(8,128)S(1)}, f32[8,8,256]{2,1,0:T(8,128)S(1)}, u32[]{:S(2)}, u32[]{:S(2)}) collective-permute-start(f32[8,8,256]{2,1,0:T(8,128)S(1)} %get-tuple-element.39), channel_id=1, source_target_pairs={{0,1},{1,0},{2,3},{3,2},{4,5},{5,4},{6,7},{7,6},{8,9},{9,8},{10,11... | collective-permute-start | bytes 196616 | tf_op jit(solution)/shard_map/ppermute | solution.py:632
  7.1 3.8 %collective-permute-start.2 = (f32[8,256]{1,0:T(8,128)S(1)}, f32[8,256]{1,0:T(8,128)S(1)}, u32[]{:S(2)}, u32[]{:S(2)}) collective-permute-start(f32[8,256]{1,0:T(8,128)S(1)} %get-tuple-element.40), channel_id=1, source_target_pairs={{0,3},{1,2},{2,1},{3,0},{4,7},{5,6},{6,5},{7,4},{8,11},{9,10},{10,... | collective-permute-start | bytes 24584 | tf_op jit(solution)/shard_map/ppermute | solution.py:643
  7.3 4.7 %collective-permute-start.4 = (f32[8,256]{1,0:T(8,128)S(1)}, f32[8,256]{1,0:T(8,128)S(1)}, u32[]{:S(2)}, u32[]{:S(2)}) collective-permute-start(f32[8,256]{1,0:T(8,128)S(1)} %get-tuple-element.48), channel_id=1, source_target_pairs={{0,1},{1,0},{2,5},{3,4},{4,3},{5,2},{6,9},{7,8},{8,7},{9,6},{10,13... | collective-permute-start | bytes 24584 | tf_op jit(solution)/shard_map/ppermute | solution.py:643
  12.0 9.6 %copy-start = (f32[19,2,16,256]{3,2,1,0:T(8,128)S(1)}, f32[19,2,16,256]{3,2,1,0:T(8,128)}, u32[]{:S(2)}) copy-start(f32[19,2,16,256]{3,2,1,0:T(8,128)} %pops.3) | copy-start | bytes 1867780
  12.8 6.0 %collective-permute-start.5 = (f32[5,8,256]{2,1,0:T(8,128)S(1)}, f32[5,8,256]{2,1,0:T(8,128)S(1)}, u32[]{:S(2)}, u32[]{:S(2)}) collective-permute-start(f32[5,8,256]{2,1,0:T(8,128)S(1)} %get-tuple-element.55), channel_id=1, source_target_pairs={{0,1},{1,0},{2,3},{3,2},{4,5},{5,4},{6,7},{7,6},{8,9},{9,8},{10,11... | collective-permute-start | bytes 122888 | tf_op jit(solution)/shard_map/ppermute | solution.py:632
  14.9 3.9 %collective-permute-start.6 = (f32[1,256]{1,0:T(1,128)S(1)}, f32[1,256]{1,0:T(1,128)S(1)}, u32[]{:S(2)}, u32[]{:S(2)}) collective-permute-start(f32[1,256]{1,0:T(1,128)S(1)} %get-tuple-element.56), channel_id=1, source_target_pairs={{0,18},{1,19},{2,16},{3,17},{4,22},{5,23},{6,20},{7,21},{8,26},{9,... | collective-permute-start | bytes 3080 | tf_op jit(solution)/shard_map/ppermute | solution.py:655
  18.8 1.5 %collective-permute-start.7 = (f32[176,256]{1,0:T(8,128)S(1)}, f32[176,256]{1,0:T(8,128)S(1)}, u32[]{:S(2)}, u32[]{:S(2)}) collective-permute-start(f32[176,256]{1,0:T(8,128)S(1)} %get-tuple-element.57), channel_id=1, source_target_pairs={{0,2},{1,3},{2,0},{3,1},{4,6},{5,7},{6,4},{7,5},{8,10},{9,11},{10,... | collective-permute-start | bytes 540680 | tf_op jit(solution)/shard_map/ppermute | solution.py:638
  19.0 7.5 %collective-permute-start.8 = (f32[168,256]{1,0:T(8,128)S(1)}, f32[168,256]{1,0:T(8,128)S(1)}, u32[]{:S(2)}, u32[]{:S(2)}) collective-permute-start(f32[168,256]{1,0:T(8,128)S(1)} %get-tuple-element.61), channel_id=1, source_target_pairs={{0,1},{1,0},{2,4},{3,5},{4,2},{5,3},{6,8},{7,9},{8,6},{9,7},{10,12... | collective-permute-start | bytes 516104 | tf_op jit(solution)/shard_map/ppermute | solution.py:638
  20.3 3.0 %collective-permute-start.9 = (f32[1,256]{1,0:T(1,128)S(1)}, f32[1,256]{1,0:T(1,128)S(1)}, u32[]{:S(2)}, u32[]{:S(2)}) collective-permute-start(f32[1,256]{1,0:T(1,128)S(1)} %slice_add_fusion), channel_id=1, source_target_pairs={{0,3},{1,2},{2,1},{3,0},{4,7},{5,6},{6,5},{7,4},{8,11},{9,10},{10,... | collective-permute-start | bytes 3080 | tf_op jit(solution)/shard_map/ppermute | solution.py:655
  23.3 4.5 %collective-permute-start.12 = (f32[1,256]{1,0:T(1,128)S(1)}, f32[1,256]{1,0:T(1,128)S(1)}, u32[]{:S(2)}, u32[]{:S(2)}) collective-permute-start(f32[1,256]{1,0:T(1,128)S(1)} %add.25), channel_id=1, source_target_pairs={{0,12},{1,13},{2,14},{3,15},{4,8},{5,9},{6,10},{7,11},{8,4},{9,5},... | collective-permute-start | bytes 3080 | tf_op jit(solution)/shard_map/ppermute | solution.py:655
  25.7 3.0 %collective-permute-start.11 = (f32[1,256]{1,0:T(1,128)S(1)}, f32[1,256]{1,0:T(1,128)S(1)}, u32[]{:S(2)}, u32[]{:S(2)}) collective-permute-start(f32[1,256]{1,0:T(1,128)S(1)} %add.25), channel_id=1, source_target_pairs={{0,10},{1,11},{2,8},{3,9},{4,14},{5,15},{6,12},{7,13},{8,2},{9,3},... | collective-permute-start | bytes 3080 | tf_op jit(solution)/shard_map/ppermute | solution.py:655
  25.9 3.0 %collective-permute-start.10 = (f32[1,256]{1,0:T(1,128)S(1)}, f32[1,256]{1,0:T(1,128)S(1)}, u32[]{:S(2)}, u32[]{:S(2)}) collective-permute-start(f32[1,256]{1,0:T(1,128)S(1)} %add.25), channel_id=1, source_target_pairs={{0,6},{1,7},{2,4},{3,5},{4,2},{5,3},{6,0},{7,1},{8,14},{9,15},{10,... | collective-permute-start | bytes 3080 | tf_op jit(solution)/shard_map/ppermute | solution.py:655
